TPU v7x, 256 devices: a whole 4x4x8 slice. The times are simulated.
256 devices in a mesh: comp: 2 (over x_hi), seq: 128 (over x_lo, z, y, core).
Axes of the slice: x: 4 (x_hi: 2, x_lo: 2; x = x_hi * 2 + x_lo), y: 4, z: 8, core: 2. Of those that a mesh axis runs over, the one named last changes fastest.
Arguments:
- stale_states: bfloat16 [2, 6144, 2432], P('comp', 'seq'), may hold values from -1.5 to 1.5
- mod_table: float32 [2, 28, 3, 2432], P('comp'), may hold values from -4.8 to 4.8
- timesteps: int32 [8], replicated, may hold values from 0 to 27
- text_count: int32 [8], replicated, may hold values from 64 to 128, as said below
- text_kv: bfloat16 [2, 1024, 1216], P(None, 'seq'), may hold values from -6 to 6
- qkv_weight: bfloat16 [2, 2432, 3648], P('comp', 'seq'), may hold values from -0.125 to 0.125
- out_weight: bfloat16 [2, 1216, 2432], P('comp', None, 'seq'), may hold values from -0.15625 to 0.15625
- qk_gain: float32 [2, 2, 1216], P('comp'), may hold values from 0.49 to 8.6
Outputs:
- new_states: bfloat16 [2, 6144, 2432], P('comp', 'seq')
Inputs may be any that keep to these rules, and one draw needn't show every extreme that they name: `text_count`: one sequence uses all 128 slots.
All inputs are finite; a program needn't handle non-finite values.
Results may differ from a plain program's by a relative error of at most 0.0085.
The roundings to bfloat16 on the way count: a program that leaves them out, or rounds other values in their place, can miss the bound.
Values may be sent and summed in bfloat16 or wider, within the bound.
No kernel may reach another device: no remote copies, remote signals or barrier semaphores. Data moves between devices by JAX's collectives and lax.ppermute only.
A program may use at most 128 MiB of HBM per device.

v0:
```python
import jax
import jax.numpy as jnp
from jax import lax
from jax.sharding import PartitionSpec as P

HEADS = 19
GROUP = 16


EPSILON = 1e-06
MASKED = -1e30


def shifted(array, axis, by):
    devices = lax.axis_size(axis)
    return lax.ppermute(array, axis, [(i, (i + by) % devices) for i in range(devices)])


def passed_along(value, axis, steps):
    count = lax.axis_size(axis)
    leading, last = (max(0, -steps), min(count, count - steps))
    return lax.ppermute(value, axis, [(source, source + steps) for source in range(leading, last)])


def head_norm(values, gain_row, head_count):
    shaped = values.reshape(values.shape[0], head_count, -1)
    shaped = shaped * lax.rsqrt(jnp.mean(shaped * shaped, axis=-1, keepdims=True) + EPSILON)
    return shaped.reshape(values.shape[0], -1) * gain_row


def shard_bias(sources, image_rows, text_rows, text_valid):
    column = jnp.arange(image_rows + text_rows, dtype=jnp.int32)
    text_slot = sources[:, None] * text_rows + (column - image_rows)[None, :]
    usable = (column[None, :] < image_rows) | (text_slot < text_valid)
    usable = usable & (sources[:, None] >= 0) & (sources[:, None] < GROUP)
    return jnp.where(usable, 0.0, MASKED).astype(jnp.float32).reshape(-1)


def absorb(running, queries, pairs, key_bias, head_count, shard_rows):
    total_rows = pairs.shape[1]
    pieces = total_rows // shard_rows
    block_rows = shard_rows * 2 if pieces % 2 == 0 else shard_rows
    scale_factor = queries.shape[2] ** (-0.5)

    def one_block(block_num, softmax_state):
        row_peak, totals, mixed_sum = softmax_state
        key_rows = pairs[0].reshape(block_rows, head_count, -1)
        values = pairs[1].reshape(block_rows, head_count, -1)
        scores = (
            jnp.einsum("qhd,khd->hqk", queries, key_rows, preferred_element_type=jnp.float32)
            * scale_factor
            + key_bias
        )
        new_peak = jnp.maximum(row_peak, jnp.max(scores, axis=-1))
        factor = jnp.exp(row_peak - new_peak)
        exp_scores = jnp.exp(scores - new_peak[:, :, None])
        totals = totals * factor + jnp.sum(exp_scores, axis=-1)
        mixed_sum = mixed_sum * jnp.transpose(factor)[:, :, None] + jnp.einsum(
            "hqk,khd->qhd",
            exp_scores.astype(jnp.bfloat16),
            values,
            preferred_element_type=jnp.float32,
        )
        return (new_peak, totals, mixed_sum)

    return lax.fori_loop(0, total_rows // block_rows, one_block, running)


def per_device(
    stale_states, mod_table, timesteps, text_count, text_kv, qkv_weight, out_weight, qk_gain
):
    image_rows = stale_states.shape[1]
    text_rows = text_kv.shape[1]
    head_width = text_kv.shape[2]
    head_count = HEADS
    shard_rows = image_rows + text_rows
    states = shifted(stale_states[0], "comp", 1).astype(jnp.float32)
    position = lax.axis_index("seq")
    group_place = position % GROUP
    sequence = position // GROUP
    step_index = lax.dynamic_index_in_dim(timesteps, sequence, 0, False)
    modulation = lax.dynamic_index_in_dim(mod_table[0], step_index, 0, False)
    text_valid = lax.dynamic_index_in_dim(text_count, sequence, 0, False)
    centred = states - jnp.mean(states, axis=-1, keepdims=True)
    normed = centred * lax.rsqrt(jnp.mean(centred * centred, axis=-1, keepdims=True) + EPSILON)
    modulated = (normed * (1.0 + modulation[1]) + modulation[0]).astype(jnp.bfloat16)
    projected = jnp.dot(
        modulated,
        lax.all_gather(qkv_weight[0], "seq", axis=0, tiled=True),
        preferred_element_type=jnp.float32,
    )
    queries = (
        head_norm(projected[:, :head_width], qk_gain[0, 0], head_count)
        .astype(jnp.bfloat16)
        .reshape(image_rows, head_count, -1)
    )
    key_rows = head_norm(
        projected[:, head_width : 2 * head_width], qk_gain[0, 1], head_count
    ).astype(jnp.bfloat16)
    values = projected[:, 2 * head_width :].astype(jnp.bfloat16)
    own_pairs = jnp.stack(
        [jnp.concatenate([key_rows, text_kv[0]], 0), jnp.concatenate([values, text_kv[1]], 0)]
    )
    running = (
        jnp.full((head_count, image_rows), -jnp.inf, jnp.float32),
        jnp.zeros((head_count, image_rows), jnp.float32),
        jnp.zeros((image_rows, head_count, head_width // head_count), jnp.float32),
    )
    running = absorb(
        running,
        queries,
        own_pairs,
        shard_bias(group_place[None], image_rows, text_rows, text_valid),
        head_count,
        shard_rows,
    )

    def turn(turn_num, carried):
        softmax_state, ahead, behind = carried
        ahead = passed_along(ahead, "seq", 1)
        behind = passed_along(behind, "seq", -1)
        anchors = jnp.stack([group_place - turn_num, group_place + turn_num])
        both = jnp.concatenate([ahead, behind], 1)
        softmax_state = absorb(
            softmax_state,
            queries,
            both,
            shard_bias(anchors, image_rows, text_rows, text_valid),
            head_count,
            shard_rows,
        )
        return (softmax_state, ahead, behind)

    running, unused_ahead, unused_behind = lax.fori_loop(
        1, GROUP, turn, (running, own_pairs, own_pairs)
    )
    row_peak, totals, mixed_sum = running
    attended = (
        (mixed_sum / jnp.transpose(totals)[:, :, None])
        .reshape(image_rows, head_width)
        .astype(jnp.bfloat16)
    )
    branch = jnp.dot(
        attended,
        lax.all_gather(out_weight[0], "seq", axis=1, tiled=True),
        preferred_element_type=jnp.float32,
    )
    return (states + modulation[2] * branch).astype(jnp.bfloat16)[None]


def solution(mesh):
    in_specs = (
        P("comp", "seq", None),
        P("comp", None, None, None),
        P(),
        P(),
        P(None, "seq", None),
        P("comp", "seq", None),
        P("comp", None, "seq"),
        P("comp", None, None),
    )
    out_specs = P("comp", "seq", None)
    return jax.shard_map(
        per_device, mesh=mesh, in_specs=in_specs, out_specs=out_specs, check_vma=False
    )
```

profile of v0, /device:TPU:2, one launch (start us, length us, event | category | flops | bytes accessed | tf_op | source)
XLA Modules:
  0.0 826.8 jit_solution(11456785433792014457)
XLA Ops:
  10.0 2.2 collective-permute-start.2
  20.0 217.8 %all-gather.7.cloned.1.call-done = bf16[1,1216,2432]{1,0,2:T(2,128)(2,1)} async-done(((bf16[1,1216,19]{1,0,2:T(2,128)(2,1)}), bf16[1,1216,2432]{1,0,2:T(2,128)(2,1)}) %all-gather.7.cloned.1.call-update) | async-done | bytes 5914640 | tf_op jit(solution)/shard_map/all_gather | solution.py:145
  237.8 24.8 %copy.49 = bf16[1,1216,2432]{2,1,0:T(8,128)(2,1)} copy(bf16[1,1216,2432]{1,0,2:T(2,128)(2,1)} %all-gather.7.cloned.1.call-done) | data formatting | bytes 11829248 | tf_op jit(solution)/shard_map/all_gather | solution.py:145
  262.7 227.0 %all-gather.5.cloned.1.call-done = bf16[1,2432,3648]{2,0,1:T(2,128)(2,1)} async-done(((bf16[1,19,3648]{2,0,1:T(2,128)(2,1)}), bf16[1,2432,3648]{2,0,1:T(2,128)(2,1)}) %all-gather.5.cloned.1.call-update) | async-done | bytes 17743888 | tf_op jit(solution)/shard_map/all_gather | solution.py:89
  489.7 72.0 %copy.40 = bf16[1,2432,3648]{1,2,0:T(8,128)(2,1)} copy(bf16[1,2432,3648]{2,0,1:T(2,128)(2,1)} %all-gather.5.cloned.1.call-done) | data formatting | bytes 35487744 | tf_op jit(solution)/shard_map/all_gather | solution.py:89
  561.7 11.3 %fusion.8 = f32[48,3648]{1,0:T(8,128)S(1)} fusion(bf16[1,2432,3648]{1,2,0:T(8,128)(2,1)} %copy.40, bf16[48,2432]{1,0:T(8,128)(2,1)S(1)} %collective-permute-done.2, f32[2432]{0:T(1024)S(1)} %get-tuple-element.325, f32[2432]{0:T(1024)S(1)} %get-tuple-element.324, f32[48]{0:T(128)S(1)} %add_rsqrt_fusion.2, f32[48]{0:T(128)S(1)} %broadcast_multiply_fusion.1), kind=kOutput, calls=%fused_computation.21 | convolution fusion | flops 852406272 | bytes 18697600 | tf_op jit(solution)/shard_map/dot_general | solution.py:87
  576.8 238.2 %while.43 = (s32[]{:T(128)}, f32[19,48]{1,0:T(8,128)S(1)}, f32[19,48]{1,0:T(8,128)S(1)}, f32[48,19,64]{2,0,1:T(8,128)S(1)}, bf16[2,56,1216]{2,1,0:T(8,128)(2,1)S...) while((s32[]{:T(128)}, f32[19,48]{1,0:T(8,128)S(1)}, ...), condition=%wide.region_9.10_spmd, body=%wide.region_6.9_spmd.sunk | while | flops 26984140 | bytes 8995377 | solution.py:134
  576.8 1.9 collective-permute-start
  578.7 7.9 collective-permute-start.1
  592.5 1.9 collective-permute-start
  594.4 8.0 collective-permute-start.1
  608.4 1.9 collective-permute-start
  610.3 8.0 collective-permute-start.1
  624.3 1.9 collective-permute-start
  626.2 8.0 collective-permute-start.1
  640.2 1.9 collective-permute-start
  642.1 8.0 collective-permute-start.1
  656.1 1.9 collective-permute-start
  658.0 8.0 collective-permute-start.1
  673.9 8.0 collective-permute-start.1
  687.9 1.9 collective-permute-start
  689.8 8.0 collective-permute-start.1
  705.7 8.0 collective-permute-start.1
  721.6 8.0 collective-permute-start.1
  735.5 1.9 collective-permute-start
  737.5 8.0 collective-permute-start.1
  753.3 8.0 collective-permute-start.1
  769.2 8.0 collective-permute-start.1
  783.2 1.9 collective-permute-start
  785.1 8.0 collective-permute-start.1
  801.0 8.0 collective-permute-start.1
  815.5 4.5 fusion.21
  (371 shorter events, 112.4 us)
Async XLA Ops:
  6.5 231.3 %all-gather.7.cloned.1.call-start = ((), (), s32[]{:S(2)}) async-start(), calls=%async_computation.1 | async-start | bytes 12549120 | tf_op jit(solution)/shard_map/all_gather | solution.py:145
  8.1 481.6 %all-gather.5.cloned.1.call-start = ((), (), s32[]{:S(2)}) async-start(), calls=%async_computation | async-start | bytes 36392448 | tf_op jit(solution)/shard_map/all_gather | solution.py:89
  576.8 12.2 %collective-permute-start = (bf16[2,56,1216]{2,1,0:T(8,128)(2,1)S(1)}, bf16[2,56,1216]{2,1,0:T(8,128)(2,1)S(1)}, u32[]{:S(2)}, u32[]{:S(2)}) collective-permute-start(bf16[2,56,1216]{2,1,0:T(8,128)(2,1)S(1)} %get-tuple-element.459), channel_id=1, source_target_pairs={{0,1},{1,2},{2,3},{3,4},{4,5},{5,6},{6,7},{7,8},{8,9},{9,10},{10,1... | collective-permute-start | bytes 817160 | tf_op jit(solution)/shard_map/while/body/eval_jaxpr/ppermute | solution.py:22
  578.7 12.0 %collective-permute-start.1 = (bf16[2,56,1216]{2,1,0:T(8,128)(2,1)S(1)}, bf16[2,56,1216]{2,1,0:T(8,128)(2,1)S(1)}, u32[]{:S(2)}, u32[]{:S(2)}) collective-permute-start(bf16[2,56,1216]{2,1,0:T(8,128)(2,1)S(1)} %get-tuple-element.460), channel_id=1, source_target_pairs={{1,0},{2,1},{3,2},{4,3},{5,4},{6,5},{7,6},{8,7},{9,8},{10,9},{11,1... | collective-permute-start | bytes 817160 | tf_op jit(solution)/shard_map/while/body/eval_jaxpr/ppermute | solution.py:22
  592.5 12.4 %collective-permute-start = (bf16[2,56,1216]{2,1,0:T(8,128)(2,1)S(1)}, bf16[2,56,1216]{2,1,0:T(8,128)(2,1)S(1)}, u32[]{:S(2)}, u32[]{:S(2)}) collective-permute-start(bf16[2,56,1216]{2,1,0:T(8,128)(2,1)S(1)} %get-tuple-element.459), channel_id=1, source_target_pairs={{0,1},{1,2},{2,3},{3,4},{4,5},{5,6},{6,7},{7,8},{8,9},{9,10},{10,1... | collective-permute-start | bytes 817160 | tf_op jit(solution)/shard_map/while/body/eval_jaxpr/ppermute | solution.py:22
  594.4 12.2 %collective-permute-start.1 = (bf16[2,56,1216]{2,1,0:T(8,128)(2,1)S(1)}, bf16[2,56,1216]{2,1,0:T(8,128)(2,1)S(1)}, u32[]{:S(2)}, u32[]{:S(2)}) collective-permute-start(bf16[2,56,1216]{2,1,0:T(8,128)(2,1)S(1)} %get-tuple-element.460), channel_id=1, source_target_pairs={{1,0},{2,1},{3,2},{4,3},{5,4},{6,5},{7,6},{8,7},{9,8},{10,9},{11,1... | collective-permute-start | bytes 817160 | tf_op jit(solution)/shard_map/while/body/eval_jaxpr/ppermute | solution.py:22
  608.4 12.4 %collective-permute-start = (bf16[2,56,1216]{2,1,0:T(8,128)(2,1)S(1)}, bf16[2,56,1216]{2,1,0:T(8,128)(2,1)S(1)}, u32[]{:S(2)}, u32[]{:S(2)}) collective-permute-start(bf16[2,56,1216]{2,1,0:T(8,128)(2,1)S(1)} %get-tuple-element.459), channel_id=1, source_target_pairs={{0,1},{1,2},{2,3},{3,4},{4,5},{5,6},{6,7},{7,8},{8,9},{9,10},{10,1... | collective-permute-start | bytes 817160 | tf_op jit(solution)/shard_map/while/body/eval_jaxpr/ppermute | solution.py:22
  610.3 12.2 %collective-permute-start.1 = (bf16[2,56,1216]{2,1,0:T(8,128)(2,1)S(1)}, bf16[2,56,1216]{2,1,0:T(8,128)(2,1)S(1)}, u32[]{:S(2)}, u32[]{:S(2)}) collective-permute-start(bf16[2,56,1216]{2,1,0:T(8,128)(2,1)S(1)} %get-tuple-element.460), channel_id=1, source_target_pairs={{1,0},{2,1},{3,2},{4,3},{5,4},{6,5},{7,6},{8,7},{9,8},{10,9},{11,1... | collective-permute-start | bytes 817160 | tf_op jit(solution)/shard_map/while/body/eval_jaxpr/ppermute | solution.py:22
  624.3 12.4 %collective-permute-start = (bf16[2,56,1216]{2,1,0:T(8,128)(2,1)S(1)}, bf16[2,56,1216]{2,1,0:T(8,128)(2,1)S(1)}, u32[]{:S(2)}, u32[]{:S(2)}) collective-permute-start(bf16[2,56,1216]{2,1,0:T(8,128)(2,1)S(1)} %get-tuple-element.459), channel_id=1, source_target_pairs={{0,1},{1,2},{2,3},{3,4},{4,5},{5,6},{6,7},{7,8},{8,9},{9,10},{10,1... | collective-permute-start | bytes 817160 | tf_op jit(solution)/shard_map/while/body/eval_jaxpr/ppermute | solution.py:22
  626.2 12.2 %collective-permute-start.1 = (bf16[2,56,1216]{2,1,0:T(8,128)(2,1)S(1)}, bf16[2,56,1216]{2,1,0:T(8,128)(2,1)S(1)}, u32[]{:S(2)}, u32[]{:S(2)}) collective-permute-start(bf16[2,56,1216]{2,1,0:T(8,128)(2,1)S(1)} %get-tuple-element.460), channel_id=1, source_target_pairs={{1,0},{2,1},{3,2},{4,3},{5,4},{6,5},{7,6},{8,7},{9,8},{10,9},{11,1... | collective-permute-start | bytes 817160 | tf_op jit(solution)/shard_map/while/body/eval_jaxpr/ppermute | solution.py:22
  640.2 12.4 %collective-permute-start = (bf16[2,56,1216]{2,1,0:T(8,128)(2,1)S(1)}, bf16[2,56,1216]{2,1,0:T(8,128)(2,1)S(1)}, u32[]{:S(2)}, u32[]{:S(2)}) collective-permute-start(bf16[2,56,1216]{2,1,0:T(8,128)(2,1)S(1)} %get-tuple-element.459), channel_id=1, source_target_pairs={{0,1},{1,2},{2,3},{3,4},{4,5},{5,6},{6,7},{7,8},{8,9},{9,10},{10,1... | collective-permute-start | bytes 817160 | tf_op jit(solution)/shard_map/while/body/eval_jaxpr/ppermute | solution.py:22
  642.1 12.2 %collective-permute-start.1 = (bf16[2,56,1216]{2,1,0:T(8,128)(2,1)S(1)}, bf16[2,56,1216]{2,1,0:T(8,128)(2,1)S(1)}, u32[]{:S(2)}, u32[]{:S(2)}) collective-permute-start(bf16[2,56,1216]{2,1,0:T(8,128)(2,1)S(1)} %get-tuple-element.460), channel_id=1, source_target_pairs={{1,0},{2,1},{3,2},{4,3},{5,4},{6,5},{7,6},{8,7},{9,8},{10,9},{11,1... | collective-permute-start | bytes 817160 | tf_op jit(solution)/shard_map/while/body/eval_jaxpr/ppermute | solution.py:22
  656.1 12.4 %collective-permute-start = (bf16[2,56,1216]{2,1,0:T(8,128)(2,1)S(1)}, bf16[2,56,1216]{2,1,0:T(8,128)(2,1)S(1)}, u32[]{:S(2)}, u32[]{:S(2)}) collective-permute-start(bf16[2,56,1216]{2,1,0:T(8,128)(2,1)S(1)} %get-tuple-element.459), channel_id=1, source_target_pairs={{0,1},{1,2},{2,3},{3,4},{4,5},{5,6},{6,7},{7,8},{8,9},{9,10},{10,1... | collective-permute-start | bytes 817160 | tf_op jit(solution)/shard_map/while/body/eval_jaxpr/ppermute | solution.py:22
  658.0 12.2 %collective-permute-start.1 = (bf16[2,56,1216]{2,1,0:T(8,128)(2,1)S(1)}, bf16[2,56,1216]{2,1,0:T(8,128)(2,1)S(1)}, u32[]{:S(2)}, u32[]{:S(2)}) collective-permute-start(bf16[2,56,1216]{2,1,0:T(8,128)(2,1)S(1)} %get-tuple-element.460), channel_id=1, source_target_pairs={{1,0},{2,1},{3,2},{4,3},{5,4},{6,5},{7,6},{8,7},{9,8},{10,9},{11,1... | collective-permute-start | bytes 817160 | tf_op jit(solution)/shard_map/while/body/eval_jaxpr/ppermute | solution.py:22
  672.0 12.4 %collective-permute-start = (bf16[2,56,1216]{2,1,0:T(8,128)(2,1)S(1)}, bf16[2,56,1216]{2,1,0:T(8,128)(2,1)S(1)}, u32[]{:S(2)}, u32[]{:S(2)}) collective-permute-start(bf16[2,56,1216]{2,1,0:T(8,128)(2,1)S(1)} %get-tuple-element.459), channel_id=1, source_target_pairs={{0,1},{1,2},{2,3},{3,4},{4,5},{5,6},{6,7},{7,8},{8,9},{9,10},{10,1... | collective-permute-start | bytes 817160 | tf_op jit(solution)/shard_map/while/body/eval_jaxpr/ppermute | solution.py:22
  673.9 12.2 %collective-permute-start.1 = (bf16[2,56,1216]{2,1,0:T(8,128)(2,1)S(1)}, bf16[2,56,1216]{2,1,0:T(8,128)(2,1)S(1)}, u32[]{:S(2)}, u32[]{:S(2)}) collective-permute-start(bf16[2,56,1216]{2,1,0:T(8,128)(2,1)S(1)} %get-tuple-element.460), channel_id=1, source_target_pairs={{1,0},{2,1},{3,2},{4,3},{5,4},{6,5},{7,6},{8,7},{9,8},{10,9},{11,1... | collective-permute-start | bytes 817160 | tf_op jit(solution)/shard_map/while/body/eval_jaxpr/ppermute | solution.py:22
  687.9 12.4 %collective-permute-start = (bf16[2,56,1216]{2,1,0:T(8,128)(2,1)S(1)}, bf16[2,56,1216]{2,1,0:T(8,128)(2,1)S(1)}, u32[]{:S(2)}, u32[]{:S(2)}) collective-permute-start(bf16[2,56,1216]{2,1,0:T(8,128)(2,1)S(1)} %get-tuple-element.459), channel_id=1, source_target_pairs={{0,1},{1,2},{2,3},{3,4},{4,5},{5,6},{6,7},{7,8},{8,9},{9,10},{10,1... | collective-permute-start | bytes 817160 | tf_op jit(solution)/shard_map/while/body/eval_jaxpr/ppermute | solution.py:22
  689.8 12.2 %collective-permute-start.1 = (bf16[2,56,1216]{2,1,0:T(8,128)(2,1)S(1)}, bf16[2,56,1216]{2,1,0:T(8,128)(2,1)S(1)}, u32[]{:S(2)}, u32[]{:S(2)}) collective-permute-start(bf16[2,56,1216]{2,1,0:T(8,128)(2,1)S(1)} %get-tuple-element.460), channel_id=1, source_target_pairs={{1,0},{2,1},{3,2},{4,3},{5,4},{6,5},{7,6},{8,7},{9,8},{10,9},{11,1... | collective-permute-start | bytes 817160 | tf_op jit(solution)/shard_map/while/body/eval_jaxpr/ppermute | solution.py:22
  703.7 12.4 %collective-permute-start = (bf16[2,56,1216]{2,1,0:T(8,128)(2,1)S(1)}, bf16[2,56,1216]{2,1,0:T(8,128)(2,1)S(1)}, u32[]{:S(2)}, u32[]{:S(2)}) collective-permute-start(bf16[2,56,1216]{2,1,0:T(8,128)(2,1)S(1)} %get-tuple-element.459), channel_id=1, source_target_pairs={{0,1},{1,2},{2,3},{3,4},{4,5},{5,6},{6,7},{7,8},{8,9},{9,10},{10,1... | collective-permute-start | bytes 817160 | tf_op jit(solution)/shard_map/while/body/eval_jaxpr/ppermute | solution.py:22
  705.7 12.2 %collective-permute-start.1 = (bf16[2,56,1216]{2,1,0:T(8,128)(2,1)S(1)}, bf16[2,56,1216]{2,1,0:T(8,128)(2,1)S(1)}, u32[]{:S(2)}, u32[]{:S(2)}) collective-permute-start(bf16[2,56,1216]{2,1,0:T(8,128)(2,1)S(1)} %get-tuple-element.460), channel_id=1, source_target_pairs={{1,0},{2,1},{3,2},{4,3},{5,4},{6,5},{7,6},{8,7},{9,8},{10,9},{11,1... | collective-permute-start | bytes 817160 | tf_op jit(solution)/shard_map/while/body/eval_jaxpr/ppermute | solution.py:22
  719.6 12.4 %collective-permute-start = (bf16[2,56,1216]{2,1,0:T(8,128)(2,1)S(1)}, bf16[2,56,1216]{2,1,0:T(8,128)(2,1)S(1)}, u32[]{:S(2)}, u32[]{:S(2)}) collective-permute-start(bf16[2,56,1216]{2,1,0:T(8,128)(2,1)S(1)} %get-tuple-element.459), channel_id=1, source_target_pairs={{0,1},{1,2},{2,3},{3,4},{4,5},{5,6},{6,7},{7,8},{8,9},{9,10},{10,1... | collective-permute-start | bytes 817160 | tf_op jit(solution)/shard_map/while/body/eval_jaxpr/ppermute | solution.py:22
  721.6 12.2 %collective-permute-start.1 = (bf16[2,56,1216]{2,1,0:T(8,128)(2,1)S(1)}, bf16[2,56,1216]{2,1,0:T(8,128)(2,1)S(1)}, u32[]{:S(2)}, u32[]{:S(2)}) collective-permute-start(bf16[2,56,1216]{2,1,0:T(8,128)(2,1)S(1)} %get-tuple-element.460), channel_id=1, source_target_pairs={{1,0},{2,1},{3,2},{4,3},{5,4},{6,5},{7,6},{8,7},{9,8},{10,9},{11,1... | collective-permute-start | bytes 817160 | tf_op jit(solution)/shard_map/while/body/eval_jaxpr/ppermute | solution.py:22
  735.5 12.4 %collective-permute-start = (bf16[2,56,1216]{2,1,0:T(8,128)(2,1)S(1)}, bf16[2,56,1216]{2,1,0:T(8,128)(2,1)S(1)}, u32[]{:S(2)}, u32[]{:S(2)}) collective-permute-start(bf16[2,56,1216]{2,1,0:T(8,128)(2,1)S(1)} %get-tuple-element.459), channel_id=1, source_target_pairs={{0,1},{1,2},{2,3},{3,4},{4,5},{5,6},{6,7},{7,8},{8,9},{9,10},{10,1... | collective-permute-start | bytes 817160 | tf_op jit(solution)/shard_map/while/body/eval_jaxpr/ppermute | solution.py:22
  737.5 12.2 %collective-permute-start.1 = (bf16[2,56,1216]{2,1,0:T(8,128)(2,1)S(1)}, bf16[2,56,1216]{2,1,0:T(8,128)(2,1)S(1)}, u32[]{:S(2)}, u32[]{:S(2)}) collective-permute-start(bf16[2,56,1216]{2,1,0:T(8,128)(2,1)S(1)} %get-tuple-element.460), channel_id=1, source_target_pairs={{1,0},{2,1},{3,2},{4,3},{5,4},{6,5},{7,6},{8,7},{9,8},{10,9},{11,1... | collective-permute-start | bytes 817160 | tf_op jit(solution)/shard_map/while/body/eval_jaxpr/ppermute | solution.py:22
  751.4 12.4 %collective-permute-start = (bf16[2,56,1216]{2,1,0:T(8,128)(2,1)S(1)}, bf16[2,56,1216]{2,1,0:T(8,128)(2,1)S(1)}, u32[]{:S(2)}, u32[]{:S(2)}) collective-permute-start(bf16[2,56,1216]{2,1,0:T(8,128)(2,1)S(1)} %get-tuple-element.459), channel_id=1, source_target_pairs={{0,1},{1,2},{2,3},{3,4},{4,5},{5,6},{6,7},{7,8},{8,9},{9,10},{10,1... | collective-permute-start | bytes 817160 | tf_op jit(solution)/shard_map/while/body/eval_jaxpr/ppermute | solution.py:22
  753.3 12.2 %collective-permute-start.1 = (bf16[2,56,1216]{2,1,0:T(8,128)(2,1)S(1)}, bf16[2,56,1216]{2,1,0:T(8,128)(2,1)S(1)}, u32[]{:S(2)}, u32[]{:S(2)}) collective-permute-start(bf16[2,56,1216]{2,1,0:T(8,128)(2,1)S(1)} %get-tuple-element.460), channel_id=1, source_target_pairs={{1,0},{2,1},{3,2},{4,3},{5,4},{6,5},{7,6},{8,7},{9,8},{10,9},{11,1... | collective-permute-start | bytes 817160 | tf_op jit(solution)/shard_map/while/body/eval_jaxpr/ppermute | solution.py:22
  767.3 12.4 %collective-permute-start = (bf16[2,56,1216]{2,1,0:T(8,128)(2,1)S(1)}, bf16[2,56,1216]{2,1,0:T(8,128)(2,1)S(1)}, u32[]{:S(2)}, u32[]{:S(2)}) collective-permute-start(bf16[2,56,1216]{2,1,0:T(8,128)(2,1)S(1)} %get-tuple-element.459), channel_id=1, source_target_pairs={{0,1},{1,2},{2,3},{3,4},{4,5},{5,6},{6,7},{7,8},{8,9},{9,10},{10,1... | collective-permute-start | bytes 817160 | tf_op jit(solution)/shard_map/while/body/eval_jaxpr/ppermute | solution.py:22
  769.2 12.2 %collective-permute-start.1 = (bf16[2,56,1216]{2,1,0:T(8,128)(2,1)S(1)}, bf16[2,56,1216]{2,1,0:T(8,128)(2,1)S(1)}, u32[]{:S(2)}, u32[]{:S(2)}) collective-permute-start(bf16[2,56,1216]{2,1,0:T(8,128)(2,1)S(1)} %get-tuple-element.460), channel_id=1, source_target_pairs={{1,0},{2,1},{3,2},{4,3},{5,4},{6,5},{7,6},{8,7},{9,8},{10,9},{11,1... | collective-permute-start | bytes 817160 | tf_op jit(solution)/shard_map/while/body/eval_jaxpr/ppermute | solution.py:22
  783.2 12.4 %collective-permute-start = (bf16[2,56,1216]{2,1,0:T(8,128)(2,1)S(1)}, bf16[2,56,1216]{2,1,0:T(8,128)(2,1)S(1)}, u32[]{:S(2)}, u32[]{:S(2)}) collective-permute-start(bf16[2,56,1216]{2,1,0:T(8,128)(2,1)S(1)} %get-tuple-element.459), channel_id=1, source_target_pairs={{0,1},{1,2},{2,3},{3,4},{4,5},{5,6},{6,7},{7,8},{8,9},{9,10},{10,1... | collective-permute-start | bytes 817160 | tf_op jit(solution)/shard_map/while/body/eval_jaxpr/ppermute | solution.py:22
  785.1 12.2 %collective-permute-start.1 = (bf16[2,56,1216]{2,1,0:T(8,128)(2,1)S(1)}, bf16[2,56,1216]{2,1,0:T(8,128)(2,1)S(1)}, u32[]{:S(2)}, u32[]{:S(2)}) collective-permute-start(bf16[2,56,1216]{2,1,0:T(8,128)(2,1)S(1)} %get-tuple-element.460), channel_id=1, source_target_pairs={{1,0},{2,1},{3,2},{4,3},{5,4},{6,5},{7,6},{8,7},{9,8},{10,9},{11,1... | collective-permute-start | bytes 817160 | tf_op jit(solution)/shard_map/while/body/eval_jaxpr/ppermute | solution.py:22
  799.1 12.4 %collective-permute-start = (bf16[2,56,1216]{2,1,0:T(8,128)(2,1)S(1)}, bf16[2,56,1216]{2,1,0:T(8,128)(2,1)S(1)}, u32[]{:S(2)}, u32[]{:S(2)}) collective-permute-start(bf16[2,56,1216]{2,1,0:T(8,128)(2,1)S(1)} %get-tuple-element.459), channel_id=1, source_target_pairs={{0,1},{1,2},{2,3},{3,4},{4,5},{5,6},{6,7},{7,8},{8,9},{9,10},{10,1... | collective-permute-start | bytes 817160 | tf_op jit(solution)/shard_map/while/body/eval_jaxpr/ppermute | solution.py:22
  801.0 12.2 %collective-permute-start.1 = (bf16[2,56,1216]{2,1,0:T(8,128)(2,1)S(1)}, bf16[2,56,1216]{2,1,0:T(8,128)(2,1)S(1)}, u32[]{:S(2)}, u32[]{:S(2)}) collective-permute-start(bf16[2,56,1216]{2,1,0:T(8,128)(2,1)S(1)} %get-tuple-element.460), channel_id=1, source_target_pairs={{1,0},{2,1},{3,2},{4,3},{5,4},{6,5},{7,6},{8,7},{9,8},{10,9},{11,1... | collective-permute-start | bytes 817160 | tf_op jit(solution)/shard_map/while/body/eval_jaxpr/ppermute | solution.py:22
  (1 other events, 9.6 us)
Sparse Core Ops, SparseCore 0:
  9.2 228.5 all-gather.6
  239.7 249.9 all-gather.4
where the time goes:
time: 831 us; the launch traced here: 827 us
  waiting for transfers between devices  494 us (59%)
  starting transfers between devices  152 us (18%)
  local copies, waits for them, and re-layouts  116 us (14%)
  matrix products  28.1 us (3%)
  other arithmetic  20.2 us (2%)
  between operations  15.3 us (2%)
    all_gather x1, waiting for transfers between devices, per_device(): lax.all_gather(qkv_weight[0], 'seq', axis=0, tiled=True)  227 us
    all_gather x1, waiting for transfers between devices, per_device(): lax.all_gather(out_weight[0], 'seq', axis=1, tiled=True)  218 us
    ppermute x30, starting transfers between devices, passed_along(): lax.ppermute(value, axis, [(source, source + steps) for source in range(l...  149 us
    all_gather x1, local copies, waits for them, and re-layouts, per_device(): lax.all_gather(qkv_weight[0], 'seq', axis=0, tiled=True)  72 us
    ppermute x30, waiting for transfers between devices, passed_along(): lax.ppermute(value, axis, [(source, source + steps) for source in range(l...  49.1 us
    all_gather x1, local copies, waits for them, and re-layouts, per_device(): lax.all_gather(out_weight[0], 'seq', axis=1, tiled=True)  24.8 us
  transfers between devices with their start and end apart: 33, of which 32 were waited for; matrix products, arithmetic and copies ran while one was open for 5% of the time, Pallas kernels for 0%

commit v1 on v0

v1 whole, which is shorter than its diff:
```python
import jax
import jax.numpy as jnp
import numpy as np
from jax import lax
from jax.experimental import pallas as pl
from jax.experimental.pallas import tpu as pltpu
from jax.sharding import Mesh
from jax.sharding import PartitionSpec as P

AXES = ("comp", "x", "z1", "z0", "y", "core")
SIZES = (2, 2, 4, 2, 4, 2)
SEQ = AXES[1:]
Z = ("z1", "z0")
HEADS = 19
HD = 64
YH = 5
YW = YH * HD
HALF = 512
TEXT_ROWS = 8
CHUNK = 152
SLOT = 160
EPSILON = 1e-06
MASKED = -1e30
BF16 = jnp.bfloat16
F32 = jnp.float32


def permuted(array, axis, by):
    devices = lax.axis_size(axis)
    return lax.ppermute(array, axis, [(i, (i + by) % devices) for i in range(devices)])


def beside_kernel(place_ref, mine_ref, other_ref, *refs):
    out_ref, room = refs[-2:]
    x = place_ref[0]
    used = mine_ref.shape[0]
    room[...] = jnp.zeros_like(room)
    mine, other = mine_ref[...].astype(F32), other_ref[...].astype(F32)
    room[:used, :] = jnp.where(x == 0, mine, other)
    room[used : 2 * used, :] = jnp.where(x == 0, other, mine)
    out_ref[...] = room[...].astype(BF16)


def arrange_kernel(gathered_ref, *refs):
    out_ref, room = refs[-2:]
    used = out_ref.shape[0] // gathered_ref.shape[0]
    for place in range(gathered_ref.shape[0]):
        room[place * used : (place + 1) * used, :] = gathered_ref[place].astype(F32)[:used]
    out_ref[...] = room[...].astype(BF16)


def prepare_kernel(weight_ref, text_ref, out_ref, room):
    weight_rows = weight_ref.shape[0]
    head_width = HEADS * HD
    room[...] = jnp.zeros_like(room)
    for y in range(4):
        first = y * YW
        split = HALF - YW
        for core in range(2):
            slot = y * 2 + core
            base = (core + 1) * head_width
            size = min(YW, head_width - first)
            room[slot, :weight_rows, :size] = weight_ref[:, base + first : base + first + size].astype(F32)
            begin = first + core * split
            query_size = min(YW - split if core else split, head_width - begin)
            room[slot, :weight_rows, YW : YW + query_size] = weight_ref[
                :, begin : begin + query_size
            ].astype(F32)
            text = text_ref[core, :, first : first + size].astype(F32)
            room[slot, 19:24, :size] = text[:5]
            room[slot, 19:22, YW:] = text[5:8, :split]
            if size > split:
                room[slot, 22:23, YW : YW + size - split] = text[5:6, split:size]
                room[slot, 23:24, YW : YW + size - split] = text[6:7, split:size]
                room[slot, 22:23, YW + 128 :] = text[7:8, split : split + 64]
            if size == YW:
                room[slot, 23:24, YW + 128 :] = text[7:8, split + 64 :]
    out_ref[...] = room[...].astype(BF16)


def compact_kernel(received_ref, *refs):
    block_ref, text_ref, rows_room, text_room = refs[-4:]
    split = HALF - YW
    rows_room[...] = jnp.zeros_like(rows_room)
    for source in range(8):
        value = received_ref[source].astype(F32)
        rows_room[source * 19 : (source + 1) * 19, :] = value[:19]
        at = source * TEXT_ROWS
        text_room[at : at + 5, :] = value[19:24, :YW]
        text_room[at + 5 : at + 8, :split] = value[19:22, YW:]
        text_room[at + 5 : at + 6, split:] = value[22:23, YW : YW + 128]
        text_room[at + 6 : at + 7, split:] = value[23:24, YW : YW + 128]
        text_room[at + 7 : at + 8, split : split + 64] = value[22:23, YW + 128 :]
        text_room[at + 7 : at + 8, split + 64 :] = value[23:24, YW + 128 :]
    block_ref[...] = rows_room[...].astype(BF16)
    text_ref[...] = text_room[...].astype(BF16)


def modulate_kernel(modulation_ref, raw_ref, *refs):
    h_ref = refs[-1]
    wide = raw_ref[...].astype(F32)
    centred = wide - jnp.mean(wide, axis=-1, keepdims=True)
    normed = centred * lax.rsqrt(jnp.mean(centred * centred, axis=-1, keepdims=True) + EPSILON)
    modulated = normed * (1.0 + modulation_ref[1:2, :]) + modulation_ref[0:1, :]
    modulated = modulated.astype(BF16)
    h_ref[...] = jnp.zeros_like(h_ref)
    for slot in range(16):
        h_ref[:, slot * SLOT : slot * SLOT + CHUNK] = modulated[:, slot * CHUNK : (slot + 1) * CHUNK]


def project_kernel(place_ref, gain_ref, plain_ref, h_ref, text_ref, *refs):
    blocks, (pairs_ref, queries_ref, whole) = refs[:16], refs[16:]
    for index, block in enumerate(blocks):
        whole[place_ref[4 + index]] = block[...]
    rows = h_ref.shape[0]
    pairs_ref[rows:, :] = text_ref[...]
    low = lax.broadcasted_iota(jnp.int32, (rows, 128), 1) < HD
    for tile in range(0, HALF, 256):
        weights = whole[:, :, tile : tile + 256].reshape(16 * SLOT, 256)
        product = jnp.dot(h_ref[...], weights, preferred_element_type=F32)
        for part in range(2):
            begin = tile + part * 128
            columns = slice(begin, begin + 128)
            value = product[:, part * 128 : part * 128 + 128]
            square = value * value
            low_sum = jnp.sum(jnp.where(low, square, 0.0), axis=-1, keepdims=True)
            high_sum = jnp.sum(jnp.where(low, 0.0, square), axis=-1, keepdims=True)
            mean = jnp.where(low, low_sum, high_sum) * (1.0 / HD)
            scaled = value * lax.rsqrt(mean + EPSILON) * gain_ref[:, columns]
            result = jnp.where(plain_ref[:, columns] > 0.0, value, scaled).astype(BF16)
            if begin + 128 <= YW:
                pairs_ref[:rows, columns] = result
            elif begin < YW:
                pairs_ref[:rows, begin:YW] = result[:, : YW - begin]
                queries_ref[:, : begin + 128 - YW] = result[:, YW - begin :]
            else:
                queries_ref[:, begin - YW : begin + 128 - YW] = result


def attend_kernel(place_ref, own, beside, own_q, beside_q, far, far_beside, out_ref, keys, values):
    core, z0, text_valid = place_ref[1], place_ref[2], place_ref[3]
    shard = own.shape[0]
    rows = out_ref.shape[0]
    image = shard - 8 * TEXT_ROWS
    for part, (mine, other) in enumerate(((own, beside), (far, far_beside))):
        at = slice(part * shard, (part + 1) * shard)

        @pl.when(core == 0)
        def _():
            keys[at, :] = mine[...]
            values[at, :] = other[...]

        @pl.when(core == 1)
        def _():
            keys[at, :] = other[...]
            values[at, :] = mine[...]

    column = lax.broadcasted_iota(jnp.int32, (1, 2 * shard), 1)
    is_far = column >= shard
    column = jnp.where(is_far, column - shard, column)
    slot = column - image + 8 * TEXT_ROWS * jnp.where(is_far, 1 - z0, z0)
    bias = jnp.where((column < image) | (slot < text_valid), 0.0, MASKED).astype(F32)
    split = HALF - YW
    each = rows // 4
    places = [pl.ds(pl.multiple_of((2 * y + core) * each, 16), each) for y in range(4)]
    mine, other = (
        jnp.concatenate([ref[at, :] for at in places], 0) for ref in (own_q, beside_q)
    )
    first = jnp.where(core == 0, mine, other)
    second = jnp.where(core == 0, other, mine)
    for head in range(YH):
        columns = slice(head * HD, (head + 1) * HD)
        if head * HD < split:
            queries = first[:, columns]
        else:
            queries = second[:, head * HD - split : (head + 1) * HD - split]
        scores = lax.dot_general(
            queries * BF16(HD**-0.5),
            keys[:, columns],
            (((1,), (1,)), ((), ())),
            preferred_element_type=F32,
        )
        scores = scores + bias
        peak = jnp.max(scores, axis=-1, keepdims=True)
        weights = jnp.exp(scores - peak)
        totals = jnp.sum(weights, axis=-1, keepdims=True)
        mixed = jnp.dot(weights.astype(BF16), values[:, columns], preferred_element_type=F32)
        out_ref[:, columns] = (mixed / totals).astype(BF16)


def finish_kernel(place_ref, a0, a1, a2, a3, own_ref, beside_ref, *refs):
    o0, o1, o2, o3, heads, result, weights = refs
    y, core = place_ref[0], place_ref[1]
    own, beside = own_ref[...].astype(F32), beside_ref[...].astype(F32)
    each = own.shape[0] // 16
    for part, value in enumerate(
        (jnp.where(core == 0, own, beside), jnp.where(core == 0, beside, own))
    ):
        for z in range(8):
            for x in range(2):
                at = ((x * 8 + z) * 2 + part) * each
                begin = (z * 2 + x) * each
                weights[at : at + each, :] = value[begin : begin + each]
    weight = weights[...].astype(BF16)
    for by, attended in enumerate((a0, a1, a2, a3)):
        heads[lax.rem(y + 4 - by, 4)] = attended[...]
    total = None
    for q in range(4):
        size = min(YW, HEADS * HD - q * YW)
        part = lax.dot_general(
            heads[q][:, :size],
            weight[:, q * YW : q * YW + size],
            (((1,), (1,)), ((), ())),
            preferred_element_type=F32,
        )
        total = part if total is None else total + part
    rows = o0.shape[0]
    result[...] = total.astype(BF16).reshape(4, rows, total.shape[1])
    for by, out_ref in enumerate((o0, o1, o2, o3)):
        out_ref[...] = result[lax.rem(y + by, 4)]


def assemble_kernel(place_ref, gate_ref, raw_ref, n0, n1, n2, n3, out_ref, branch):
    y = place_ref[0]
    run = n0.shape[1] // 16
    for by, part in enumerate((n0, n1, n2, n3)):
        value = part[...].astype(F32)
        for q in range(4):

            @pl.when(lax.rem(y + 4 - by, 4) == q)
            def _():
                for m in range(16):
                    at = (m * 4 + q) * run
                    branch[:, at : at + run] = value[:, m * run : (m + 1) * run]

    out_ref[...] = (raw_ref[...].astype(F32) + gate_ref[...] * branch[...]).astype(BF16)


def in_vmem(kernel, out_shape, args, flops=0, scratch=(), scalars=0, after=()):
    size = sum(a.size * a.dtype.itemsize for a in args)
    vmem = pl.BlockSpec(memory_space=pltpu.VMEM)
    return pl.pallas_call(
        kernel,
        out_shape=out_shape,
        in_specs=[pl.BlockSpec(memory_space=pltpu.SMEM)] * scalars
        + [vmem] * (len(args) - scalars)
        + [vmem] * len(after),
        out_specs=jax.tree.map(lambda _: vmem, out_shape),
        scratch_shapes=list(scratch),
        compiler_params=pltpu.CompilerParams(vmem_limit_bytes=16 * 1024 * 1024),
        cost_estimate=pl.CostEstimate(flops=flops, bytes_accessed=size, transcendentals=0),
    )(*args, *after)


def per_device(
    stale_states, mod_table, timesteps, text_count, text_kv, qkv_weight, out_weight, qk_gain
):
    rows, width = stale_states.shape[1:]
    head_width = HEADS * HD
    weight_rows = qkv_weight.shape[1]
    quarter = width // 4
    split = HALF - YW
    x, y, core, z0 = (lax.axis_index(name) for name in ("x", "y", "core", "z0"))
    z = lax.axis_index(Z)
    sequence = lax.axis_index(("x", "z1"))

    halves = in_vmem(
        prepare_kernel,
        jax.ShapeDtypeStruct((8, 24, HALF), BF16),
        (qkv_weight[0], text_kv),
        scratch=[pltpu.VMEM((8, 24, HALF), F32)],
    )
    received = lax.all_to_all(halves, ("y", "core"), split_axis=0, concat_axis=0, tiled=True)
    shard = jnp.transpose(out_weight[0])
    shard_beside = permuted(shard, "x", 1)

    raw = permuted(stale_states[0], "comp", 1)
    step_index = lax.dynamic_index_in_dim(timesteps, sequence, 0, False)
    modulation = lax.dynamic_index_in_dim(mod_table[0], step_index, 0, False)
    text_valid = lax.dynamic_index_in_dim(text_count, sequence, 0, False)
    gate = modulation[2:3]
    h = in_vmem(
        modulate_kernel,
        jax.ShapeDtypeStruct((rows, 16 * SLOT), BF16),
        (modulation, raw),
        after=(received, shard_beside),
    )
    block, text = in_vmem(
        compact_kernel,
        (
            jax.ShapeDtypeStruct((SLOT, HALF), BF16),
            jax.ShapeDtypeStruct((8 * TEXT_ROWS, YW), BF16),
        ),
        (received,),
        scratch=[pltpu.VMEM((SLOT, HALF), F32), pltpu.VMEM((8 * TEXT_ROWS, YW), F32)],
        after=(h,),
    )
    h = lax.all_gather(h, ("y", "core"), axis=0, tiled=True)

    gains = jnp.pad(qk_gain[0], ((0, 0), (0, 4 * YW - head_width)))
    gains = lax.dynamic_slice_in_dim(gains, y * YW, YW, 1)
    first_gain = jnp.concatenate([gains[1], gains[0, :split]])
    second_gain = jnp.concatenate(
        [jnp.ones((YW,), F32), gains[0, split:], jnp.ones((2 * HALF - 3 * YW,), F32)]
    )
    gain = jnp.where(core == 0, first_gain, second_gain)[None]
    plain = jnp.where((core == 1) & (jnp.arange(HALF) < YW), 1.0, 0.0).astype(F32)[None]

    ahead = lambda part: permuted(part, Z, 1)
    behind = lambda part: permuted(part, Z, 7)
    other = permuted(block, "x", 1)
    own_aheads, own_behinds = [ahead(block)], [behind(block)]
    other_aheads, other_behinds = [ahead(other)], [behind(other)]
    for step in range(2, 5):
        own_aheads.append(ahead(own_aheads[-1]))
        other_behinds.append(behind(other_behinds[-1]))
        if step < 4:
            own_behinds.append(behind(own_behinds[-1]))
            other_aheads.append(ahead(other_aheads[-1]))
    blocks = [(block, x, z), (other, 1 - x, z)]
    for step in range(1, 5):
        blocks.append((own_aheads[step - 1], x, z + 8 - step))
        blocks.append((other_behinds[step - 1], 1 - x, z + step))
        if step < 4:
            blocks.append((own_behinds[step - 1], x, z + step))
            blocks.append((other_aheads[step - 1], 1 - x, z + 8 - step))
    slots = [x_place * 8 + z_place % 8 for _, x_place, z_place in blocks]
    blocks = [part for part, _, _ in blocks]

    place = jnp.stack([y, core, z0, text_valid] + slots).astype(jnp.int32)
    both = in_vmem(
        beside_kernel,
        jax.ShapeDtypeStruct((56, head_width), BF16),
        (x.astype(jnp.int32)[None], shard, shard_beside),
        scratch=[pltpu.VMEM((56, head_width), F32)],
        scalars=1,
        after=(own_aheads[1], own_behinds[1], other_aheads[0], other_behinds[0]),
    )
    out_half = lax.all_gather(both, Z, axis=0, tiled=False)

    shard_rows = 8 * (rows + TEXT_ROWS)
    pairs, queries = in_vmem(
        project_kernel,
        (
            jax.ShapeDtypeStruct((shard_rows, YW), BF16),
            jax.ShapeDtypeStruct((8 * rows, split), BF16),
        ),
        (place, gain, plain, h, text, *blocks),
        flops=2 * 8 * rows * 16 * SLOT * HALF,
        scratch=[pltpu.VMEM((16, SLOT, HALF), BF16)],
        scalars=1,
    )

    far = permuted(pairs, "z0", 1)
    attended = in_vmem(
        attend_kernel,
        jax.ShapeDtypeStruct((4 * rows, YW), BF16),
        (
            place,
            pairs,
            permuted(pairs, "core", 1),
            queries,
            permuted(queries, "core", 1),
            far,
            permuted(far, "core", 1),
        ),
        flops=4 * 4 * rows * 2 * shard_rows * YW,
        scratch=[pltpu.VMEM((2 * shard_rows, YW), BF16)] * 2,
        scalars=1,
    )

    gathered = tuple(permuted(attended, "y", by) for by in (1, 2, 3))
    out_half = in_vmem(
        arrange_kernel,
        jax.ShapeDtypeStruct((16 * weight_rows, head_width), BF16),
        (out_half,),
        scratch=[pltpu.VMEM((16 * weight_rows, head_width), F32)],
        after=(attended,),
    )
    parts = in_vmem(
        finish_kernel,
        (jax.ShapeDtypeStruct((rows, quarter), BF16),) * 4,
        (place, attended)
        + gathered
        + (out_half, permuted(out_half, "core", 1)),
        flops=2 * 4 * rows * head_width * quarter,
        scratch=[
            pltpu.VMEM((4, 4 * rows, YW), BF16),
            pltpu.VMEM((4, rows, quarter), BF16),
            pltpu.VMEM((32 * weight_rows, head_width), F32),
        ],
        scalars=1,
    )
    parts = [parts[0]] + [permuted(parts[by], "y", by) for by in (1, 2, 3)]
    new = in_vmem(
        assemble_kernel,
        jax.ShapeDtypeStruct((rows, width), BF16),
        (place, gate, raw, *parts),
        scratch=[pltpu.VMEM((rows, width), F32)],
        scalars=1,
    )
    return new[None]


def solution(mesh):
    fine = Mesh(np.asarray(mesh.devices).reshape(SIZES), AXES)
    in_specs = (
        P("comp", SEQ, None),
        P("comp", None, None, None),
        P(),
        P(),
        P(None, SEQ, None),
        P("comp", SEQ, None),
        P("comp", None, SEQ),
        P("comp", None, None),
    )
    return jax.shard_map(
        per_device, mesh=fine, in_specs=in_specs, out_specs=P("comp", SEQ, None), check_vma=False
    )
```

time: 831 us -> 125 us (0.15)
  waiting for transfers between devices: 494 us -> 42.1 us
  starting transfers between devices: 152 us -> 43.1 us
  local copies, waits for them, and re-layouts: 116 us -> 10.5 us
  matrix products: 28.1 us -> 0 us
  other arithmetic: 20.2 us -> 0.08 us
  Pallas kernels: 0 us -> 12.9 us
    all_gather x2, waiting for transfers between devices: 445 us -> 4.06 us  [the longest x1 4.06 us: per_device(): out_half = lax.all_gather(both, Z, axis=0, tiled=False)]
    ppermute x31 -> x28, starting transfers between devices: 152 us -> 38.5 us  [permuted(): lax.ppermute(array, axis, [(i, (i + by) % devices) for i in range(devices)])]
    all_gather x2 -> x0, local copies, waits for them, and re-layouts: 96.8 us -> none  [the longest x1 72 us: per_device(): lax.all_gather(qkv_weight[0], 'seq', axis=0, tiled=True)]
    dot_general x34 -> x0, matrix products: 28.1 us -> none  [the longest x1 11.3 us: per_device(): jnp.dot(modulated, lax.all_gather(qkv_weight[0], 'seq', axis=0, tiled=Tru...]
    ppermute x31 -> x28, waiting for transfers between devices: 49.1 us -> 36 us  [permuted(): lax.ppermute(array, axis, [(i, (i + by) % devices) for i in range(devices)])]
    pallas_call x0 -> x9, Pallas kernels: none -> 12.9 us  [in_vmem(): pl.pallas_call(kernel, out_shape=out_shape, in_specs=[pl.BlockSpec(memory...]
    select_n x16 -> x1, other arithmetic: 10.3 us -> 0.08 us  [per_device(): jnp.where((core == 1) & (jnp.arange(HALF) < YW), 1.0, 0.0).astype(F32)[None]]
  transfers between devices with their start and end apart: 33 -> 31, of which waited for: 32 -> 17; matrix products, arithmetic and copies ran while one was open for 5% -> 2% of each run, Pallas kernels for 0% -> 6%
where the time goes in v1:
time: 125 us; the launch traced here: 124 us
  starting transfers between devices  43.1 us (34%)
  waiting for transfers between devices  42.1 us (34%)
  between operations  15.5 us (12%)
  Pallas kernels  12.9 us (10%)
  local copies, waits for them, and re-layouts  10.5 us (8%)
    ppermute x28, starting transfers between devices, permuted(): lax.ppermute(array, axis, [(i, (i + by) % devices) for i in range(devices)])  38.5 us
    ppermute x28, waiting for transfers between devices, permuted(): lax.ppermute(array, axis, [(i, (i + by) % devices) for i in range(devices)])  36 us
    pallas_call x9, Pallas kernels, in_vmem(): pl.pallas_call(kernel, out_shape=out_shape, in_specs=[pl.BlockSpec(memory...  12.9 us
    unnamed x25, local copies, waits for them, and re-layouts  7.68 us
    all_to_all x1, starting transfers between devices, per_device(): lax.all_to_all(halves, ('y', 'core'), split_axis=0, concat_axis=0, tiled=...  4.47 us
    all_gather x1, waiting for transfers between devices, per_device(): out_half = lax.all_gather(both, Z, axis=0, tiled=False)  4.06 us
  transfers between devices with their start and end apart: 31, of which 17 were waited for; matrix products, arithmetic and copies ran while one was open for 2% of the time, Pallas kernels for 6%

profile of v1, /device:TPU:2, one launch (start us, length us, event | category | flops | bytes accessed | tf_op | source)
XLA Modules:
  0.0 124.2 jit_solution(15593356829644334412)
XLA Ops:
  6.5 2.1 %collective-permute-start = (bf16[48,2432]{1,0:T(8,128)(2,1)}, bf16[48,2432]{1,0:T(8,128)(2,1)S(1)}, u32[]{:S(2)}, u32[]{:S(2)}) collective-permute-start(bf16[48,2432]{1,0:T(8,128)(2,1)} %bitcast.46), channel_id=1, source_target_pairs={{0,128},{128,0},{1,129},{129,1},{2,130},{130,2},{3,131},{131,3},{4... | collective-permute-start | bytes 700424 | tf_op jit(solution)/shard_map/ppermute | solution.py:30
  11.2 4.5 %all-to-all-start = ((bf16[8,24,512]{2,1,0:T(8,128)(2,1)}), bf16[8,24,512]{2,1,0:T(8,128)(2,1)S(1)}, u32[]{:S(2)}, u32[]{:S(2)}) async-start(bf16[8,24,512]{2,1,0:T(8,128)(2,1)} %shard_map.82), calls=%async_computation | async-start | bytes 393216 | tf_op jit(solution)/shard_map/all_to_all | solution.py:273
  15.7 1.5 %collective-permute-start.1 = (bf16[19,1216]{1,0:T(8,128)(2,1)}, bf16[19,1216]{1,0:T(8,128)(2,1)S(1)}, u32[]{:S(2)}, u32[]{:S(2)}) collective-permute-start(bf16[19,1216]{1,0:T(8,128)(2,1)} %bitcast.39), channel_id=1, source_target_pairs={{0,64},{64,0},{1,65},{65,1},{2,66},{66,2},{3,67},{67,3},{4,68},{68... | collective-permute-start | bytes 138632 | tf_op jit(solution)/shard_map/ppermute | solution.py:30
  20.5 2.0 %all-to-all-done.refs_0_.received_ref = bf16[8,24,512]{2,1,0:T(8,128)(2,1)S(1)} async-done(((bf16[8,24,512]{2,1,0:T(8,128)(2,1)}), bf16[8,24,512]{2,1,0:T(8,128)(2,1)S(1)}, u32[]{:S(2)}, u32[]{:S(2)}) %all-to-all-start) | async-done | bytes 196640 | tf_op jit(solution)/shard_map/all_to_all | solution.py:273
  24.8 1.5 %collective-permute-start.2 = (bf16[160,512]{1,0:T(8,128)(2,1)S(1)}, bf16[160,512]{1,0:T(8,128)(2,1)S(1)}, u32[]{:S(2)}, u32[]{:S(2)}) collective-permute-start(bf16[160,512]{1,0:T(8,128)(2,1)S(1)} %get-tuple-element.14.refs_0_), channel_id=1, source_target_pairs={{0,64},{64,0},{1,65},{65,1},{2,66},{66,2},{3,67},{67,3},{4,68},{68... | collective-permute-start | bytes 491528 | tf_op jit(solution)/shard_map/ppermute | solution.py:30
  26.3 1.9 %collective-permute-start.3 = (bf16[160,512]{1,0:T(8,128)(2,1)S(1)}, bf16[160,512]{1,0:T(8,128)(2,1)S(1)}, u32[]{:S(2)}, u32[]{:S(2)}) collective-permute-start(bf16[160,512]{1,0:T(8,128)(2,1)S(1)} %get-tuple-element.14.refs_0_), channel_id=1, source_target_pairs={{0,8},{8,16},{16,24},{24,32},{32,40},{40,48},{48,56},{56,0},{1,9},... | collective-permute-start | bytes 491528 | tf_op jit(solution)/shard_map/ppermute | solution.py:30
  28.2 3.9 %collective-permute-start.5 = (bf16[160,512]{1,0:T(8,128)(2,1)S(1)}, bf16[160,512]{1,0:T(8,128)(2,1)S(1)}, u32[]{:S(2)}, u32[]{:S(2)}) collective-permute-start(bf16[160,512]{1,0:T(8,128)(2,1)S(1)} %get-tuple-element.14.refs_0_), channel_id=1, source_target_pairs={{0,56},{8,0},{16,8},{24,16},{32,24},{40,32},{48,40},{56,48},{1,57}... | collective-permute-start | bytes 491528 | tf_op jit(solution)/shard_map/ppermute | solution.py:30
  32.2 4.2 %collective-permute-start.4 = (bf16[160,512]{1,0:T(8,128)(2,1)S(1)}, bf16[160,512]{1,0:T(8,128)(2,1)S(1)}, u32[]{:S(2)}, u32[]{:S(2)}) collective-permute-start(bf16[160,512]{1,0:T(8,128)(2,1)S(1)} %collective-permute-done.2.refs_1_), channel_id=1, source_target_pairs={{0,56},{8,0},{16,8},{24,16},{32,24},{40,32},{48,40},{56,48},{1,57}... | collective-permute-start | bytes 491528 | tf_op jit(solution)/shard_map/ppermute | solution.py:30
  36.4 3.3 %collective-permute-start.9 = (bf16[160,512]{1,0:T(8,128)(2,1)S(1)}, bf16[160,512]{1,0:T(8,128)(2,1)S(1)}, u32[]{:S(2)}, u32[]{:S(2)}) collective-permute-start(bf16[160,512]{1,0:T(8,128)(2,1)S(1)} %collective-permute-done.5.refs_4_), channel_id=1, source_target_pairs={{0,56},{8,0},{16,8},{24,16},{32,24},{40,32},{48,40},{56,48},{1,57}... | collective-permute-start | bytes 491528 | tf_op jit(solution)/shard_map/ppermute | solution.py:30
  40.6 3.2 %collective-permute-done.6.refs_5_.refs_2_ = bf16[160,512]{1,0:T(8,128)(2,1)S(1)} collective-permute-done((bf16[160,512]{1,0:T(8,128)(2,1)S(1)}, bf16[160,512]{1,0:T(8,128)(2,1)S(1)}, u32[]{:S(2)}, u32[]{:S(2)}) %collective-permute-start.6) | collective-permute-done | bytes 163872 | tf_op jit(solution)/shard_map/ppermute | solution.py:30
  43.8 1.8 %collective-permute-done.7.refs_6_.refs_0_ = bf16[160,512]{1,0:T(8,128)(2,1)S(1)} collective-permute-done((bf16[160,512]{1,0:T(8,128)(2,1)S(1)}, bf16[160,512]{1,0:T(8,128)(2,1)S(1)}, u32[]{:S(2)}, u32[]{:S(2)}) %collective-permute-start.7) | collective-permute-done | bytes 163872 | tf_op jit(solution)/shard_map/ppermute | solution.py:30
  48.6 3.8 %collective-permute-done.8.refs_7_ = bf16[160,512]{1,0:T(8,128)(2,1)S(1)} collective-permute-done((bf16[160,512]{1,0:T(8,128)(2,1)S(1)}, bf16[160,512]{1,0:T(8,128)(2,1)S(1)}, u32[]{:S(2)}, u32[]{:S(2)}) %collective-permute-start.8) | collective-permute-done | bytes 163872 | tf_op jit(solution)/shard_map/ppermute | solution.py:30
  55.4 2.0 %collective-permute-start.14 = (bf16[160,512]{1,0:T(8,128)(2,1)S(1)}, bf16[160,512]{1,0:T(8,128)(2,1)S(1)}, u32[]{:S(2)}, u32[]{:S(2)}) collective-permute-start(bf16[160,512]{1,0:T(8,128)(2,1)S(1)} %collective-permute-done.10.refs_9_), channel_id=1, source_target_pairs={{0,8},{8,16},{16,24},{24,32},{32,40},{40,48},{48,56},{56,0},{1,9},... | collective-permute-start | bytes 491528 | tf_op jit(solution)/shard_map/ppermute | solution.py:30
  58.0 1.4 %collective-permute-done.12.refs_11_ = bf16[160,512]{1,0:T(8,128)(2,1)S(1)} collective-permute-done((bf16[160,512]{1,0:T(8,128)(2,1)S(1)}, bf16[160,512]{1,0:T(8,128)(2,1)S(1)}, u32[]{:S(2)}, u32[]{:S(2)}) %collective-permute-start.12) | collective-permute-done | bytes 163872 | tf_op jit(solution)/shard_map/ppermute | solution.py:30
  60.7 1.4 %collective-permute-done.13.refs_12_ = bf16[160,512]{1,0:T(8,128)(2,1)S(1)} collective-permute-done((bf16[160,512]{1,0:T(8,128)(2,1)S(1)}, bf16[160,512]{1,0:T(8,128)(2,1)S(1)}, u32[]{:S(2)}, u32[]{:S(2)}) %collective-permute-start.13) | collective-permute-done | bytes 163872 | tf_op jit(solution)/shard_map/ppermute | solution.py:30
  62.1 1.8 %collective-permute-done.15.refs_14_ = bf16[160,512]{1,0:T(8,128)(2,1)S(1)} collective-permute-done((bf16[160,512]{1,0:T(8,128)(2,1)S(1)}, bf16[160,512]{1,0:T(8,128)(2,1)S(1)}, u32[]{:S(2)}, u32[]{:S(2)}) %collective-permute-start.15) | collective-permute-done | bytes 163872 | tf_op jit(solution)/shard_map/ppermute | solution.py:30
  65.4 1.5 %copy-done.1 = bf16[384,2560]{1,0:T(8,128)(2,1)S(1)} copy-done((bf16[384,2560]{1,0:T(8,128)(2,1)S(1)}, bf16[384,2560]{1,0:T(8,128)(2,1)}, u32[]{:S(2)}) %copy-start.1) | copy-done | bytes 1966104
  68.8 2.4 %shard_map.85 = (bf16[448,320]{1,0:T(8,128)(2,1)S(1)}, bf16[384,192]{1,0:T(8,128)(2,1)S(1)}) custom-call(s32[20]{0:T(128)S(1)} %stack.80.place_ref, f32[1,512]{1,0:T(1,128)S(1)} %get-tuple-element.22.gain_ref, f32[1,512]{1,0:T(1,128)S(1)} %get-tuple-element.21.plain_ref, bf16[384,2560]{1,0:T(8,128)(2,1)S(1)} %copy-done.1, ...), custom_call_target="tpu_custom_call" | custom-call | flops 1006632960 | bytes 4632656 | tf_op jit(solution)/shard_map/pallas_call | solution.py:242
  71.9 11.7 %collective-permute-done.19.far = bf16[448,320]{1,0:T(8,128)(2,1)S(1)} collective-permute-done((bf16[448,320]{1,0:T(8,128)(2,1)S(1)}, bf16[448,320]{1,0:T(8,128)(2,1)S(1)}, u32[]{:S(2)}, u32[]{:S(2)}) %collective-permute-start.19) | collective-permute-done | bytes 286752 | tf_op jit(solution)/shard_map/ppermute | solution.py:30
  84.1 1.4 %collective-permute-done.18.beside_q = bf16[384,192]{1,0:T(8,128)(2,1)S(1)} collective-permute-done((bf16[384,192]{1,0:T(8,128)(2,1)S(1)}, bf16[384,192]{1,0:T(8,128)(2,1)S(1)}, u32[]{:S(2)}, u32[]{:S(2)}) %collective-permute-start.18) | collective-permute-done | bytes 147488 | tf_op jit(solution)/shard_map/ppermute | solution.py:30
  85.5 2.9 %shard_map.86.refs_0_.a0 = bf16[192,320]{1,0:T(8,128)(2,1)S(1)} custom-call(s32[20]{0:T(128)S(1)} %stack.80.place_ref, bf16[448,320]{1,0:T(8,128)(2,1)S(1)} %get-tuple-element.15.own, bf16[448,320]{1,0:T(8,128)(2,1)S(1)} %collective-permute-done.17.beside, bf16[384,192]{1,0:T(8,128)(2,1)S(1)} %get-tuple-element.16.own_q, ...), custom_call_target="tpu_custom_call" | custom-call | flops 220200960 | bytes 1441872 | tf_op jit(solution)/shard_map/pallas_call | solution.py:242
  88.4 4.1 %all-gather.6.cloned.1.call-done = bf16[448,1216]{1,0:T(8,128)(2,1)} async-done(((bf16[56,1216]{1,0:T(8,128)(2,1)}), bf16[448,1216]{1,0:T(8,128)(2,1)}) %all-gather.6.cloned.1.call-update) | async-done | bytes 1089552 | tf_op jit(solution)/shard_map/all_gather | solution.py:339
  94.0 1.7 %collective-permute-start.21 = (bf16[192,320]{1,0:T(8,128)(2,1)S(1)}, bf16[192,320]{1,0:T(8,128)(2,1)S(1)}, u32[]{:S(2)}, u32[]{:S(2)}) collective-permute-start(bf16[192,320]{1,0:T(8,128)(2,1)S(1)} %shard_map.86.refs_0_.a0), channel_id=1, source_target_pairs={{0,2},{2,4},{4,6},{6,0},{1,3},{3,5},{5,7},{7,1},{8,10},{10,12},{12... | collective-permute-start | bytes 368648 | tf_op jit(solution)/shard_map/ppermute | solution.py:30
  95.8 2.5 %collective-permute-start.22 = (bf16[192,320]{1,0:T(8,128)(2,1)S(1)}, bf16[192,320]{1,0:T(8,128)(2,1)S(1)}, u32[]{:S(2)}, u32[]{:S(2)}) collective-permute-start(bf16[192,320]{1,0:T(8,128)(2,1)S(1)} %shard_map.86.refs_0_.a0), channel_id=1, source_target_pairs={{0,4},{2,6},{4,0},{6,2},{1,5},{3,7},{5,1},{7,3},{8,12},{10,14},{12... | collective-permute-start | bytes 368648 | tf_op jit(solution)/shard_map/ppermute | solution.py:30
  98.3 1.5 %collective-permute-start.23 = (bf16[192,320]{1,0:T(8,128)(2,1)S(1)}, bf16[192,320]{1,0:T(8,128)(2,1)S(1)}, u32[]{:S(2)}, u32[]{:S(2)}) collective-permute-start(bf16[192,320]{1,0:T(8,128)(2,1)S(1)} %shard_map.86.refs_0_.a0), channel_id=1, source_target_pairs={{0,6},{2,0},{4,2},{6,4},{1,7},{3,1},{5,3},{7,5},{8,14},{10,8},{12,... | collective-permute-start | bytes 368648 | tf_op jit(solution)/shard_map/ppermute | solution.py:30
  99.8 1.7 %collective-permute-done.21.a1 = bf16[192,320]{1,0:T(8,128)(2,1)S(1)} collective-permute-done((bf16[192,320]{1,0:T(8,128)(2,1)S(1)}, bf16[192,320]{1,0:T(8,128)(2,1)S(1)}, u32[]{:S(2)}, u32[]{:S(2)}) %collective-permute-start.21) | collective-permute-done | bytes 122912 | tf_op jit(solution)/shard_map/ppermute | solution.py:30
  101.5 4.1 %collective-permute-done.22.a2 = bf16[192,320]{1,0:T(8,128)(2,1)S(1)} collective-permute-done((bf16[192,320]{1,0:T(8,128)(2,1)S(1)}, bf16[192,320]{1,0:T(8,128)(2,1)S(1)}, u32[]{:S(2)}, u32[]{:S(2)}) %collective-permute-start.22) | collective-permute-done | bytes 122912 | tf_op jit(solution)/shard_map/ppermute | solution.py:30
  105.6 1.8 %shard_map.89 = (bf16[48,608]{1,0:T(8,128)(2,1)S(1)}, bf16[48,608]{1,0:T(8,128)(2,1)S(1)}, bf16[48,608]{1,0:T(8,128)(2,1)S(1)}, bf16[48,608]{1,0:T(8,128)(2,1)S(1)}) custom-call(s32[20]{0:T(128)S(1)} %stack.80.place_ref, bf16[192,320]{1,0:T(8,128)(2,1)S(1)} %shard_map.86.refs_0_.a0, bf16[192,320]{1,0:T(8,128)(2,1)S(1)} %collective-permute-done.21.a1, ...), custom_call_target="tpu_custom_call" | custom-call | flops 283901952 | bytes 1970256 | tf_op jit(solution)/shard_map/pallas_call | solution.py:242
  107.4 1.5 %collective-permute-start.25 = (bf16[48,608]{1,0:T(8,128)(2,1)S(1)}, bf16[48,608]{1,0:T(8,128)(2,1)S(1)}, u32[]{:S(2)}, u32[]{:S(2)}) collective-permute-start(bf16[48,608]{1,0:T(8,128)(2,1)S(1)} %get-tuple-element.18), channel_id=1, source_target_pairs={{0,2},{2,4},{4,6},{6,0},{1,3},{3,5},{5,7},{7,1},{8,10},{10,12},{12... | collective-permute-start | bytes 175112 | tf_op jit(solution)/shard_map/ppermute | solution.py:30
  108.8 2.4 %collective-permute-start.26 = (bf16[48,608]{1,0:T(8,128)(2,1)S(1)}, bf16[48,608]{1,0:T(8,128)(2,1)S(1)}, u32[]{:S(2)}, u32[]{:S(2)}) collective-permute-start(bf16[48,608]{1,0:T(8,128)(2,1)S(1)} %get-tuple-element.19), channel_id=1, source_target_pairs={{0,4},{2,6},{4,0},{6,2},{1,5},{3,7},{5,1},{7,3},{8,12},{10,14},{12... | collective-permute-start | bytes 175112 | tf_op jit(solution)/shard_map/ppermute | solution.py:30
  111.2 1.6 %collective-permute-start.27 = (bf16[48,608]{1,0:T(8,128)(2,1)S(1)}, bf16[48,608]{1,0:T(8,128)(2,1)S(1)}, u32[]{:S(2)}, u32[]{:S(2)}) collective-permute-start(bf16[48,608]{1,0:T(8,128)(2,1)S(1)} %get-tuple-element.20), channel_id=1, source_target_pairs={{0,6},{2,0},{4,2},{6,4},{1,7},{3,1},{5,3},{7,5},{8,14},{10,8},{12,... | collective-permute-start | bytes 175112 | tf_op jit(solution)/shard_map/ppermute | solution.py:30
  115.5 1.9 %shard_map.90 = bf16[48,2432]{1,0:T(8,128)(2,1)} custom-call(s32[20]{0:T(128)S(1)} %stack.80.place_ref, f32[1,2432]{1,0:T(1,128)S(1)} %dynamic-slice_bitcast_fusion.gate_ref, bf16[48,2432]{1,0:T(8,128)(2,1)S(1)} %collective-permute-done.raw_ref, bf16[48,608]{1,0:T(8,128)(2,1)S(1)} %get-tuple-element.17.n0, bf16[48,608]{1,0:T(8,128)(2,1)S(1)} %collective-permute-done.25.n1, ...), custom_call_target="tpu_custom_call" | custom-call | bytes 476752 | tf_op jit(solution)/shard_map/pallas_call | solution.py:242
  (79 shorter events, 23.6 us)
Async XLA Ops:
  6.5 47.3 %copy-start.11 = (s32[8]{0:T(128)S(1)}, s32[8]{0:T(128)}, u32[]{:S(2)}) copy-start(s32[8]{0:T(128)} %param.11) | copy-start | bytes 100
  6.5 16.0 %collective-permute-start = (bf16[48,2432]{1,0:T(8,128)(2,1)}, bf16[48,2432]{1,0:T(8,128)(2,1)S(1)}, u32[]{:S(2)}, u32[]{:S(2)}) collective-permute-start(bf16[48,2432]{1,0:T(8,128)(2,1)} %bitcast.46), channel_id=1, source_target_pairs={{0,128},{128,0},{1,129},{129,1},{2,130},{130,2},{3,131},{131,3},{4... | collective-permute-start | bytes 700424 | tf_op jit(solution)/shard_map/ppermute | solution.py:30
  11.2 11.3 %all-to-all-start = ((bf16[8,24,512]{2,1,0:T(8,128)(2,1)}), bf16[8,24,512]{2,1,0:T(8,128)(2,1)S(1)}, u32[]{:S(2)}, u32[]{:S(2)}) async-start(bf16[8,24,512]{2,1,0:T(8,128)(2,1)} %shard_map.82), calls=%async_computation | async-start | bytes 393216 | tf_op jit(solution)/shard_map/all_to_all | solution.py:273
  15.7 49.7 %all-gather.4.cloned.1.call-start = ((), (), s32[]{:S(2)}) async-start(), calls=%async_computation.1 | async-start | bytes 2211840 | tf_op jit(solution)/shard_map/all_gather | solution.py:298
  15.7 4.8 %collective-permute-start.1 = (bf16[19,1216]{1,0:T(8,128)(2,1)}, bf16[19,1216]{1,0:T(8,128)(2,1)S(1)}, u32[]{:S(2)}, u32[]{:S(2)}) collective-permute-start(bf16[19,1216]{1,0:T(8,128)(2,1)} %bitcast.39), channel_id=1, source_target_pairs={{0,64},{64,0},{1,65},{65,1},{2,66},{66,2},{3,67},{67,3},{4,68},{68... | collective-permute-start | bytes 138632 | tf_op jit(solution)/shard_map/ppermute | solution.py:30
  23.7 68.8 %all-gather.6.cloned.1.call-start = ((), (), s32[]{:S(2)}) async-start(), calls=%async_computation.2 | async-start | bytes 1290240 | tf_op jit(solution)/shard_map/all_gather | solution.py:339
  24.8 7.4 %collective-permute-start.2 = (bf16[160,512]{1,0:T(8,128)(2,1)S(1)}, bf16[160,512]{1,0:T(8,128)(2,1)S(1)}, u32[]{:S(2)}, u32[]{:S(2)}) collective-permute-start(bf16[160,512]{1,0:T(8,128)(2,1)S(1)} %get-tuple-element.14.refs_0_), channel_id=1, source_target_pairs={{0,64},{64,0},{1,65},{65,1},{2,66},{66,2},{3,67},{67,3},{4,68},{68... | collective-permute-start | bytes 491528 | tf_op jit(solution)/shard_map/ppermute | solution.py:30
  26.3 10.1 %collective-permute-start.3 = (bf16[160,512]{1,0:T(8,128)(2,1)S(1)}, bf16[160,512]{1,0:T(8,128)(2,1)S(1)}, u32[]{:S(2)}, u32[]{:S(2)}) collective-permute-start(bf16[160,512]{1,0:T(8,128)(2,1)S(1)} %get-tuple-element.14.refs_0_), channel_id=1, source_target_pairs={{0,8},{8,16},{16,24},{24,32},{32,40},{40,48},{48,56},{56,0},{1,9},... | collective-permute-start | bytes 491528 | tf_op jit(solution)/shard_map/ppermute | solution.py:30
  28.2 8.2 %collective-permute-start.5 = (bf16[160,512]{1,0:T(8,128)(2,1)S(1)}, bf16[160,512]{1,0:T(8,128)(2,1)S(1)}, u32[]{:S(2)}, u32[]{:S(2)}) collective-permute-start(bf16[160,512]{1,0:T(8,128)(2,1)S(1)} %get-tuple-element.14.refs_0_), channel_id=1, source_target_pairs={{0,56},{8,0},{16,8},{24,16},{32,24},{40,32},{48,40},{56,48},{1,57}... | collective-permute-start | bytes 491528 | tf_op jit(solution)/shard_map/ppermute | solution.py:30
  32.2 8.5 %collective-permute-start.4 = (bf16[160,512]{1,0:T(8,128)(2,1)S(1)}, bf16[160,512]{1,0:T(8,128)(2,1)S(1)}, u32[]{:S(2)}, u32[]{:S(2)}) collective-permute-start(bf16[160,512]{1,0:T(8,128)(2,1)S(1)} %collective-permute-done.2.refs_1_), channel_id=1, source_target_pairs={{0,56},{8,0},{16,8},{24,16},{32,24},{40,32},{48,40},{56,48},{1,57}... | collective-permute-start | bytes 491528 | tf_op jit(solution)/shard_map/ppermute | solution.py:30
  36.4 7.4 %collective-permute-start.6 = (bf16[160,512]{1,0:T(8,128)(2,1)S(1)}, bf16[160,512]{1,0:T(8,128)(2,1)S(1)}, u32[]{:S(2)}, u32[]{:S(2)}) collective-permute-start(bf16[160,512]{1,0:T(8,128)(2,1)S(1)} %collective-permute-done.2.refs_1_), channel_id=1, source_target_pairs={{0,8},{8,16},{16,24},{24,32},{32,40},{40,48},{48,56},{56,0},{1,9},... | collective-permute-start | bytes 491528 | tf_op jit(solution)/shard_map/ppermute | solution.py:30
  36.4 9.2 %collective-permute-start.7 = (bf16[160,512]{1,0:T(8,128)(2,1)S(1)}, bf16[160,512]{1,0:T(8,128)(2,1)S(1)}, u32[]{:S(2)}, u32[]{:S(2)}) collective-permute-start(bf16[160,512]{1,0:T(8,128)(2,1)S(1)} %collective-permute-done.3.refs_2_), channel_id=1, source_target_pairs={{0,8},{8,16},{16,24},{24,32},{32,40},{40,48},{48,56},{56,0},{1,9},... | collective-permute-start | bytes 491528 | tf_op jit(solution)/shard_map/ppermute | solution.py:30
  36.4 9.2 %collective-permute-start.9 = (bf16[160,512]{1,0:T(8,128)(2,1)S(1)}, bf16[160,512]{1,0:T(8,128)(2,1)S(1)}, u32[]{:S(2)}, u32[]{:S(2)}) collective-permute-start(bf16[160,512]{1,0:T(8,128)(2,1)S(1)} %collective-permute-done.5.refs_4_), channel_id=1, source_target_pairs={{0,56},{8,0},{16,8},{24,16},{32,24},{40,32},{48,40},{56,48},{1,57}... | collective-permute-start | bytes 491528 | tf_op jit(solution)/shard_map/ppermute | solution.py:30
  46.3 6.0 %collective-permute-start.8 = (bf16[160,512]{1,0:T(8,128)(2,1)S(1)}, bf16[160,512]{1,0:T(8,128)(2,1)S(1)}, u32[]{:S(2)}, u32[]{:S(2)}) collective-permute-start(bf16[160,512]{1,0:T(8,128)(2,1)S(1)} %collective-permute-done.4.refs_3_), channel_id=1, source_target_pairs={{0,56},{8,0},{16,8},{24,16},{32,24},{40,32},{48,40},{56,48},{1,57}... | collective-permute-start | bytes 491528 | tf_op jit(solution)/shard_map/ppermute | solution.py:30
  47.3 8.0 %collective-permute-start.10 = (bf16[160,512]{1,0:T(8,128)(2,1)S(1)}, bf16[160,512]{1,0:T(8,128)(2,1)S(1)}, u32[]{:S(2)}, u32[]{:S(2)}) collective-permute-start(bf16[160,512]{1,0:T(8,128)(2,1)S(1)} %collective-permute-done.6.refs_5_.refs_2_), channel_id=1, source_target_pairs={{0,8},{8,16},{16,24},{24,32},{32,40},{40,48},{48,56},{56,0},{1,9},... | collective-permute-start | bytes 491528 | tf_op jit(solution)/shard_map/ppermute | solution.py:30
  48.5 8.8 %collective-permute-start.11 = (bf16[160,512]{1,0:T(8,128)(2,1)S(1)}, bf16[160,512]{1,0:T(8,128)(2,1)S(1)}, u32[]{:S(2)}, u32[]{:S(2)}) collective-permute-start(bf16[160,512]{1,0:T(8,128)(2,1)S(1)} %collective-permute-done.7.refs_6_.refs_0_), channel_id=1, source_target_pairs={{0,8},{8,16},{16,24},{24,32},{32,40},{40,48},{48,56},{56,0},{1,9},... | collective-permute-start | bytes 491528 | tf_op jit(solution)/shard_map/ppermute | solution.py:30
  52.4 7.0 %collective-permute-start.12 = (bf16[160,512]{1,0:T(8,128)(2,1)S(1)}, bf16[160,512]{1,0:T(8,128)(2,1)S(1)}, u32[]{:S(2)}, u32[]{:S(2)}) collective-permute-start(bf16[160,512]{1,0:T(8,128)(2,1)S(1)} %collective-permute-done.8.refs_7_), channel_id=1, source_target_pairs={{0,56},{8,0},{16,8},{24,16},{32,24},{40,32},{48,40},{56,48},{1,57}... | collective-permute-start | bytes 491528 | tf_op jit(solution)/shard_map/ppermute | solution.py:30
  55.3 6.8 %collective-permute-start.13 = (bf16[160,512]{1,0:T(8,128)(2,1)S(1)}, bf16[160,512]{1,0:T(8,128)(2,1)S(1)}, u32[]{:S(2)}, u32[]{:S(2)}) collective-permute-start(bf16[160,512]{1,0:T(8,128)(2,1)S(1)} %collective-permute-done.9.refs_8_.refs_1_), channel_id=1, source_target_pairs={{0,56},{8,0},{16,8},{24,16},{32,24},{40,32},{48,40},{56,48},{1,57}... | collective-permute-start | bytes 491528 | tf_op jit(solution)/shard_map/ppermute | solution.py:30
  55.4 6.7 %collective-permute-start.14 = (bf16[160,512]{1,0:T(8,128)(2,1)S(1)}, bf16[160,512]{1,0:T(8,128)(2,1)S(1)}, u32[]{:S(2)}, u32[]{:S(2)}) collective-permute-start(bf16[160,512]{1,0:T(8,128)(2,1)S(1)} %collective-permute-done.10.refs_9_), channel_id=1, source_target_pairs={{0,8},{8,16},{16,24},{24,32},{32,40},{40,48},{48,56},{56,0},{1,9},... | collective-permute-start | bytes 491528 | tf_op jit(solution)/shard_map/ppermute | solution.py:30
  57.4 6.5 %collective-permute-start.15 = (bf16[160,512]{1,0:T(8,128)(2,1)S(1)}, bf16[160,512]{1,0:T(8,128)(2,1)S(1)}, u32[]{:S(2)}, u32[]{:S(2)}) collective-permute-start(bf16[160,512]{1,0:T(8,128)(2,1)S(1)} %collective-permute-done.11.refs_10_), channel_id=1, source_target_pairs={{0,8},{8,16},{16,24},{24,32},{32,40},{40,48},{48,56},{56,0},{1,9},... | collective-permute-start | bytes 491528 | tf_op jit(solution)/shard_map/ppermute | solution.py:30
  59.4 5.3 %collective-permute-start.16 = (bf16[160,512]{1,0:T(8,128)(2,1)S(1)}, bf16[160,512]{1,0:T(8,128)(2,1)S(1)}, u32[]{:S(2)}, u32[]{:S(2)}) collective-permute-start(bf16[160,512]{1,0:T(8,128)(2,1)S(1)} %collective-permute-done.12.refs_11_), channel_id=1, source_target_pairs={{0,56},{8,0},{16,8},{24,16},{32,24},{40,32},{48,40},{56,48},{1,57}... | collective-permute-start | bytes 491528 | tf_op jit(solution)/shard_map/ppermute | solution.py:30
  71.2 12.4 %collective-permute-start.19 = (bf16[448,320]{1,0:T(8,128)(2,1)S(1)}, bf16[448,320]{1,0:T(8,128)(2,1)S(1)}, u32[]{:S(2)}, u32[]{:S(2)}) collective-permute-start(bf16[448,320]{1,0:T(8,128)(2,1)S(1)} %get-tuple-element.15.own), channel_id=1, source_target_pairs={{0,8},{8,0},{1,9},{9,1},{2,10},{10,2},{3,11},{11,3},{4,12},{12,4},... | collective-permute-start | bytes 860168 | tf_op jit(solution)/shard_map/ppermute | solution.py:30
  71.9 13.6 %collective-permute-start.17 = (bf16[448,320]{1,0:T(8,128)(2,1)S(1)}, bf16[448,320]{1,0:T(8,128)(2,1)S(1)}, u32[]{:S(2)}, u32[]{:S(2)}) collective-permute-start(bf16[448,320]{1,0:T(8,128)(2,1)S(1)} %get-tuple-element.15.own), channel_id=1, source_target_pairs={{0,1},{1,0},{2,3},{3,2},{4,5},{5,4},{6,7},{7,6},{8,9},{9,8},{10,11... | collective-permute-start | bytes 860168 | tf_op jit(solution)/shard_map/ppermute | solution.py:30
  83.6 1.9 %collective-permute-start.20 = (bf16[448,320]{1,0:T(8,128)(2,1)S(1)}, bf16[448,320]{1,0:T(8,128)(2,1)S(1)}, u32[]{:S(2)}, u32[]{:S(2)}) collective-permute-start(bf16[448,320]{1,0:T(8,128)(2,1)S(1)} %collective-permute-done.19.far), channel_id=1, source_target_pairs={{0,1},{1,0},{2,3},{3,2},{4,5},{5,4},{6,7},{7,6},{8,9},{9,8},{10,11... | collective-permute-start | bytes 860168 | tf_op jit(solution)/shard_map/ppermute | solution.py:30
  83.6 1.9 %collective-permute-start.18 = (bf16[384,192]{1,0:T(8,128)(2,1)S(1)}, bf16[384,192]{1,0:T(8,128)(2,1)S(1)}, u32[]{:S(2)}, u32[]{:S(2)}) collective-permute-start(bf16[384,192]{1,0:T(8,128)(2,1)S(1)} %get-tuple-element.16.own_q), channel_id=1, source_target_pairs={{0,1},{1,0},{2,3},{3,2},{4,5},{5,4},{6,7},{7,6},{8,9},{9,8},{10,11... | collective-permute-start | bytes 442376 | tf_op jit(solution)/shard_map/ppermute | solution.py:30
  93.9 11.7 %collective-permute-start.24 = (bf16[304,1216]{1,0:T(8,128)(2,1)S(1)}, bf16[304,1216]{1,0:T(8,128)(2,1)S(1)}, u32[]{:S(2)}, u32[]{:S(2)}) collective-permute-start(bf16[304,1216]{1,0:T(8,128)(2,1)S(1)} %shard_map.88.own_ref), channel_id=1, source_target_pairs={{0,1},{1,0},{2,3},{3,2},{4,5},{5,4},{6,7},{7,6},{8,9},{9,8},{10,11... | collective-permute-start | bytes 2217992 | tf_op jit(solution)/shard_map/ppermute | solution.py:30
  94.0 7.5 %collective-permute-start.21 = (bf16[192,320]{1,0:T(8,128)(2,1)S(1)}, bf16[192,320]{1,0:T(8,128)(2,1)S(1)}, u32[]{:S(2)}, u32[]{:S(2)}) collective-permute-start(bf16[192,320]{1,0:T(8,128)(2,1)S(1)} %shard_map.86.refs_0_.a0), channel_id=1, source_target_pairs={{0,2},{2,4},{4,6},{6,0},{1,3},{3,5},{5,7},{7,1},{8,10},{10,12},{12... | collective-permute-start | bytes 368648 | tf_op jit(solution)/shard_map/ppermute | solution.py:30
  95.8 9.8 %collective-permute-start.22 = (bf16[192,320]{1,0:T(8,128)(2,1)S(1)}, bf16[192,320]{1,0:T(8,128)(2,1)S(1)}, u32[]{:S(2)}, u32[]{:S(2)}) collective-permute-start(bf16[192,320]{1,0:T(8,128)(2,1)S(1)} %shard_map.86.refs_0_.a0), channel_id=1, source_target_pairs={{0,4},{2,6},{4,0},{6,2},{1,5},{3,7},{5,1},{7,3},{8,12},{10,14},{12... | collective-permute-start | bytes 368648 | tf_op jit(solution)/shard_map/ppermute | solution.py:30
  98.3 7.3 %collective-permute-start.23 = (bf16[192,320]{1,0:T(8,128)(2,1)S(1)}, bf16[192,320]{1,0:T(8,128)(2,1)S(1)}, u32[]{:S(2)}, u32[]{:S(2)}) collective-permute-start(bf16[192,320]{1,0:T(8,128)(2,1)S(1)} %shard_map.86.refs_0_.a0), channel_id=1, source_target_pairs={{0,6},{2,0},{4,2},{6,4},{1,7},{3,1},{5,3},{7,5},{8,14},{10,8},{12,... | collective-permute-start | bytes 368648 | tf_op jit(solution)/shard_map/ppermute | solution.py:30
  107.4 6.2 %collective-permute-start.25 = (bf16[48,608]{1,0:T(8,128)(2,1)S(1)}, bf16[48,608]{1,0:T(8,128)(2,1)S(1)}, u32[]{:S(2)}, u32[]{:S(2)}) collective-permute-start(bf16[48,608]{1,0:T(8,128)(2,1)S(1)} %get-tuple-element.18), channel_id=1, source_target_pairs={{0,2},{2,4},{4,6},{6,0},{1,3},{3,5},{5,7},{7,1},{8,10},{10,12},{12... | collective-permute-start | bytes 175112 | tf_op jit(solution)/shard_map/ppermute | solution.py:30
  108.8 5.7 %collective-permute-start.26 = (bf16[48,608]{1,0:T(8,128)(2,1)S(1)}, bf16[48,608]{1,0:T(8,128)(2,1)S(1)}, u32[]{:S(2)}, u32[]{:S(2)}) collective-permute-start(bf16[48,608]{1,0:T(8,128)(2,1)S(1)} %get-tuple-element.19), channel_id=1, source_target_pairs={{0,4},{2,6},{4,0},{6,2},{1,5},{3,7},{5,1},{7,3},{8,12},{10,14},{12... | collective-permute-start | bytes 175112 | tf_op jit(solution)/shard_map/ppermute | solution.py:30
  111.2 4.2 %collective-permute-start.27 = (bf16[48,608]{1,0:T(8,128)(2,1)S(1)}, bf16[48,608]{1,0:T(8,128)(2,1)S(1)}, u32[]{:S(2)}, u32[]{:S(2)}) collective-permute-start(bf16[48,608]{1,0:T(8,128)(2,1)S(1)} %get-tuple-element.20), channel_id=1, source_target_pairs={{0,6},{2,0},{4,2},{6,4},{1,7},{3,1},{5,3},{7,5},{8,14},{10,8},{12,... | collective-permute-start | bytes 175112 | tf_op jit(solution)/shard_map/ppermute | solution.py:30
  (11 other events, 93.6 us)
Sparse Core Ops, SparseCore 0:
  23.8 27.6 all-gather.3
  53.3 39.1 all-gather.5

commit v2 on v1

--- a/solution.py
+++ b/solution.py
@@ -38,14 +38,6 @@
     mine, other = mine_ref[...].astype(F32), other_ref[...].astype(F32)
     room[:used, :] = jnp.where(x == 0, mine, other)
     room[used : 2 * used, :] = jnp.where(x == 0, other, mine)
-    out_ref[...] = room[...].astype(BF16)
-
-
-def arrange_kernel(gathered_ref, *refs):
-    out_ref, room = refs[-2:]
-    used = out_ref.shape[0] // gathered_ref.shape[0]
-    for place in range(gathered_ref.shape[0]):
-        room[place * used : (place + 1) * used, :] = gathered_ref[place].astype(F32)[:used]
     out_ref[...] = room[...].astype(BF16)
 
 
@@ -113,7 +105,11 @@
     for index, block in enumerate(blocks):
         whole[place_ref[4 + index]] = block[...]
     rows = h_ref.shape[0]
-    pairs_ref[rows:, :] = text_ref[...]
+    shard = pairs_ref.shape[0] * 2 // YH
+    half = shard // 2
+    pairs_ref[rows:shard, :] = text_ref[:, :128]
+    pairs_ref[shard + rows : 2 * shard, :] = text_ref[:, 128:256]
+    pairs_ref[shard + half + rows :, HD:] = text_ref[:, 256:]
     low = lax.broadcasted_iota(jnp.int32, (rows, 128), 1) < HD
     for tile in range(0, HALF, 256):
         weights = whole[:, :, tile : tile + 256].reshape(16 * SLOT, 256)
@@ -129,31 +125,41 @@
             scaled = value * lax.rsqrt(mean + EPSILON) * gain_ref[:, columns]
             result = jnp.where(plain_ref[:, columns] > 0.0, value, scaled).astype(BF16)
             if begin + 128 <= YW:
-                pairs_ref[:rows, columns] = result
+                pairs_ref[begin // 128 * shard : begin // 128 * shard + rows, :] = result
             elif begin < YW:
-                pairs_ref[:rows, begin:YW] = result[:, : YW - begin]
-                queries_ref[:, : begin + 128 - YW] = result[:, YW - begin :]
+                pairs_ref[2 * shard :, :HD] = result[:half, :HD]
+                pairs_ref[2 * shard : shard + half + rows, HD:] = result[half:, :HD]
+                queries_ref[:, :HD] = result[:, HD:]
             else:
                 queries_ref[:, begin - YW : begin + 128 - YW] = result
 
 
+def unpack(packed, room, part):
+    shard = packed.shape[0] * 2 // YH
+    half = shard // 2
+    begin = part * shard
+    room[0, begin : begin + shard, :] = packed[:shard, :]
+    room[1, begin : begin + shard, :] = packed[shard : 2 * shard, :]
+    room[2, begin : begin + half, :HD] = packed[2 * shard :, :HD]
+    room[2, begin + half : begin + shard, :HD] = packed[2 * shard :, HD:]
+
+
 def attend_kernel(place_ref, own, beside, own_q, beside_q, far, far_beside, out_ref, keys, values):
     core, z0, text_valid = place_ref[1], place_ref[2], place_ref[3]
-    shard = own.shape[0]
-    rows = out_ref.shape[0]
+    shard = own.shape[0] * 2 // YH
+    rows = out_ref.shape[0] * 2 // YH
     image = shard - 8 * TEXT_ROWS
     for part, (mine, other) in enumerate(((own, beside), (far, far_beside))):
-        at = slice(part * shard, (part + 1) * shard)
 
         @pl.when(core == 0)
         def _():
-            keys[at, :] = mine[...]
-            values[at, :] = other[...]
+            unpack(mine, keys, part)
+            unpack(other, values, part)
 
         @pl.when(core == 1)
         def _():
-            keys[at, :] = other[...]
-            values[at, :] = mine[...]
+            unpack(other, keys, part)
+            unpack(mine, values, part)
 
     column = lax.broadcasted_iota(jnp.int32, (1, 2 * shard), 1)
     is_far = column >= shard
@@ -162,6 +168,7 @@
     bias = jnp.where((column < image) | (slot < text_valid), 0.0, MASKED).astype(F32)
     split = HALF - YW
     each = rows // 4
+    half = rows // 2
     places = [pl.ds(pl.multiple_of((2 * y + core) * each, 16), each) for y in range(4)]
     mine, other = (
         jnp.concatenate([ref[at, :] for at in places], 0) for ref in (own_q, beside_q)
@@ -170,13 +177,14 @@
     second = jnp.where(core == 0, other, mine)
     for head in range(YH):
         columns = slice(head * HD, (head + 1) * HD)
+        lanes = head % 2 * HD
         if head * HD < split:
             queries = first[:, columns]
         else:
             queries = second[:, head * HD - split : (head + 1) * HD - split]
         scores = lax.dot_general(
             queries * BF16(HD**-0.5),
-            keys[:, columns],
+            keys[head // 2, :, lanes : lanes + HD],
             (((1,), (1,)), ((), ())),
             preferred_element_type=F32,
         )
@@ -184,26 +192,40 @@
         peak = jnp.max(scores, axis=-1, keepdims=True)
         weights = jnp.exp(scores - peak)
         totals = jnp.sum(weights, axis=-1, keepdims=True)
-        mixed = jnp.dot(weights.astype(BF16), values[:, columns], preferred_element_type=F32)
-        out_ref[:, columns] = (mixed / totals).astype(BF16)
-
-
-def finish_kernel(place_ref, a0, a1, a2, a3, own_ref, beside_ref, *refs):
+        mixed = jnp.dot(
+            weights.astype(BF16),
+            values[head // 2, :, lanes : lanes + HD],
+            preferred_element_type=F32,
+        )
+        attended = (mixed / totals).astype(BF16)
+        at = head // 2 * rows
+        if head < YH - 1:
+            out_ref[at : at + rows, lanes : lanes + HD] = attended
+        else:
+            out_ref[at : at + half, :HD] = attended[:half]
+            out_ref[at : at + half, HD:] = attended[half:]
+
+
+def finish_kernel(place_ref, a0, a1, a2, a3, gathered_ref, *refs):
     o0, o1, o2, o3, heads, result, weights = refs
-    y, core = place_ref[0], place_ref[1]
-    own, beside = own_ref[...].astype(F32), beside_ref[...].astype(F32)
-    each = own.shape[0] // 16
-    for part, value in enumerate(
-        (jnp.where(core == 0, own, beside), jnp.where(core == 0, beside, own))
-    ):
-        for z in range(8):
-            for x in range(2):
-                at = ((x * 8 + z) * 2 + part) * each
-                begin = (z * 2 + x) * each
-                weights[at : at + each, :] = value[begin : begin + each]
+    y = place_ref[0]
+    each = weights.shape[0] // 32
+    gap = gathered_ref.shape[0] // 16
+    for place in range(16):
+        value = gathered_ref[place * gap : (place + 1) * gap, :].astype(F32)
+        z, core = divmod(place, 2)
+        for x in range(2):
+            at = ((x * 8 + z) * 2 + core) * each
+            weights[at : at + each, :] = value[x * each : (x + 1) * each]
     weight = weights[...].astype(BF16)
+    rows = a0.shape[0] * 2 // YH
+    half = rows // 2
     for by, attended in enumerate((a0, a1, a2, a3)):
-        heads[lax.rem(y + 4 - by, 4)] = attended[...]
+        place = lax.rem(y + 4 - by, 4)
+        heads[place, :, :128] = attended[:rows, :]
+        heads[place, :, 128:256] = attended[rows : 2 * rows, :]
+        heads[place, :half, 256:YW] = attended[2 * rows :, :HD]
+        heads[place, half:, 256:YW] = attended[2 * rows :, HD:]
     total = None
     for q in range(4):
         size = min(YW, HEADS * HD - q * YW)
@@ -247,7 +269,7 @@
         + [vmem] * len(after),
         out_specs=jax.tree.map(lambda _: vmem, out_shape),
         scratch_shapes=list(scratch),
-        compiler_params=pltpu.CompilerParams(vmem_limit_bytes=16 * 1024 * 1024),
+        compiler_params=pltpu.CompilerParams(vmem_limit_bytes=10 * 1024 * 1024),
         cost_estimate=pl.CostEstimate(flops=flops, bytes_accessed=size, transcendentals=0),
     )(*args, *after)
 
@@ -283,7 +305,7 @@
         modulate_kernel,
         jax.ShapeDtypeStruct((rows, 16 * SLOT), BF16),
         (modulation, raw),
-        after=(received, shard_beside),
+        after=(shard_beside,),
     )
     block, text = in_vmem(
         compact_kernel,
@@ -292,6 +314,7 @@
             jax.ShapeDtypeStruct((8 * TEXT_ROWS, YW), BF16),
         ),
         (received,),
+        flops=7 * 10**10,
         scratch=[pltpu.VMEM((SLOT, HALF), F32), pltpu.VMEM((8 * TEXT_ROWS, YW), F32)],
         after=(h,),
     )
@@ -330,19 +353,19 @@
     place = jnp.stack([y, core, z0, text_valid] + slots).astype(jnp.int32)
     both = in_vmem(
         beside_kernel,
-        jax.ShapeDtypeStruct((56, head_width), BF16),
+        jax.ShapeDtypeStruct((40, head_width), BF16),
         (x.astype(jnp.int32)[None], shard, shard_beside),
-        scratch=[pltpu.VMEM((56, head_width), F32)],
+        scratch=[pltpu.VMEM((40, head_width), F32)],
         scalars=1,
         after=(own_aheads[1], own_behinds[1], other_aheads[0], other_behinds[0]),
     )
-    out_half = lax.all_gather(both, Z, axis=0, tiled=False)
+    out_columns = lax.all_gather(both, ("z1", "z0", "core"), axis=0, tiled=True)
 
     shard_rows = 8 * (rows + TEXT_ROWS)
     pairs, queries = in_vmem(
         project_kernel,
         (
-            jax.ShapeDtypeStruct((shard_rows, YW), BF16),
+            jax.ShapeDtypeStruct((shard_rows // 2 * YH, 128), BF16),
             jax.ShapeDtypeStruct((8 * rows, split), BF16),
         ),
         (place, gain, plain, h, text, *blocks),
@@ -354,7 +377,7 @@
     far = permuted(pairs, "z0", 1)
     attended = in_vmem(
         attend_kernel,
-        jax.ShapeDtypeStruct((4 * rows, YW), BF16),
+        jax.ShapeDtypeStruct((2 * rows * YH, 128), BF16),
         (
             place,
             pairs,
@@ -365,24 +388,17 @@
             permuted(far, "core", 1),
         ),
         flops=4 * 4 * rows * 2 * shard_rows * YW,
-        scratch=[pltpu.VMEM((2 * shard_rows, YW), BF16)] * 2,
+        scratch=[pltpu.VMEM((3, 2 * shard_rows, 128), BF16)] * 2,
         scalars=1,
     )
 
     gathered = tuple(permuted(attended, "y", by) for by in (1, 2, 3))
-    out_half = in_vmem(
-        arrange_kernel,
-        jax.ShapeDtypeStruct((16 * weight_rows, head_width), BF16),
-        (out_half,),
-        scratch=[pltpu.VMEM((16 * weight_rows, head_width), F32)],
-        after=(attended,),
-    )
     parts = in_vmem(
         finish_kernel,
         (jax.ShapeDtypeStruct((rows, quarter), BF16),) * 4,
         (place, attended)
         + gathered
-        + (out_half, permuted(out_half, "core", 1)),
+        + (out_columns,),
         flops=2 * 4 * rows * head_width * quarter,
         scratch=[
             pltpu.VMEM((4, 4 * rows, YW), BF16),

time: 125 us -> 116 us (0.928)
  waiting for transfers between devices: 42.1 us -> 36.4 us
  starting transfers between devices: 43.1 us -> 39.7 us
    ppermute x28 -> x27, waiting for transfers between devices: 36 us -> 30.4 us  [permuted(): lax.ppermute(array, axis, [(i, (i + by) % devices) for i in range(devices)])]
    ppermute x28 -> x27, starting transfers between devices: 38.5 us -> 35.2 us  [permuted(): lax.ppermute(array, axis, [(i, (i + by) % devices) for i in range(devices)])]
    pallas_call x9 -> x8, Pallas kernels: 12.9 us -> 12.8 us  [in_vmem(): pl.pallas_call(kernel, out_shape=out_shape, in_specs=[pl.BlockSpec(memory...]
  transfers between devices with their start and end apart: 31 -> 30, of which waited for: 17 -> 17; matrix products, arithmetic and copies ran while one was open for 2% -> 3% of each run, Pallas kernels for 6% -> 8%
where the time goes in v2:
time: 116 us; the launch traced here: 115 us
  starting transfers between devices  39.7 us (34%)
  waiting for transfers between devices  36.4 us (31%)
  between operations  15.5 us (13%)
  Pallas kernels  12.8 us (11%)
  local copies, waits for them, and re-layouts  10.7 us (9%)
    ppermute x27, starting transfers between devices, permuted(): lax.ppermute(array, axis, [(i, (i + by) % devices) for i in range(devices)])  35.2 us
    ppermute x27, waiting for transfers between devices, permuted(): lax.ppermute(array, axis, [(i, (i + by) % devices) for i in range(devices)])  30.4 us
    pallas_call x8, Pallas kernels, in_vmem(): pl.pallas_call(kernel, out_shape=out_shape, in_specs=[pl.BlockSpec(memory...  12.8 us
    unnamed x25, local copies, waits for them, and re-layouts  7.87 us
    all_to_all x1, starting transfers between devices, per_device(): lax.all_to_all(halves, ('y', 'core'), split_axis=0, concat_axis=0, tiled=...  4.47 us
    all_gather x1, waiting for transfers between devices, per_device(): out_columns = lax.all_gather(both, ('z1', 'z0', 'core'), axis=0, tiled=True)  3.65 us
  transfers between devices with their start and end apart: 30, of which 17 were waited for; matrix products, arithmetic and copies ran while one was open for 3% of the time, Pallas kernels for 8%

profile of v2, /device:TPU:2, one launch (start us, length us, event | category | flops | bytes accessed | tf_op | source)
XLA Modules:
  0.0 115.2 jit_solution(12235297772656132790)
XLA Ops:
  6.5 2.1 %collective-permute-start = (bf16[48,2432]{1,0:T(8,128)(2,1)}, bf16[48,2432]{1,0:T(8,128)(2,1)S(1)}, u32[]{:S(2)}, u32[]{:S(2)}) collective-permute-start(bf16[48,2432]{1,0:T(8,128)(2,1)} %bitcast.44), channel_id=1, source_target_pairs={{0,128},{128,0},{1,129},{129,1},{2,130},{130,2},{3,131},{131,3},{4... | collective-permute-start | bytes 700424 | tf_op jit(solution)/shard_map/ppermute | solution.py:30
  8.7 1.4 %collective-permute-start.1 = (bf16[19,1216]{1,0:T(8,128)(2,1)}, bf16[19,1216]{1,0:T(8,128)(2,1)S(1)}, u32[]{:S(2)}, u32[]{:S(2)}) collective-permute-start(bf16[19,1216]{1,0:T(8,128)(2,1)} %bitcast.37), channel_id=1, source_target_pairs={{0,64},{64,0},{1,65},{65,1},{2,66},{66,2},{3,67},{67,3},{4,68},{68... | collective-permute-start | bytes 138632 | tf_op jit(solution)/shard_map/ppermute | solution.py:30
  12.6 4.5 %all-to-all-start = ((bf16[8,24,512]{2,1,0:T(8,128)(2,1)}), bf16[8,24,512]{2,1,0:T(8,128)(2,1)S(1)}, u32[]{:S(2)}, u32[]{:S(2)}) async-start(bf16[8,24,512]{2,1,0:T(8,128)(2,1)} %shard_map.83), calls=%async_computation | async-start | bytes 393216 | tf_op jit(solution)/shard_map/all_to_all | solution.py:295
  17.1 1.3 %dynamic_slice.15 = s32[1]{0:T(128)} dynamic-slice(s32[8]{0:T(128)} %param.10, s32[]{:T(128)S(6)} %select_n.89), dynamic_slice_sizes={1} | dynamic-slice | bytes 12 | tf_op jit(solution)/shard_map/jit(dynamic_index_in_dim)/dynamic_slice | solution.py:300
  21.6 2.3 %all-to-all-done.received_ref = bf16[8,24,512]{2,1,0:T(8,128)(2,1)S(1)} async-done(((bf16[8,24,512]{2,1,0:T(8,128)(2,1)}), bf16[8,24,512]{2,1,0:T(8,128)(2,1)S(1)}, u32[]{:S(2)}, u32[]{:S(2)}) %all-to-all-start) | async-done | bytes 196640 | tf_op jit(solution)/shard_map/all_to_all | solution.py:295
  25.7 1.9 %collective-permute-start.3 = (bf16[160,512]{1,0:T(8,128)(2,1)S(1)}, bf16[160,512]{1,0:T(8,128)(2,1)S(1)}, u32[]{:S(2)}, u32[]{:S(2)}) collective-permute-start(bf16[160,512]{1,0:T(8,128)(2,1)S(1)} %get-tuple-element.14.refs_0_), channel_id=1, source_target_pairs={{0,8},{8,16},{16,24},{24,32},{32,40},{40,48},{48,56},{56,0},{1,9},... | collective-permute-start | bytes 491528 | tf_op jit(solution)/shard_map/ppermute | solution.py:30
  27.6 3.9 %collective-permute-start.5 = (bf16[160,512]{1,0:T(8,128)(2,1)S(1)}, bf16[160,512]{1,0:T(8,128)(2,1)S(1)}, u32[]{:S(2)}, u32[]{:S(2)}) collective-permute-start(bf16[160,512]{1,0:T(8,128)(2,1)S(1)} %get-tuple-element.14.refs_0_), channel_id=1, source_target_pairs={{0,56},{8,0},{16,8},{24,16},{32,24},{40,32},{48,40},{56,48},{1,57}... | collective-permute-start | bytes 491528 | tf_op jit(solution)/shard_map/ppermute | solution.py:30
  31.5 5.1 %collective-permute-start.4 = (bf16[160,512]{1,0:T(8,128)(2,1)S(1)}, bf16[160,512]{1,0:T(8,128)(2,1)S(1)}, u32[]{:S(2)}, u32[]{:S(2)}) collective-permute-start(bf16[160,512]{1,0:T(8,128)(2,1)S(1)} %collective-permute-done.2.refs_1_), channel_id=1, source_target_pairs={{0,56},{8,0},{16,8},{24,16},{32,24},{40,32},{48,40},{56,48},{1,57}... | collective-permute-start | bytes 491528 | tf_op jit(solution)/shard_map/ppermute | solution.py:30
  36.6 3.3 %collective-permute-start.9 = (bf16[160,512]{1,0:T(8,128)(2,1)S(1)}, bf16[160,512]{1,0:T(8,128)(2,1)S(1)}, u32[]{:S(2)}, u32[]{:S(2)}) collective-permute-start(bf16[160,512]{1,0:T(8,128)(2,1)S(1)} %collective-permute-done.5.refs_4_), channel_id=1, source_target_pairs={{0,56},{8,0},{16,8},{24,16},{32,24},{40,32},{48,40},{56,48},{1,57}... | collective-permute-start | bytes 491528 | tf_op jit(solution)/shard_map/ppermute | solution.py:30
  40.8 3.2 %collective-permute-done.6.refs_5_.refs_2_ = bf16[160,512]{1,0:T(8,128)(2,1)S(1)} collective-permute-done((bf16[160,512]{1,0:T(8,128)(2,1)S(1)}, bf16[160,512]{1,0:T(8,128)(2,1)S(1)}, u32[]{:S(2)}, u32[]{:S(2)}) %collective-permute-start.6) | collective-permute-done | bytes 163872 | tf_op jit(solution)/shard_map/ppermute | solution.py:30
  44.0 1.8 %collective-permute-done.7.refs_6_.refs_0_ = bf16[160,512]{1,0:T(8,128)(2,1)S(1)} collective-permute-done((bf16[160,512]{1,0:T(8,128)(2,1)S(1)}, bf16[160,512]{1,0:T(8,128)(2,1)S(1)}, u32[]{:S(2)}, u32[]{:S(2)}) %collective-permute-start.7) | collective-permute-done | bytes 163872 | tf_op jit(solution)/shard_map/ppermute | solution.py:30
  48.8 3.8 %collective-permute-done.8.refs_7_ = bf16[160,512]{1,0:T(8,128)(2,1)S(1)} collective-permute-done((bf16[160,512]{1,0:T(8,128)(2,1)S(1)}, bf16[160,512]{1,0:T(8,128)(2,1)S(1)}, u32[]{:S(2)}, u32[]{:S(2)}) %collective-permute-start.8) | collective-permute-done | bytes 163872 | tf_op jit(solution)/shard_map/ppermute | solution.py:30
  52.6 1.4 %collective-permute-start.12 = (bf16[160,512]{1,0:T(8,128)(2,1)S(1)}, bf16[160,512]{1,0:T(8,128)(2,1)S(1)}, u32[]{:S(2)}, u32[]{:S(2)}) collective-permute-start(bf16[160,512]{1,0:T(8,128)(2,1)S(1)} %collective-permute-done.8.refs_7_), channel_id=1, source_target_pairs={{0,56},{8,0},{16,8},{24,16},{32,24},{40,32},{48,40},{56,48},{1,57}... | collective-permute-start | bytes 491528 | tf_op jit(solution)/shard_map/ppermute | solution.py:30
  55.5 2.0 %collective-permute-start.14 = (bf16[160,512]{1,0:T(8,128)(2,1)S(1)}, bf16[160,512]{1,0:T(8,128)(2,1)S(1)}, u32[]{:S(2)}, u32[]{:S(2)}) collective-permute-start(bf16[160,512]{1,0:T(8,128)(2,1)S(1)} %collective-permute-done.10.refs_9_), channel_id=1, source_target_pairs={{0,8},{8,16},{16,24},{24,32},{32,40},{40,48},{48,56},{56,0},{1,9},... | collective-permute-start | bytes 491528 | tf_op jit(solution)/shard_map/ppermute | solution.py:30
  58.2 1.4 %collective-permute-done.12.refs_11_ = bf16[160,512]{1,0:T(8,128)(2,1)S(1)} collective-permute-done((bf16[160,512]{1,0:T(8,128)(2,1)S(1)}, bf16[160,512]{1,0:T(8,128)(2,1)S(1)}, u32[]{:S(2)}, u32[]{:S(2)}) %collective-permute-start.12) | collective-permute-done | bytes 163872 | tf_op jit(solution)/shard_map/ppermute | solution.py:30
  59.6 1.2 %collective-permute-start.16 = (bf16[160,512]{1,0:T(8,128)(2,1)S(1)}, bf16[160,512]{1,0:T(8,128)(2,1)S(1)}, u32[]{:S(2)}, u32[]{:S(2)}) collective-permute-start(bf16[160,512]{1,0:T(8,128)(2,1)S(1)} %collective-permute-done.12.refs_11_), channel_id=1, source_target_pairs={{0,56},{8,0},{16,8},{24,16},{32,24},{40,32},{48,40},{56,48},{1,57}... | collective-permute-start | bytes 491528 | tf_op jit(solution)/shard_map/ppermute | solution.py:30
  60.9 1.7 %collective-permute-done.13.refs_12_ = bf16[160,512]{1,0:T(8,128)(2,1)S(1)} collective-permute-done((bf16[160,512]{1,0:T(8,128)(2,1)S(1)}, bf16[160,512]{1,0:T(8,128)(2,1)S(1)}, u32[]{:S(2)}, u32[]{:S(2)}) %collective-permute-start.13) | collective-permute-done | bytes 163872 | tf_op jit(solution)/shard_map/ppermute | solution.py:30
  62.7 1.4 %collective-permute-done.15.refs_14_ = bf16[160,512]{1,0:T(8,128)(2,1)S(1)} collective-permute-done((bf16[160,512]{1,0:T(8,128)(2,1)S(1)}, bf16[160,512]{1,0:T(8,128)(2,1)S(1)}, u32[]{:S(2)}, u32[]{:S(2)}) %collective-permute-start.15) | collective-permute-done | bytes 163872 | tf_op jit(solution)/shard_map/ppermute | solution.py:30
  65.6 1.5 %copy-done.1 = bf16[384,2560]{1,0:T(8,128)(2,1)S(1)} copy-done((bf16[384,2560]{1,0:T(8,128)(2,1)S(1)}, bf16[384,2560]{1,0:T(8,128)(2,1)}, u32[]{:S(2)}) %copy-start.1) | copy-done | bytes 1966104
  69.0 2.5 %shard_map.85 = (bf16[1120,128]{1,0:T(8,128)(2,1)S(1)}, bf16[384,192]{1,0:T(8,128)(2,1)S(1)}) custom-call(s32[20]{0:T(128)S(1)} %stack.80.place_ref, f32[1,512]{1,0:T(1,128)S(1)} %get-tuple-element.22.gain_ref, f32[1,512]{1,0:T(1,128)S(1)} %get-tuple-element.21.plain_ref, bf16[384,2560]{1,0:T(8,128)(2,1)S(1)} %copy-done.1, ...), custom_call_target="tpu_custom_call" | custom-call | flops 1006632960 | bytes 4632656 | tf_op jit(solution)/shard_map/pallas_call | solution.py:264
  71.9 8.2 %collective-permute-done.19.far = bf16[1120,128]{1,0:T(8,128)(2,1)S(1)} collective-permute-done((bf16[1120,128]{1,0:T(8,128)(2,1)S(1)}, bf16[1120,128]{1,0:T(8,128)(2,1)S(1)}, u32[]{:S(2)}, u32[]{:S(2)}) %collective-permute-start.19) | collective-permute-done | bytes 286752 | tf_op jit(solution)/shard_map/ppermute | solution.py:30
  80.6 1.4 %collective-permute-done.18.beside_q = bf16[384,192]{1,0:T(8,128)(2,1)S(1)} collective-permute-done((bf16[384,192]{1,0:T(8,128)(2,1)S(1)}, bf16[384,192]{1,0:T(8,128)(2,1)S(1)}, u32[]{:S(2)}, u32[]{:S(2)}) %collective-permute-start.18) | collective-permute-done | bytes 147488 | tf_op jit(solution)/shard_map/ppermute | solution.py:30
  82.0 3.0 %shard_map.86.a0 = bf16[480,128]{1,0:T(8,128)(2,1)S(1)} custom-call(s32[20]{0:T(128)S(1)} %stack.80.place_ref, bf16[1120,128]{1,0:T(8,128)(2,1)S(1)} %get-tuple-element.15.own, bf16[1120,128]{1,0:T(8,128)(2,1)S(1)} %collective-permute-done.17.beside, bf16[384,192]{1,0:T(8,128)(2,1)S(1)} %get-tuple-element.16.own_q, ...), custom_call_target="tpu_custom_call" | custom-call | flops 220200960 | bytes 1441872 | tf_op jit(solution)/shard_map/pallas_call | solution.py:264
  85.2 2.9 %collective-permute-start.22 = (bf16[480,128]{1,0:T(8,128)(2,1)S(1)}, bf16[480,128]{1,0:T(8,128)(2,1)S(1)}, u32[]{:S(2)}, u32[]{:S(2)}) collective-permute-start(bf16[480,128]{1,0:T(8,128)(2,1)S(1)} %shard_map.86.a0), channel_id=1, source_target_pairs={{0,4},{2,6},{4,0},{6,2},{1,5},{3,7},{5,1},{7,3},{8,12},{10,14},{12... | collective-permute-start | bytes 368648 | tf_op jit(solution)/shard_map/ppermute | solution.py:30
  89.2 3.7 %all-gather.5.cloned.1.call-done.gathered_ref = bf16[640,1216]{1,0:T(8,128)(2,1)} async-done(((bf16[40,1216]{1,0:T(8,128)(2,1)}), bf16[640,1216]{1,0:T(8,128)(2,1)}) %all-gather.5.cloned.1.call-update) | async-done | bytes 1556496 | tf_op jit(solution)/shard_map/all_gather | solution.py:362
  92.8 1.5 %collective-permute-done.21.a1 = bf16[480,128]{1,0:T(8,128)(2,1)S(1)} collective-permute-done((bf16[480,128]{1,0:T(8,128)(2,1)S(1)}, bf16[480,128]{1,0:T(8,128)(2,1)S(1)}, u32[]{:S(2)}, u32[]{:S(2)}) %collective-permute-start.21) | collective-permute-done | bytes 122912 | tf_op jit(solution)/shard_map/ppermute | solution.py:30
  94.9 1.4 %copy-done.2 = bf16[640,1216]{1,0:T(8,128)(2,1)S(1)} copy-done((bf16[640,1216]{1,0:T(8,128)(2,1)S(1)}, bf16[640,1216]{1,0:T(8,128)(2,1)}, u32[]{:S(2)}) %copy-start.2) | copy-done | bytes 1556504
  96.4 1.7 %shard_map.88 = (bf16[48,608]{1,0:T(8,128)(2,1)S(1)}, bf16[48,608]{1,0:T(8,128)(2,1)S(1)}, bf16[48,608]{1,0:T(8,128)(2,1)S(1)}, bf16[48,608]{1,0:T(8,128)(2,1)S(1)}) custom-call(s32[20]{0:T(128)S(1)} %stack.80.place_ref, bf16[480,128]{1,0:T(8,128)(2,1)S(1)} %shard_map.86.a0, bf16[480,128]{1,0:T(8,128)(2,1)S(1)} %collective-permute-done.21.a1, ...), custom_call_target="tpu_custom_call" | custom-call | flops 283901952 | bytes 2048080 | tf_op jit(solution)/shard_map/pallas_call | solution.py:264
  98.9 3.4 %collective-permute-start.25 = (bf16[48,608]{1,0:T(8,128)(2,1)S(1)}, bf16[48,608]{1,0:T(8,128)(2,1)S(1)}, u32[]{:S(2)}, u32[]{:S(2)}) collective-permute-start(bf16[48,608]{1,0:T(8,128)(2,1)S(1)} %get-tuple-element.19), channel_id=1, source_target_pairs={{0,4},{2,6},{4,0},{6,2},{1,5},{3,7},{5,1},{7,3},{8,12},{10,14},{12... | collective-permute-start | bytes 175112 | tf_op jit(solution)/shard_map/ppermute | solution.py:30
  102.3 1.3 %collective-permute-done.24.n1 = bf16[48,608]{1,0:T(8,128)(2,1)S(1)} collective-permute-done((bf16[48,608]{1,0:T(8,128)(2,1)S(1)}, bf16[48,608]{1,0:T(8,128)(2,1)S(1)}, u32[]{:S(2)}, u32[]{:S(2)}) %collective-permute-start.24) | collective-permute-done | bytes 58400 | tf_op jit(solution)/shard_map/ppermute | solution.py:30
  103.6 1.9 %collective-permute-done.25.n2 = bf16[48,608]{1,0:T(8,128)(2,1)S(1)} collective-permute-done((bf16[48,608]{1,0:T(8,128)(2,1)S(1)}, bf16[48,608]{1,0:T(8,128)(2,1)S(1)}, u32[]{:S(2)}, u32[]{:S(2)}) %collective-permute-start.25) | collective-permute-done | bytes 58400 | tf_op jit(solution)/shard_map/ppermute | solution.py:30
  106.5 1.9 %shard_map.89 = bf16[48,2432]{1,0:T(8,128)(2,1)} custom-call(s32[20]{0:T(128)S(1)} %stack.80.place_ref, f32[1,2432]{1,0:T(1,128)S(1)} %dynamic-slice_bitcast_fusion.gate_ref, bf16[48,2432]{1,0:T(8,128)(2,1)S(1)} %collective-permute-done.raw_ref, bf16[48,608]{1,0:T(8,128)(2,1)S(1)} %get-tuple-element.17.n0, bf16[48,608]{1,0:T(8,128)(2,1)S(1)} %collective-permute-done.24.n1, ...), custom_call_target="tpu_custom_call" | custom-call | bytes 476752 | tf_op jit(solution)/shard_map/pallas_call | solution.py:264
  (76 shorter events, 19.6 us)
Async XLA Ops:
  6.5 13.8 %collective-permute-start = (bf16[48,2432]{1,0:T(8,128)(2,1)}, bf16[48,2432]{1,0:T(8,128)(2,1)S(1)}, u32[]{:S(2)}, u32[]{:S(2)}) collective-permute-start(bf16[48,2432]{1,0:T(8,128)(2,1)} %bitcast.44), channel_id=1, source_target_pairs={{0,128},{128,0},{1,129},{129,1},{2,130},{130,2},{3,131},{131,3},{4... | collective-permute-start | bytes 700424 | tf_op jit(solution)/shard_map/ppermute | solution.py:30
  8.7 11.7 %collective-permute-start.1 = (bf16[19,1216]{1,0:T(8,128)(2,1)}, bf16[19,1216]{1,0:T(8,128)(2,1)S(1)}, u32[]{:S(2)}, u32[]{:S(2)}) collective-permute-start(bf16[19,1216]{1,0:T(8,128)(2,1)} %bitcast.37), channel_id=1, source_target_pairs={{0,64},{64,0},{1,65},{65,1},{2,66},{66,2},{3,67},{67,3},{4,68},{68... | collective-permute-start | bytes 138632 | tf_op jit(solution)/shard_map/ppermute | solution.py:30
  12.6 11.3 %all-to-all-start = ((bf16[8,24,512]{2,1,0:T(8,128)(2,1)}), bf16[8,24,512]{2,1,0:T(8,128)(2,1)S(1)}, u32[]{:S(2)}, u32[]{:S(2)}) async-start(bf16[8,24,512]{2,1,0:T(8,128)(2,1)} %shard_map.83), calls=%async_computation | async-start | bytes 393216 | tf_op jit(solution)/shard_map/all_to_all | solution.py:295
  17.1 48.5 %all-gather.3.cloned.1.call-start = ((), (), s32[]{:S(2)}) async-start(), calls=%async_computation.1 | async-start | bytes 2211840 | tf_op jit(solution)/shard_map/all_gather | solution.py:321
  21.6 25.9 %copy-start.10 = (f32[1,2,1216]{2,1,0:T(2,128)S(1)}, f32[1,2,1216]{2,1,0:T(2,128)}, u32[]{:S(2)}) copy-start(f32[1,2,1216]{2,1,0:T(2,128)} %param.15) | copy-start | bytes 29188
  21.6 32.5 %copy-start.11 = (s32[8]{0:T(128)S(1)}, s32[8]{0:T(128)}, u32[]{:S(2)}) copy-start(s32[8]{0:T(128)} %param.11) | copy-start | bytes 100
  21.6 71.2 %all-gather.5.cloned.1.call-start = ((), (), s32[]{:S(2)}) async-start(), calls=%async_computation.2 | async-start | bytes 1740800 | tf_op jit(solution)/shard_map/all_gather | solution.py:362
  25.0 6.5 %collective-permute-start.2 = (bf16[160,512]{1,0:T(8,128)(2,1)S(1)}, bf16[160,512]{1,0:T(8,128)(2,1)S(1)}, u32[]{:S(2)}, u32[]{:S(2)}) collective-permute-start(bf16[160,512]{1,0:T(8,128)(2,1)S(1)} %get-tuple-element.14.refs_0_), channel_id=1, source_target_pairs={{0,64},{64,0},{1,65},{65,1},{2,66},{66,2},{3,67},{67,3},{4,68},{68... | collective-permute-start | bytes 491528 | tf_op jit(solution)/shard_map/ppermute | solution.py:30
  25.7 10.9 %collective-permute-start.3 = (bf16[160,512]{1,0:T(8,128)(2,1)S(1)}, bf16[160,512]{1,0:T(8,128)(2,1)S(1)}, u32[]{:S(2)}, u32[]{:S(2)}) collective-permute-start(bf16[160,512]{1,0:T(8,128)(2,1)S(1)} %get-tuple-element.14.refs_0_), channel_id=1, source_target_pairs={{0,8},{8,16},{16,24},{24,32},{32,40},{40,48},{48,56},{56,0},{1,9},... | collective-permute-start | bytes 491528 | tf_op jit(solution)/shard_map/ppermute | solution.py:30
  27.6 9.0 %collective-permute-start.5 = (bf16[160,512]{1,0:T(8,128)(2,1)S(1)}, bf16[160,512]{1,0:T(8,128)(2,1)S(1)}, u32[]{:S(2)}, u32[]{:S(2)}) collective-permute-start(bf16[160,512]{1,0:T(8,128)(2,1)S(1)} %get-tuple-element.14.refs_0_), channel_id=1, source_target_pairs={{0,56},{8,0},{16,8},{24,16},{32,24},{40,32},{48,40},{56,48},{1,57}... | collective-permute-start | bytes 491528 | tf_op jit(solution)/shard_map/ppermute | solution.py:30
  31.5 9.3 %collective-permute-start.4 = (bf16[160,512]{1,0:T(8,128)(2,1)S(1)}, bf16[160,512]{1,0:T(8,128)(2,1)S(1)}, u32[]{:S(2)}, u32[]{:S(2)}) collective-permute-start(bf16[160,512]{1,0:T(8,128)(2,1)S(1)} %collective-permute-done.2.refs_1_), channel_id=1, source_target_pairs={{0,56},{8,0},{16,8},{24,16},{32,24},{40,32},{48,40},{56,48},{1,57}... | collective-permute-start | bytes 491528 | tf_op jit(solution)/shard_map/ppermute | solution.py:30
  36.6 7.4 %collective-permute-start.6 = (bf16[160,512]{1,0:T(8,128)(2,1)S(1)}, bf16[160,512]{1,0:T(8,128)(2,1)S(1)}, u32[]{:S(2)}, u32[]{:S(2)}) collective-permute-start(bf16[160,512]{1,0:T(8,128)(2,1)S(1)} %collective-permute-done.2.refs_1_), channel_id=1, source_target_pairs={{0,8},{8,16},{16,24},{24,32},{32,40},{40,48},{48,56},{56,0},{1,9},... | collective-permute-start | bytes 491528 | tf_op jit(solution)/shard_map/ppermute | solution.py:30
  36.6 9.2 %collective-permute-start.7 = (bf16[160,512]{1,0:T(8,128)(2,1)S(1)}, bf16[160,512]{1,0:T(8,128)(2,1)S(1)}, u32[]{:S(2)}, u32[]{:S(2)}) collective-permute-start(bf16[160,512]{1,0:T(8,128)(2,1)S(1)} %collective-permute-done.3.refs_2_), channel_id=1, source_target_pairs={{0,8},{8,16},{16,24},{24,32},{32,40},{40,48},{48,56},{56,0},{1,9},... | collective-permute-start | bytes 491528 | tf_op jit(solution)/shard_map/ppermute | solution.py:30
  36.6 9.2 %collective-permute-start.9 = (bf16[160,512]{1,0:T(8,128)(2,1)S(1)}, bf16[160,512]{1,0:T(8,128)(2,1)S(1)}, u32[]{:S(2)}, u32[]{:S(2)}) collective-permute-start(bf16[160,512]{1,0:T(8,128)(2,1)S(1)} %collective-permute-done.5.refs_4_), channel_id=1, source_target_pairs={{0,56},{8,0},{16,8},{24,16},{32,24},{40,32},{48,40},{56,48},{1,57}... | collective-permute-start | bytes 491528 | tf_op jit(solution)/shard_map/ppermute | solution.py:30
  46.5 6.1 %collective-permute-start.8 = (bf16[160,512]{1,0:T(8,128)(2,1)S(1)}, bf16[160,512]{1,0:T(8,128)(2,1)S(1)}, u32[]{:S(2)}, u32[]{:S(2)}) collective-permute-start(bf16[160,512]{1,0:T(8,128)(2,1)S(1)} %collective-permute-done.4.refs_3_), channel_id=1, source_target_pairs={{0,56},{8,0},{16,8},{24,16},{32,24},{40,32},{48,40},{56,48},{1,57}... | collective-permute-start | bytes 491528 | tf_op jit(solution)/shard_map/ppermute | solution.py:30
  47.5 8.0 %collective-permute-start.10 = (bf16[160,512]{1,0:T(8,128)(2,1)S(1)}, bf16[160,512]{1,0:T(8,128)(2,1)S(1)}, u32[]{:S(2)}, u32[]{:S(2)}) collective-permute-start(bf16[160,512]{1,0:T(8,128)(2,1)S(1)} %collective-permute-done.6.refs_5_.refs_2_), channel_id=1, source_target_pairs={{0,8},{8,16},{16,24},{24,32},{32,40},{40,48},{48,56},{56,0},{1,9},... | collective-permute-start | bytes 491528 | tf_op jit(solution)/shard_map/ppermute | solution.py:30
  48.7 8.8 %collective-permute-start.11 = (bf16[160,512]{1,0:T(8,128)(2,1)S(1)}, bf16[160,512]{1,0:T(8,128)(2,1)S(1)}, u32[]{:S(2)}, u32[]{:S(2)}) collective-permute-start(bf16[160,512]{1,0:T(8,128)(2,1)S(1)} %collective-permute-done.7.refs_6_.refs_0_), channel_id=1, source_target_pairs={{0,8},{8,16},{16,24},{24,32},{32,40},{40,48},{48,56},{56,0},{1,9},... | collective-permute-start | bytes 491528 | tf_op jit(solution)/shard_map/ppermute | solution.py:30
  52.6 7.0 %collective-permute-start.12 = (bf16[160,512]{1,0:T(8,128)(2,1)S(1)}, bf16[160,512]{1,0:T(8,128)(2,1)S(1)}, u32[]{:S(2)}, u32[]{:S(2)}) collective-permute-start(bf16[160,512]{1,0:T(8,128)(2,1)S(1)} %collective-permute-done.8.refs_7_), channel_id=1, source_target_pairs={{0,56},{8,0},{16,8},{24,16},{32,24},{40,32},{48,40},{56,48},{1,57}... | collective-permute-start | bytes 491528 | tf_op jit(solution)/shard_map/ppermute | solution.py:30
  55.5 7.2 %collective-permute-start.13 = (bf16[160,512]{1,0:T(8,128)(2,1)S(1)}, bf16[160,512]{1,0:T(8,128)(2,1)S(1)}, u32[]{:S(2)}, u32[]{:S(2)}) collective-permute-start(bf16[160,512]{1,0:T(8,128)(2,1)S(1)} %collective-permute-done.9.refs_8_.refs_1_), channel_id=1, source_target_pairs={{0,56},{8,0},{16,8},{24,16},{32,24},{40,32},{48,40},{56,48},{1,57}... | collective-permute-start | bytes 491528 | tf_op jit(solution)/shard_map/ppermute | solution.py:30
  55.5 7.2 %collective-permute-start.14 = (bf16[160,512]{1,0:T(8,128)(2,1)S(1)}, bf16[160,512]{1,0:T(8,128)(2,1)S(1)}, u32[]{:S(2)}, u32[]{:S(2)}) collective-permute-start(bf16[160,512]{1,0:T(8,128)(2,1)S(1)} %collective-permute-done.10.refs_9_), channel_id=1, source_target_pairs={{0,8},{8,16},{16,24},{24,32},{32,40},{40,48},{48,56},{56,0},{1,9},... | collective-permute-start | bytes 491528 | tf_op jit(solution)/shard_map/ppermute | solution.py:30
  57.5 6.5 %collective-permute-start.15 = (bf16[160,512]{1,0:T(8,128)(2,1)S(1)}, bf16[160,512]{1,0:T(8,128)(2,1)S(1)}, u32[]{:S(2)}, u32[]{:S(2)}) collective-permute-start(bf16[160,512]{1,0:T(8,128)(2,1)S(1)} %collective-permute-done.11.refs_10_), channel_id=1, source_target_pairs={{0,8},{8,16},{16,24},{24,32},{32,40},{40,48},{48,56},{56,0},{1,9},... | collective-permute-start | bytes 491528 | tf_op jit(solution)/shard_map/ppermute | solution.py:30
  59.6 5.3 %collective-permute-start.16 = (bf16[160,512]{1,0:T(8,128)(2,1)S(1)}, bf16[160,512]{1,0:T(8,128)(2,1)S(1)}, u32[]{:S(2)}, u32[]{:S(2)}) collective-permute-start(bf16[160,512]{1,0:T(8,128)(2,1)S(1)} %collective-permute-done.12.refs_11_), channel_id=1, source_target_pairs={{0,56},{8,0},{16,8},{24,16},{32,24},{40,32},{48,40},{56,48},{1,57}... | collective-permute-start | bytes 491528 | tf_op jit(solution)/shard_map/ppermute | solution.py:30
  71.5 8.6 %collective-permute-start.19 = (bf16[1120,128]{1,0:T(8,128)(2,1)S(1)}, bf16[1120,128]{1,0:T(8,128)(2,1)S(1)}, u32[]{:S(2)}, u32[]{:S(2)}) collective-permute-start(bf16[1120,128]{1,0:T(8,128)(2,1)S(1)} %get-tuple-element.15.own), channel_id=1, source_target_pairs={{0,8},{8,0},{1,9},{9,1},{2,10},{10,2},{3,11},{11,3},{4,12},{12,4},... | collective-permute-start | bytes 860168 | tf_op jit(solution)/shard_map/ppermute | solution.py:30
  71.9 10.1 %collective-permute-start.17 = (bf16[1120,128]{1,0:T(8,128)(2,1)S(1)}, bf16[1120,128]{1,0:T(8,128)(2,1)S(1)}, u32[]{:S(2)}, u32[]{:S(2)}) collective-permute-start(bf16[1120,128]{1,0:T(8,128)(2,1)S(1)} %get-tuple-element.15.own), channel_id=1, source_target_pairs={{0,1},{1,0},{2,3},{3,2},{4,5},{5,4},{6,7},{7,6},{8,9},{9,8},{10,11... | collective-permute-start | bytes 860168 | tf_op jit(solution)/shard_map/ppermute | solution.py:30
  80.1 1.9 %collective-permute-start.20 = (bf16[1120,128]{1,0:T(8,128)(2,1)S(1)}, bf16[1120,128]{1,0:T(8,128)(2,1)S(1)}, u32[]{:S(2)}, u32[]{:S(2)}) collective-permute-start(bf16[1120,128]{1,0:T(8,128)(2,1)S(1)} %collective-permute-done.19.far), channel_id=1, source_target_pairs={{0,1},{1,0},{2,3},{3,2},{4,5},{5,4},{6,7},{7,6},{8,9},{9,8},{10,11... | collective-permute-start | bytes 860168 | tf_op jit(solution)/shard_map/ppermute | solution.py:30
  80.1 1.9 %collective-permute-start.18 = (bf16[384,192]{1,0:T(8,128)(2,1)S(1)}, bf16[384,192]{1,0:T(8,128)(2,1)S(1)}, u32[]{:S(2)}, u32[]{:S(2)}) collective-permute-start(bf16[384,192]{1,0:T(8,128)(2,1)S(1)} %get-tuple-element.16.own_q), channel_id=1, source_target_pairs={{0,1},{1,0},{2,3},{3,2},{4,5},{5,4},{6,7},{7,6},{8,9},{9,8},{10,11... | collective-permute-start | bytes 442376 | tf_op jit(solution)/shard_map/ppermute | solution.py:30
  85.1 9.3 %collective-permute-start.21 = (bf16[480,128]{1,0:T(8,128)(2,1)S(1)}, bf16[480,128]{1,0:T(8,128)(2,1)S(1)}, u32[]{:S(2)}, u32[]{:S(2)}) collective-permute-start(bf16[480,128]{1,0:T(8,128)(2,1)S(1)} %shard_map.86.a0), channel_id=1, source_target_pairs={{0,2},{2,4},{4,6},{6,0},{1,3},{3,5},{5,7},{7,1},{8,10},{10,12},{12... | collective-permute-start | bytes 368648 | tf_op jit(solution)/shard_map/ppermute | solution.py:30
  85.2 9.2 %collective-permute-start.22 = (bf16[480,128]{1,0:T(8,128)(2,1)S(1)}, bf16[480,128]{1,0:T(8,128)(2,1)S(1)}, u32[]{:S(2)}, u32[]{:S(2)}) collective-permute-start(bf16[480,128]{1,0:T(8,128)(2,1)S(1)} %shard_map.86.a0), channel_id=1, source_target_pairs={{0,4},{2,6},{4,0},{6,2},{1,5},{3,7},{5,1},{7,3},{8,12},{10,14},{12... | collective-permute-start | bytes 368648 | tf_op jit(solution)/shard_map/ppermute | solution.py:30
  88.1 6.9 %collective-permute-start.23 = (bf16[480,128]{1,0:T(8,128)(2,1)S(1)}, bf16[480,128]{1,0:T(8,128)(2,1)S(1)}, u32[]{:S(2)}, u32[]{:S(2)}) collective-permute-start(bf16[480,128]{1,0:T(8,128)(2,1)S(1)} %shard_map.86.a0), channel_id=1, source_target_pairs={{0,6},{2,0},{4,2},{6,4},{1,7},{3,1},{5,3},{7,5},{8,14},{10,8},{12,... | collective-permute-start | bytes 368648 | tf_op jit(solution)/shard_map/ppermute | solution.py:30
  98.1 5.5 %collective-permute-start.24 = (bf16[48,608]{1,0:T(8,128)(2,1)S(1)}, bf16[48,608]{1,0:T(8,128)(2,1)S(1)}, u32[]{:S(2)}, u32[]{:S(2)}) collective-permute-start(bf16[48,608]{1,0:T(8,128)(2,1)S(1)} %get-tuple-element.18), channel_id=1, source_target_pairs={{0,2},{2,4},{4,6},{6,0},{1,3},{3,5},{5,7},{7,1},{8,10},{10,12},{12... | collective-permute-start | bytes 175112 | tf_op jit(solution)/shard_map/ppermute | solution.py:30
  98.9 6.6 %collective-permute-start.25 = (bf16[48,608]{1,0:T(8,128)(2,1)S(1)}, bf16[48,608]{1,0:T(8,128)(2,1)S(1)}, u32[]{:S(2)}, u32[]{:S(2)}) collective-permute-start(bf16[48,608]{1,0:T(8,128)(2,1)S(1)} %get-tuple-element.19), channel_id=1, source_target_pairs={{0,4},{2,6},{4,0},{6,2},{1,5},{3,7},{5,1},{7,3},{8,12},{10,14},{12... | collective-permute-start | bytes 175112 | tf_op jit(solution)/shard_map/ppermute | solution.py:30
  102.3 4.2 %collective-permute-start.26 = (bf16[48,608]{1,0:T(8,128)(2,1)S(1)}, bf16[48,608]{1,0:T(8,128)(2,1)S(1)}, u32[]{:S(2)}, u32[]{:S(2)}) collective-permute-start(bf16[48,608]{1,0:T(8,128)(2,1)S(1)} %get-tuple-element.20), channel_id=1, source_target_pairs={{0,6},{2,0},{4,2},{6,4},{1,7},{3,1},{5,3},{7,5},{8,14},{10,8},{12,... | collective-permute-start | bytes 175112 | tf_op jit(solution)/shard_map/ppermute | solution.py:30
  (10 other events, 45.9 us)
Sparse Core Ops, SparseCore 0:
  21.7 29.7 all-gather.2
  53.3 39.4 all-gather.4

commit v3 on v2

--- a/solution.py
+++ b/solution.py
@@ -30,9 +30,19 @@
     return lax.ppermute(array, axis, [(i, (i + by) % devices) for i in range(devices)])
 
 
-def beside_kernel(place_ref, mine_ref, other_ref, *refs):
+def hold_kernel(array_ref, after_ref, out_ref):
+    out_ref[...] = array_ref[...]
+
+
+def hold(array, after):
+    return in_vmem(
+        hold_kernel, jax.ShapeDtypeStruct(array.shape, array.dtype), (array,), after=(after,)
+    )
+
+
+def beside_kernel(mine_ref, other_ref, *refs):
     out_ref, room = refs[-2:]
-    x = place_ref[0]
+    x = lax.axis_index("x")
     used = mine_ref.shape[0]
     room[...] = jnp.zeros_like(room)
     mine, other = mine_ref[...].astype(F32), other_ref[...].astype(F32)
@@ -73,7 +83,6 @@
 def compact_kernel(received_ref, *refs):
     block_ref, text_ref, rows_room, text_room = refs[-4:]
     split = HALF - YW
-    rows_room[...] = jnp.zeros_like(rows_room)
     for source in range(8):
         value = received_ref[source].astype(F32)
         rows_room[source * 19 : (source + 1) * 19, :] = value[:19]
@@ -88,22 +97,55 @@
     text_ref[...] = text_room[...].astype(BF16)
 
 
-def modulate_kernel(modulation_ref, raw_ref, *refs):
-    h_ref = refs[-1]
+def modulate_kernel(steps_ref, raw_ref, table_ref, *refs):
+    h_ref, gate_ref, modulation, arrived = refs[-4:]
+    step = steps_ref[lax.axis_index("x") * 4 + lax.axis_index("z1")]
+    copy = pltpu.make_async_copy(table_ref.at[step], modulation, arrived)
+    copy.start()
     wide = raw_ref[...].astype(F32)
     centred = wide - jnp.mean(wide, axis=-1, keepdims=True)
     normed = centred * lax.rsqrt(jnp.mean(centred * centred, axis=-1, keepdims=True) + EPSILON)
-    modulated = normed * (1.0 + modulation_ref[1:2, :]) + modulation_ref[0:1, :]
+    copy.wait()
+    gate_ref[...] = modulation[2]
+    modulated = normed * (1.0 + modulation[1]) + modulation[0]
     modulated = modulated.astype(BF16)
     h_ref[...] = jnp.zeros_like(h_ref)
     for slot in range(16):
         h_ref[:, slot * SLOT : slot * SLOT + CHUNK] = modulated[:, slot * CHUNK : (slot + 1) * CHUNK]
 
 
-def project_kernel(place_ref, gain_ref, plain_ref, h_ref, text_ref, *refs):
-    blocks, (pairs_ref, queries_ref, whole) = refs[:16], refs[16:]
-    for index, block in enumerate(blocks):
-        whole[place_ref[4 + index]] = block[...]
+def places_of_blocks():
+    x = lax.axis_index("x")
+    z = lax.axis_index("z1") * 2 + lax.axis_index("z0")
+    slots = [x * 8 + z, (1 - x) * 8 + z]
+    for step in range(1, 5):
+        slots += [x * 8 + lax.rem(z + 8 - step, 8), (1 - x) * 8 + lax.rem(z + step, 8)]
+        if step < 4:
+            slots += [x * 8 + lax.rem(z + step, 8), (1 - x) * 8 + lax.rem(z + 8 - step, 8)]
+    return slots
+
+
+def project_kernel(gains_ref, h_ref, text_ref, *refs):
+    blocks, (pairs_ref, queries_ref, whole, gain_ref) = refs[:16], refs[16:]
+    y, core = lax.axis_index("y"), lax.axis_index("core")
+    split = HALF - YW
+    gain_ref[...] = jnp.ones_like(gain_ref)
+    for at in range(4):
+        first = at * YW
+        size = min(YW, HEADS * HD - first)
+
+        @pl.when((y == at) & (core == 0))
+        def _():
+            gain_ref[:, :size] = gains_ref[1:2, first : first + size]
+            gain_ref[:, YW:] = gains_ref[0:1, first : first + split]
+
+        @pl.when((y == at) & (core == 1))
+        def _():
+            gain_ref[:, YW : YW + size - split] = gains_ref[0:1, first + split : first + size]
+
+    whole[:, CHUNK:, :] = jnp.zeros((16, SLOT - CHUNK, HALF), BF16)
+    for slot, block in zip(places_of_blocks(), blocks):
+        whole[slot, :CHUNK, :] = block[...]
     rows = h_ref.shape[0]
     shard = pairs_ref.shape[0] * 2 // YH
     half = shard // 2
@@ -123,7 +165,9 @@
             high_sum = jnp.sum(jnp.where(low, 0.0, square), axis=-1, keepdims=True)
             mean = jnp.where(low, low_sum, high_sum) * (1.0 / HD)
             scaled = value * lax.rsqrt(mean + EPSILON) * gain_ref[:, columns]
-            result = jnp.where(plain_ref[:, columns] > 0.0, value, scaled).astype(BF16)
+            column = lax.broadcasted_iota(jnp.int32, (1, 128), 1) + begin
+            plain = (core == 1) & (column < YW)
+            result = jnp.where(plain, value, scaled).astype(BF16)
             if begin + 128 <= YW:
                 pairs_ref[begin // 128 * shard : begin // 128 * shard + rows, :] = result
             elif begin < YW:
@@ -144,8 +188,9 @@
     room[2, begin + half : begin + shard, :HD] = packed[2 * shard :, HD:]
 
 
-def attend_kernel(place_ref, own, beside, own_q, beside_q, far, far_beside, out_ref, keys, values):
-    core, z0, text_valid = place_ref[1], place_ref[2], place_ref[3]
+def attend_kernel(counts_ref, own, beside, own_q, beside_q, far, far_beside, out_ref, keys, values):
+    core, z0 = lax.axis_index("core"), lax.axis_index("z0")
+    text_valid = counts_ref[lax.axis_index("x") * 4 + lax.axis_index("z1")]
     shard = own.shape[0] * 2 // YH
     rows = out_ref.shape[0] * 2 // YH
     image = shard - 8 * TEXT_ROWS
@@ -206,18 +251,20 @@
             out_ref[at : at + half, HD:] = attended[half:]
 
 
-def finish_kernel(place_ref, a0, a1, a2, a3, gathered_ref, *refs):
-    o0, o1, o2, o3, heads, result, weights = refs
-    y = place_ref[0]
+def arrange_kernel(gathered_ref, out_ref, weights):
     each = weights.shape[0] // 32
     gap = gathered_ref.shape[0] // 16
     for place in range(16):
         value = gathered_ref[place * gap : (place + 1) * gap, :].astype(F32)
-        z, core = divmod(place, 2)
+        core, z = divmod(place, 8)
         for x in range(2):
             at = ((x * 8 + z) * 2 + core) * each
             weights[at : at + each, :] = value[x * each : (x + 1) * each]
-    weight = weights[...].astype(BF16)
+    out_ref[...] = weights[...].astype(BF16)
+
+
+def finish_kernel(a0, a1, a2, a3, weight_ref, o0, o1, o2, o3, heads, result):
+    y = lax.axis_index("y")
     rows = a0.shape[0] * 2 // YH
     half = rows // 2
     for by, attended in enumerate((a0, a1, a2, a3)):
@@ -231,7 +278,7 @@
         size = min(YW, HEADS * HD - q * YW)
         part = lax.dot_general(
             heads[q][:, :size],
-            weight[:, q * YW : q * YW + size],
+            weight_ref[:, q * YW : q * YW + size],
             (((1,), (1,)), ((), ())),
             preferred_element_type=F32,
         )
@@ -242,8 +289,8 @@
         out_ref[...] = result[lax.rem(y + by, 4)]
 
 
-def assemble_kernel(place_ref, gate_ref, raw_ref, n0, n1, n2, n3, out_ref, branch):
-    y = place_ref[0]
+def assemble_kernel(gate_ref, raw_ref, n0, n1, n2, n3, out_ref, branch):
+    y = lax.axis_index("y")
     run = n0.shape[1] // 16
     for by, part in enumerate((n0, n1, n2, n3)):
         value = part[...].astype(F32)
@@ -258,7 +305,7 @@
     out_ref[...] = (raw_ref[...].astype(F32) + gate_ref[...] * branch[...]).astype(BF16)
 
 
-def in_vmem(kernel, out_shape, args, flops=0, scratch=(), scalars=0, after=()):
+def in_vmem(kernel, out_shape, args, flops=0, scratch=(), scalars=0, after=(), anywhere=(), limit=8):
     size = sum(a.size * a.dtype.itemsize for a in args)
     vmem = pl.BlockSpec(memory_space=pltpu.VMEM)
     return pl.pallas_call(
@@ -266,12 +313,13 @@
         out_shape=out_shape,
         in_specs=[pl.BlockSpec(memory_space=pltpu.SMEM)] * scalars
         + [vmem] * (len(args) - scalars)
+        + [pl.BlockSpec(memory_space=pl.ANY)] * len(anywhere)
         + [vmem] * len(after),
         out_specs=jax.tree.map(lambda _: vmem, out_shape),
         scratch_shapes=list(scratch),
-        compiler_params=pltpu.CompilerParams(vmem_limit_bytes=10 * 1024 * 1024),
+        compiler_params=pltpu.CompilerParams(vmem_limit_bytes=limit * 1024 * 1024),
         cost_estimate=pl.CostEstimate(flops=flops, bytes_accessed=size, transcendentals=0),
-    )(*args, *after)
+    )(*args, *anywhere, *after)
 
 
 def per_device(
@@ -282,9 +330,6 @@
     weight_rows = qkv_weight.shape[1]
     quarter = width // 4
     split = HALF - YW
-    x, y, core, z0 = (lax.axis_index(name) for name in ("x", "y", "core", "z0"))
-    z = lax.axis_index(Z)
-    sequence = lax.axis_index(("x", "z1"))
 
     halves = in_vmem(
         prepare_kernel,
@@ -294,40 +339,32 @@
     )
     received = lax.all_to_all(halves, ("y", "core"), split_axis=0, concat_axis=0, tiled=True)
     shard = jnp.transpose(out_weight[0])
-    shard_beside = permuted(shard, "x", 1)
 
     raw = permuted(stale_states[0], "comp", 1)
-    step_index = lax.dynamic_index_in_dim(timesteps, sequence, 0, False)
-    modulation = lax.dynamic_index_in_dim(mod_table[0], step_index, 0, False)
-    text_valid = lax.dynamic_index_in_dim(text_count, sequence, 0, False)
-    gate = modulation[2:3]
-    h = in_vmem(
+    h, gate = in_vmem(
         modulate_kernel,
-        jax.ShapeDtypeStruct((rows, 16 * SLOT), BF16),
-        (modulation, raw),
-        after=(shard_beside,),
+        (
+            jax.ShapeDtypeStruct((rows, 16 * SLOT), BF16),
+            jax.ShapeDtypeStruct((1, width), F32),
+        ),
+        (timesteps, raw),
+        scratch=[pltpu.VMEM((3, 1, width), F32), pltpu.SemaphoreType.DMA],
+        scalars=1,
+        anywhere=(mod_table.reshape(mod_table.shape[1:3] + (1, width)),),
+        limit=60,
     )
     block, text = in_vmem(
         compact_kernel,
         (
-            jax.ShapeDtypeStruct((SLOT, HALF), BF16),
+            jax.ShapeDtypeStruct((CHUNK, HALF), BF16),
             jax.ShapeDtypeStruct((8 * TEXT_ROWS, YW), BF16),
         ),
         (received,),
         flops=7 * 10**10,
-        scratch=[pltpu.VMEM((SLOT, HALF), F32), pltpu.VMEM((8 * TEXT_ROWS, YW), F32)],
+        scratch=[pltpu.VMEM((CHUNK, HALF), F32), pltpu.VMEM((8 * TEXT_ROWS, YW), F32)],
         after=(h,),
     )
     h = lax.all_gather(h, ("y", "core"), axis=0, tiled=True)
-
-    gains = jnp.pad(qk_gain[0], ((0, 0), (0, 4 * YW - head_width)))
-    gains = lax.dynamic_slice_in_dim(gains, y * YW, YW, 1)
-    first_gain = jnp.concatenate([gains[1], gains[0, :split]])
-    second_gain = jnp.concatenate(
-        [jnp.ones((YW,), F32), gains[0, split:], jnp.ones((2 * HALF - 3 * YW,), F32)]
-    )
-    gain = jnp.where(core == 0, first_gain, second_gain)[None]
-    plain = jnp.where((core == 1) & (jnp.arange(HALF) < YW), 1.0, 0.0).astype(F32)[None]
 
     ahead = lambda part: permuted(part, Z, 1)
     behind = lambda part: permuted(part, Z, 7)
@@ -340,26 +377,21 @@
         if step < 4:
             own_behinds.append(behind(own_behinds[-1]))
             other_aheads.append(ahead(other_aheads[-1]))
-    blocks = [(block, x, z), (other, 1 - x, z)]
+    blocks = [block, other]
     for step in range(1, 5):
-        blocks.append((own_aheads[step - 1], x, z + 8 - step))
-        blocks.append((other_behinds[step - 1], 1 - x, z + step))
+        blocks += [own_aheads[step - 1], other_behinds[step - 1]]
         if step < 4:
-            blocks.append((own_behinds[step - 1], x, z + step))
-            blocks.append((other_aheads[step - 1], 1 - x, z + 8 - step))
-    slots = [x_place * 8 + z_place % 8 for _, x_place, z_place in blocks]
-    blocks = [part for part, _, _ in blocks]
-
-    place = jnp.stack([y, core, z0, text_valid] + slots).astype(jnp.int32)
+            blocks += [own_behinds[step - 1], other_aheads[step - 1]]
+
+    shard_beside = permuted(hold(shard, block), "x", 1)
     both = in_vmem(
         beside_kernel,
         jax.ShapeDtypeStruct((40, head_width), BF16),
-        (x.astype(jnp.int32)[None], shard, shard_beside),
+        (shard, shard_beside),
         scratch=[pltpu.VMEM((40, head_width), F32)],
-        scalars=1,
         after=(own_aheads[1], own_behinds[1], other_aheads[0], other_behinds[0]),
     )
-    out_columns = lax.all_gather(both, ("z1", "z0", "core"), axis=0, tiled=True)
+    out_columns = lax.all_gather(both, ("core", "z1", "z0"), axis=0, tiled=True)
 
     shard_rows = 8 * (rows + TEXT_ROWS)
     pairs, queries = in_vmem(
@@ -368,10 +400,12 @@
             jax.ShapeDtypeStruct((shard_rows // 2 * YH, 128), BF16),
             jax.ShapeDtypeStruct((8 * rows, split), BF16),
         ),
-        (place, gain, plain, h, text, *blocks),
+        (qk_gain[0], h, text, *blocks),
         flops=2 * 8 * rows * 16 * SLOT * HALF,
-        scratch=[pltpu.VMEM((16, SLOT, HALF), BF16)],
-        scalars=1,
+        scratch=[
+            pltpu.VMEM((16, SLOT, HALF), BF16),
+            pltpu.VMEM((1, HALF), F32),
+        ],
     )
 
     far = permuted(pairs, "z0", 1)
@@ -379,7 +413,7 @@
         attend_kernel,
         jax.ShapeDtypeStruct((2 * rows * YH, 128), BF16),
         (
-            place,
+            text_count,
             pairs,
             permuted(pairs, "core", 1),
             queries,
@@ -392,28 +426,32 @@
         scalars=1,
     )
 
+    out_columns = in_vmem(
+        arrange_kernel,
+        jax.ShapeDtypeStruct((32 * weight_rows, head_width), BF16),
+        (out_columns,),
+        flops=10**10,
+        scratch=[pltpu.VMEM((32 * weight_rows, head_width), F32)],
+    )
     gathered = tuple(permuted(attended, "y", by) for by in (1, 2, 3))
     parts = in_vmem(
         finish_kernel,
         (jax.ShapeDtypeStruct((rows, quarter), BF16),) * 4,
-        (place, attended)
+        (attended,)
         + gathered
         + (out_columns,),
         flops=2 * 4 * rows * head_width * quarter,
         scratch=[
             pltpu.VMEM((4, 4 * rows, YW), BF16),
             pltpu.VMEM((4, rows, quarter), BF16),
-            pltpu.VMEM((32 * weight_rows, head_width), F32),
         ],
-        scalars=1,
     )
     parts = [parts[0]] + [permuted(parts[by], "y", by) for by in (1, 2, 3)]
     new = in_vmem(
         assemble_kernel,
         jax.ShapeDtypeStruct((rows, width), BF16),
-        (place, gate, raw, *parts),
+        (gate, raw, *parts),
         scratch=[pltpu.VMEM((rows, width), F32)],
-        scalars=1,
     )
     return new[None]
 

time: 116 us -> 111 us (0.957)
  local copies, waits for them, and re-layouts: 10.7 us -> 6.33 us
  waiting for transfers between devices: 36.4 us -> 39 us
  between operations: 15.5 us -> 13.6 us
    all_gather x1, waiting for transfers between devices: 3.65 us -> 8.67 us  [per_device(): out_columns = lax.all_gather(both, ('core', 'z1', 'z0'), axis=0, tiled=True)]
    ppermute x27, waiting for transfers between devices: 30.4 us -> 26.9 us  [permuted(): lax.ppermute(array, axis, [(i, (i + by) % devices) for i in range(devices)])]
    dynamic_slice x3 -> x0, local copies, waits for them, and re-layouts: 1.88 us -> none  [the longest x1 1.31 us: per_device(): step_index = lax.dynamic_index_in_dim(timesteps, sequence, 0, False)]
    unnamed x25 -> x22, local copies, waits for them, and re-layouts: 7.87 us -> 6.33 us
    pallas_call x8 -> x10, Pallas kernels: 12.8 us -> 12.2 us  [in_vmem(): pl.pallas_call(kernel, out_shape=out_shape, in_specs=[pl.BlockSpec(memory...]
  transfers between devices with their start and end apart: 30 -> 30, of which waited for: 17 -> 16; matrix products, arithmetic and copies ran while one was open for 3% -> 0% of each run, Pallas kernels for 8% -> 9%
where the time goes in v3:
time: 111 us; the launch traced here: 110 us
  starting transfers between devices  39.4 us (35%)
  waiting for transfers between devices  39 us (35%)
  between operations  13.6 us (12%)
  Pallas kernels  12.2 us (11%)
  local copies, waits for them, and re-layouts  6.33 us (6%)
    ppermute x27, starting transfers between devices, permuted(): lax.ppermute(array, axis, [(i, (i + by) % devices) for i in range(devices)])  34.9 us
    ppermute x27, waiting for transfers between devices, permuted(): lax.ppermute(array, axis, [(i, (i + by) % devices) for i in range(devices)])  26.9 us
    pallas_call x10, Pallas kernels, in_vmem(): pl.pallas_call(kernel, out_shape=out_shape, in_specs=[pl.BlockSpec(memory...  12.2 us
    all_gather x1, waiting for transfers between devices, per_device(): out_columns = lax.all_gather(both, ('core', 'z1', 'z0'), axis=0, tiled=True)  8.67 us
    unnamed x22, local copies, waits for them, and re-layouts  6.33 us
    all_to_all x1, starting transfers between devices, per_device(): lax.all_to_all(halves, ('y', 'core'), split_axis=0, concat_axis=0, tiled=...  4.47 us
    all_to_all x1, waiting for transfers between devices, per_device(): lax.all_to_all(halves, ('y', 'core'), split_axis=0, concat_axis=0, tiled=...  3.37 us
  transfers between devices with their start and end apart: 30, of which 16 were waited for; matrix products, arithmetic and copies ran while one was open for 0% of the time, Pallas kernels for 9%

profile of v3, /device:TPU:2, one launch (start us, length us, event | category | flops | bytes accessed | tf_op | source)
XLA Modules:
  0.0 110.5 jit_solution(6028230346585160333)
XLA Ops:
  6.5 2.1 %collective-permute-start = (bf16[48,2432]{1,0:T(8,128)(2,1)}, bf16[48,2432]{1,0:T(8,128)(2,1)S(1)}, u32[]{:S(2)}, u32[]{:S(2)}) collective-permute-start(bf16[48,2432]{1,0:T(8,128)(2,1)} %bitcast.13), channel_id=1, source_target_pairs={{0,128},{128,0},{1,129},{129,1},{2,130},{130,2},{3,131},{131,3},{4... | collective-permute-start | bytes 700424 | tf_op jit(solution)/shard_map/ppermute | solution.py:30
  11.2 4.5 %all-to-all-start = ((bf16[8,24,512]{2,1,0:T(8,128)(2,1)}), bf16[8,24,512]{2,1,0:T(8,128)(2,1)S(1)}, u32[]{:S(2)}, u32[]{:S(2)}) async-start(bf16[8,24,512]{2,1,0:T(8,128)(2,1)} %shard_map.83), calls=%async_computation | async-start | bytes 393216 | tf_op jit(solution)/shard_map/all_to_all | solution.py:340
  16.4 2.6 %shard_map.82 = (bf16[48,2560]{1,0:T(8,128)(2,1)}, f32[1,2432]{1,0:T(1,128)}) custom-call(s32[8]{0:T(128)} %steps_ref.1, bf16[48,2432]{1,0:T(8,128)(2,1)} %copy-done.1, f32[28,3,1,2432]{3,2,1,0:T(1,128)} %bitcast.12), custom_call_target="tpu_custom_call" | custom-call | bytes 233504 | tf_op jit(solution)/shard_map/pallas_call | solution.py:311
  19.1 3.4 %all-to-all-done.received_ref = bf16[8,24,512]{2,1,0:T(8,128)(2,1)S(1)} async-done(((bf16[8,24,512]{2,1,0:T(8,128)(2,1)}), bf16[8,24,512]{2,1,0:T(8,128)(2,1)S(1)}, u32[]{:S(2)}, u32[]{:S(2)}) %all-to-all-start) | async-done | bytes 196640 | tf_op jit(solution)/shard_map/all_to_all | solution.py:340
  23.6 1.5 %collective-permute-start.1 = (bf16[152,512]{1,0:T(8,128)(2,1)S(1)}, bf16[152,512]{1,0:T(8,128)(2,1)S(1)}, u32[]{:S(2)}, u32[]{:S(2)}) collective-permute-start(bf16[152,512]{1,0:T(8,128)(2,1)S(1)} %get-tuple-element.18.refs_0_.after_ref), channel_id=1, source_target_pairs={{0,64},{64,0},{1,65},{65,1},{2,66},{66,2},{3,67},{67,3},{4,68},{68... | collective-permute-start | bytes 466952 | tf_op jit(solution)/shard_map/ppermute | solution.py:30
  25.1 1.9 %collective-permute-start.2 = (bf16[152,512]{1,0:T(8,128)(2,1)S(1)}, bf16[152,512]{1,0:T(8,128)(2,1)S(1)}, u32[]{:S(2)}, u32[]{:S(2)}) collective-permute-start(bf16[152,512]{1,0:T(8,128)(2,1)S(1)} %get-tuple-element.18.refs_0_.after_ref), channel_id=1, source_target_pairs={{0,8},{8,16},{16,24},{24,32},{32,40},{40,48},{48,56},{56,0},{1,9},... | collective-permute-start | bytes 466952 | tf_op jit(solution)/shard_map/ppermute | solution.py:30
  27.0 3.9 %collective-permute-start.4 = (bf16[152,512]{1,0:T(8,128)(2,1)S(1)}, bf16[152,512]{1,0:T(8,128)(2,1)S(1)}, u32[]{:S(2)}, u32[]{:S(2)}) collective-permute-start(bf16[152,512]{1,0:T(8,128)(2,1)S(1)} %get-tuple-element.18.refs_0_.after_ref), channel_id=1, source_target_pairs={{0,56},{8,0},{16,8},{24,16},{32,24},{40,32},{48,40},{56,48},{1,57}... | collective-permute-start | bytes 466952 | tf_op jit(solution)/shard_map/ppermute | solution.py:30
  31.0 4.0 %collective-permute-start.3 = (bf16[152,512]{1,0:T(8,128)(2,1)S(1)}, bf16[152,512]{1,0:T(8,128)(2,1)S(1)}, u32[]{:S(2)}, u32[]{:S(2)}) collective-permute-start(bf16[152,512]{1,0:T(8,128)(2,1)S(1)} %collective-permute-done.1.refs_1_), channel_id=1, source_target_pairs={{0,56},{8,0},{16,8},{24,16},{32,24},{40,32},{48,40},{56,48},{1,57}... | collective-permute-start | bytes 466952 | tf_op jit(solution)/shard_map/ppermute | solution.py:30
  35.0 3.3 %collective-permute-start.8 = (bf16[152,512]{1,0:T(8,128)(2,1)S(1)}, bf16[152,512]{1,0:T(8,128)(2,1)S(1)}, u32[]{:S(2)}, u32[]{:S(2)}) collective-permute-start(bf16[152,512]{1,0:T(8,128)(2,1)S(1)} %collective-permute-done.4.refs_4_), channel_id=1, source_target_pairs={{0,56},{8,0},{16,8},{24,16},{32,24},{40,32},{48,40},{56,48},{1,57}... | collective-permute-start | bytes 466952 | tf_op jit(solution)/shard_map/ppermute | solution.py:30
  38.3 1.5 %collective-permute-start.23 = (bf16[19,1216]{1,0:T(8,128)(2,1)S(1)}, bf16[19,1216]{1,0:T(8,128)(2,1)S(1)}, u32[]{:S(2)}, u32[]{:S(2)}) collective-permute-start(bf16[19,1216]{1,0:T(8,128)(2,1)S(1)} %shard_map.87), channel_id=1, source_target_pairs={{0,64},{64,0},{1,65},{65,1},{2,66},{66,2},{3,67},{67,3},{4,68},{68... | collective-permute-start | bytes 138632 | tf_op jit(solution)/shard_map/ppermute | solution.py:30
  39.9 2.8 %collective-permute-done.23.other_ref = bf16[19,1216]{1,0:T(8,128)(2,1)S(1)} collective-permute-done((bf16[19,1216]{1,0:T(8,128)(2,1)S(1)}, bf16[19,1216]{1,0:T(8,128)(2,1)S(1)}, u32[]{:S(2)}, u32[]{:S(2)}) %collective-permute-start.23) | collective-permute-done | bytes 46240 | tf_op jit(solution)/shard_map/ppermute | solution.py:30
  42.7 1.2 %collective-permute-done.6.refs_6_.refs_0_ = bf16[152,512]{1,0:T(8,128)(2,1)S(1)} collective-permute-done((bf16[152,512]{1,0:T(8,128)(2,1)S(1)}, bf16[152,512]{1,0:T(8,128)(2,1)S(1)}, u32[]{:S(2)}, u32[]{:S(2)}) %collective-permute-start.6) | collective-permute-done | bytes 155680 | tf_op jit(solution)/shard_map/ppermute | solution.py:30
  46.7 3.9 %collective-permute-done.7.refs_7_ = bf16[152,512]{1,0:T(8,128)(2,1)S(1)} collective-permute-done((bf16[152,512]{1,0:T(8,128)(2,1)S(1)}, bf16[152,512]{1,0:T(8,128)(2,1)S(1)}, u32[]{:S(2)}, u32[]{:S(2)}) %collective-permute-start.7) | collective-permute-done | bytes 155680 | tf_op jit(solution)/shard_map/ppermute | solution.py:30
  50.6 1.4 %collective-permute-start.11 = (bf16[152,512]{1,0:T(8,128)(2,1)S(1)}, bf16[152,512]{1,0:T(8,128)(2,1)S(1)}, u32[]{:S(2)}, u32[]{:S(2)}) collective-permute-start(bf16[152,512]{1,0:T(8,128)(2,1)S(1)} %collective-permute-done.7.refs_7_), channel_id=1, source_target_pairs={{0,56},{8,0},{16,8},{24,16},{32,24},{40,32},{48,40},{56,48},{1,57}... | collective-permute-start | bytes 466952 | tf_op jit(solution)/shard_map/ppermute | solution.py:30
  52.7 1.4 %collective-permute-start.13 = (bf16[152,512]{1,0:T(8,128)(2,1)S(1)}, bf16[152,512]{1,0:T(8,128)(2,1)S(1)}, u32[]{:S(2)}, u32[]{:S(2)}) collective-permute-start(bf16[152,512]{1,0:T(8,128)(2,1)S(1)} %collective-permute-done.9.refs_9_), channel_id=1, source_target_pairs={{0,8},{8,16},{16,24},{24,32},{32,40},{40,48},{48,56},{56,0},{1,9},... | collective-permute-start | bytes 466952 | tf_op jit(solution)/shard_map/ppermute | solution.py:30
  54.1 1.5 %collective-permute-done.10.refs_10_ = bf16[152,512]{1,0:T(8,128)(2,1)S(1)} collective-permute-done((bf16[152,512]{1,0:T(8,128)(2,1)S(1)}, bf16[152,512]{1,0:T(8,128)(2,1)S(1)}, u32[]{:S(2)}, u32[]{:S(2)}) %collective-permute-start.10) | collective-permute-done | bytes 155680 | tf_op jit(solution)/shard_map/ppermute | solution.py:30
  55.6 1.8 %collective-permute-done.11.refs_11_ = bf16[152,512]{1,0:T(8,128)(2,1)S(1)} collective-permute-done((bf16[152,512]{1,0:T(8,128)(2,1)S(1)}, bf16[152,512]{1,0:T(8,128)(2,1)S(1)}, u32[]{:S(2)}, u32[]{:S(2)}) %collective-permute-start.11) | collective-permute-done | bytes 155680 | tf_op jit(solution)/shard_map/ppermute | solution.py:30
  57.4 1.5 %collective-permute-start.15 = (bf16[152,512]{1,0:T(8,128)(2,1)S(1)}, bf16[152,512]{1,0:T(8,128)(2,1)S(1)}, u32[]{:S(2)}, u32[]{:S(2)}) collective-permute-start(bf16[152,512]{1,0:T(8,128)(2,1)S(1)} %collective-permute-done.11.refs_11_), channel_id=1, source_target_pairs={{0,56},{8,0},{16,8},{24,16},{32,24},{40,32},{48,40},{56,48},{1,57}... | collective-permute-start | bytes 466952 | tf_op jit(solution)/shard_map/ppermute | solution.py:30
  59.3 2.7 %collective-permute-done.14.refs_14_ = bf16[152,512]{1,0:T(8,128)(2,1)S(1)} collective-permute-done((bf16[152,512]{1,0:T(8,128)(2,1)S(1)}, bf16[152,512]{1,0:T(8,128)(2,1)S(1)}, u32[]{:S(2)}, u32[]{:S(2)}) %collective-permute-start.14) | collective-permute-done | bytes 155680 | tf_op jit(solution)/shard_map/ppermute | solution.py:30
  62.6 1.5 %copy-done = bf16[384,2560]{1,0:T(8,128)(2,1)S(1)} copy-done((bf16[384,2560]{1,0:T(8,128)(2,1)S(1)}, bf16[384,2560]{1,0:T(8,128)(2,1)}, u32[]{:S(2)}) %copy-start) | copy-done | bytes 1966104
  64.2 2.0 %shard_map.85 = (bf16[1120,128]{1,0:T(8,128)(2,1)S(1)}, bf16[384,192]{1,0:T(8,128)(2,1)S(1)}) custom-call(f32[2,1216]{1,0:T(2,128)S(1)} %bitcast.11, bf16[384,2560]{1,0:T(8,128)(2,1)S(1)} %copy-done, bf16[64,320]{1,0:T(8,128)(2,1)S(1)} %get-tuple-element.17.text_ref, bf16[152,512]{1,0:T(8,128)(2,1)S(1)} %get-tuple-element.18.refs_0_.after_ref, ...), custom_call_target="tpu_custom_call" | custom-call | flops 1006632960 | bytes 4507136 | tf_op jit(solution)/shard_map/pallas_call | solution.py:311
  66.4 7.2 %collective-permute-done.18.far = bf16[1120,128]{1,0:T(8,128)(2,1)S(1)} collective-permute-done((bf16[1120,128]{1,0:T(8,128)(2,1)S(1)}, bf16[1120,128]{1,0:T(8,128)(2,1)S(1)}, u32[]{:S(2)}, u32[]{:S(2)}) %collective-permute-start.18) | collective-permute-done | bytes 286752 | tf_op jit(solution)/shard_map/ppermute | solution.py:30
  74.1 1.3 %collective-permute-done.17.beside_q = bf16[384,192]{1,0:T(8,128)(2,1)S(1)} collective-permute-done((bf16[384,192]{1,0:T(8,128)(2,1)S(1)}, bf16[384,192]{1,0:T(8,128)(2,1)S(1)}, u32[]{:S(2)}, u32[]{:S(2)}) %collective-permute-start.17) | collective-permute-done | bytes 147488 | tf_op jit(solution)/shard_map/ppermute | solution.py:30
  75.5 3.1 %shard_map.86.a0 = bf16[480,128]{1,0:T(8,128)(2,1)S(1)} custom-call(s32[8]{0:T(128)S(1)} %copy-done.9, bf16[1120,128]{1,0:T(8,128)(2,1)S(1)} %get-tuple-element.19.own, bf16[1120,128]{1,0:T(8,128)(2,1)S(1)} %collective-permute-done.16.beside, bf16[384,192]{1,0:T(8,128)(2,1)S(1)} %get-tuple-element.20.own_q, ...), custom_call_target="tpu_custom_call" | custom-call | flops 220200960 | bytes 1441824 | tf_op jit(solution)/shard_map/pallas_call | solution.py:311
  79.5 2.2 %collective-permute-start.21 = (bf16[480,128]{1,0:T(8,128)(2,1)S(1)}, bf16[480,128]{1,0:T(8,128)(2,1)S(1)}, u32[]{:S(2)}, u32[]{:S(2)}) collective-permute-start(bf16[480,128]{1,0:T(8,128)(2,1)S(1)} %shard_map.86.a0), channel_id=1, source_target_pairs={{0,4},{2,6},{4,0},{6,2},{1,5},{3,7},{5,1},{7,3},{8,12},{10,14},{12... | collective-permute-start | bytes 368648 | tf_op jit(solution)/shard_map/ppermute | solution.py:30
  82.4 8.7 %all-gather.5.cloned.1.call-done.gathered_ref = bf16[640,1216]{1,0:T(8,128)(2,1)} async-done(((bf16[40,1216]{1,0:T(8,128)(2,1)}), bf16[640,1216]{1,0:T(8,128)(2,1)}) %all-gather.5.cloned.1.call-update) | async-done | bytes 1556496 | tf_op jit(solution)/shard_map/all_gather | solution.py:394
  91.1 1.4 %copy-done.10 = bf16[640,1216]{1,0:T(8,128)(2,1)S(1)} copy-done((bf16[640,1216]{1,0:T(8,128)(2,1)S(1)}, bf16[640,1216]{1,0:T(8,128)(2,1)}, u32[]{:S(2)}) %copy-start.10) | copy-done | bytes 1556504
  94.1 1.3 %collective-permute-start.24 = (bf16[48,608]{1,0:T(8,128)(2,1)S(1)}, bf16[48,608]{1,0:T(8,128)(2,1)S(1)}, u32[]{:S(2)}, u32[]{:S(2)}) collective-permute-start(bf16[48,608]{1,0:T(8,128)(2,1)S(1)} %get-tuple-element.22), channel_id=1, source_target_pairs={{0,2},{2,4},{4,6},{6,0},{1,3},{3,5},{5,7},{7,1},{8,10},{10,12},{12... | collective-permute-start | bytes 175112 | tf_op jit(solution)/shard_map/ppermute | solution.py:30
  95.4 2.7 %collective-permute-start.25 = (bf16[48,608]{1,0:T(8,128)(2,1)S(1)}, bf16[48,608]{1,0:T(8,128)(2,1)S(1)}, u32[]{:S(2)}, u32[]{:S(2)}) collective-permute-start(bf16[48,608]{1,0:T(8,128)(2,1)S(1)} %get-tuple-element.23), channel_id=1, source_target_pairs={{0,4},{2,6},{4,0},{6,2},{1,5},{3,7},{5,1},{7,3},{8,12},{10,14},{12... | collective-permute-start | bytes 175112 | tf_op jit(solution)/shard_map/ppermute | solution.py:30
  98.1 1.5 %collective-permute-start.26 = (bf16[48,608]{1,0:T(8,128)(2,1)S(1)}, bf16[48,608]{1,0:T(8,128)(2,1)S(1)}, u32[]{:S(2)}, u32[]{:S(2)}) collective-permute-start(bf16[48,608]{1,0:T(8,128)(2,1)S(1)} %get-tuple-element.24), channel_id=1, source_target_pairs={{0,6},{2,0},{4,2},{6,4},{1,7},{3,1},{5,3},{7,5},{8,14},{10,8},{12,... | collective-permute-start | bytes 175112 | tf_op jit(solution)/shard_map/ppermute | solution.py:30
  99.6 1.9 %collective-permute-done.25.n2 = bf16[48,608]{1,0:T(8,128)(2,1)S(1)} collective-permute-done((bf16[48,608]{1,0:T(8,128)(2,1)S(1)}, bf16[48,608]{1,0:T(8,128)(2,1)S(1)}, u32[]{:S(2)}, u32[]{:S(2)}) %collective-permute-start.25) | collective-permute-done | bytes 58400 | tf_op jit(solution)/shard_map/ppermute | solution.py:30
  102.3 1.3 %shard_map.91 = bf16[48,2432]{1,0:T(8,128)(2,1)} custom-call(f32[1,2432]{1,0:T(1,128)S(1)} %copy-done.8, bf16[48,2432]{1,0:T(8,128)(2,1)S(1)} %copy-done.2, bf16[48,608]{1,0:T(8,128)(2,1)S(1)} %get-tuple-element.21.n0, bf16[48,608]{1,0:T(8,128)(2,1)S(1)} %collective-permute-done.24.n1, bf16[48,608]{1,0:T(8,128)(2,1)S(1)} %collective-permute-done.25.n2, ...), custom_call_target="tpu_custom_call" | custom-call | bytes 476672 | tf_op jit(solution)/shard_map/pallas_call | solution.py:311
  (62 shorter events, 13.7 us)
Async XLA Ops:
  6.5 9.2 %collective-permute-start = (bf16[48,2432]{1,0:T(8,128)(2,1)}, bf16[48,2432]{1,0:T(8,128)(2,1)S(1)}, u32[]{:S(2)}, u32[]{:S(2)}) collective-permute-start(bf16[48,2432]{1,0:T(8,128)(2,1)} %bitcast.13), channel_id=1, source_target_pairs={{0,128},{128,0},{1,129},{129,1},{2,130},{130,2},{3,131},{131,3},{4... | collective-permute-start | bytes 700424 | tf_op jit(solution)/shard_map/ppermute | solution.py:30
  11.2 11.3 %all-to-all-start = ((bf16[8,24,512]{2,1,0:T(8,128)(2,1)}), bf16[8,24,512]{2,1,0:T(8,128)(2,1)S(1)}, u32[]{:S(2)}, u32[]{:S(2)}) async-start(bf16[8,24,512]{2,1,0:T(8,128)(2,1)} %shard_map.83), calls=%async_computation | async-start | bytes 393216 | tf_op jit(solution)/shard_map/all_to_all | solution.py:340
  15.7 47.0 %all-gather.3.cloned.1.call-start = ((), (), s32[]{:S(2)}) async-start(), calls=%async_computation.1 | async-start | bytes 2211840 | tf_op jit(solution)/shard_map/all_gather | solution.py:367
  19.0 19.3 %copy-start.4 = (bf16[1,1216,19]{1,2,0:T(8,128)(2,1)S(1)}, bf16[1,1216,19]{1,2,0:T(8,128)(2,1)}, u32[]{:S(2)}) copy-start(bf16[1,1216,19]{1,2,0:T(8,128)(2,1)} %param.14) | copy-start | bytes 138628
  19.0 43.6 %copy-start.7 = (f32[1,2,1216]{2,1,0:T(2,128)S(1)}, f32[1,2,1216]{2,1,0:T(2,128)}, u32[]{:S(2)}) copy-start(f32[1,2,1216]{2,1,0:T(2,128)} %param.15) | copy-start | bytes 29188
  19.1 72.0 %all-gather.5.cloned.1.call-start = ((), (), s32[]{:S(2)}) async-start(), calls=%async_computation.2 | async-start | bytes 1740800 | tf_op jit(solution)/shard_map/all_gather | solution.py:394
  23.6 7.4 %collective-permute-start.1 = (bf16[152,512]{1,0:T(8,128)(2,1)S(1)}, bf16[152,512]{1,0:T(8,128)(2,1)S(1)}, u32[]{:S(2)}, u32[]{:S(2)}) collective-permute-start(bf16[152,512]{1,0:T(8,128)(2,1)S(1)} %get-tuple-element.18.refs_0_.after_ref), channel_id=1, source_target_pairs={{0,64},{64,0},{1,65},{65,1},{2,66},{66,2},{3,67},{67,3},{4,68},{68... | collective-permute-start | bytes 466952 | tf_op jit(solution)/shard_map/ppermute | solution.py:30
  25.1 9.9 %collective-permute-start.2 = (bf16[152,512]{1,0:T(8,128)(2,1)S(1)}, bf16[152,512]{1,0:T(8,128)(2,1)S(1)}, u32[]{:S(2)}, u32[]{:S(2)}) collective-permute-start(bf16[152,512]{1,0:T(8,128)(2,1)S(1)} %get-tuple-element.18.refs_0_.after_ref), channel_id=1, source_target_pairs={{0,8},{8,16},{16,24},{24,32},{32,40},{40,48},{48,56},{56,0},{1,9},... | collective-permute-start | bytes 466952 | tf_op jit(solution)/shard_map/ppermute | solution.py:30
  27.0 8.0 %collective-permute-start.4 = (bf16[152,512]{1,0:T(8,128)(2,1)S(1)}, bf16[152,512]{1,0:T(8,128)(2,1)S(1)}, u32[]{:S(2)}, u32[]{:S(2)}) collective-permute-start(bf16[152,512]{1,0:T(8,128)(2,1)S(1)} %get-tuple-element.18.refs_0_.after_ref), channel_id=1, source_target_pairs={{0,56},{8,0},{16,8},{24,16},{32,24},{40,32},{48,40},{56,48},{1,57}... | collective-permute-start | bytes 466952 | tf_op jit(solution)/shard_map/ppermute | solution.py:30
  31.0 11.7 %collective-permute-start.3 = (bf16[152,512]{1,0:T(8,128)(2,1)S(1)}, bf16[152,512]{1,0:T(8,128)(2,1)S(1)}, u32[]{:S(2)}, u32[]{:S(2)}) collective-permute-start(bf16[152,512]{1,0:T(8,128)(2,1)S(1)} %collective-permute-done.1.refs_1_), channel_id=1, source_target_pairs={{0,56},{8,0},{16,8},{24,16},{32,24},{40,32},{48,40},{56,48},{1,57}... | collective-permute-start | bytes 466952 | tf_op jit(solution)/shard_map/ppermute | solution.py:30
  35.0 7.7 %collective-permute-start.5 = (bf16[152,512]{1,0:T(8,128)(2,1)S(1)}, bf16[152,512]{1,0:T(8,128)(2,1)S(1)}, u32[]{:S(2)}, u32[]{:S(2)}) collective-permute-start(bf16[152,512]{1,0:T(8,128)(2,1)S(1)} %collective-permute-done.1.refs_1_), channel_id=1, source_target_pairs={{0,8},{8,16},{16,24},{24,32},{32,40},{40,48},{48,56},{56,0},{1,9},... | collective-permute-start | bytes 466952 | tf_op jit(solution)/shard_map/ppermute | solution.py:30
  35.0 8.8 %collective-permute-start.6 = (bf16[152,512]{1,0:T(8,128)(2,1)S(1)}, bf16[152,512]{1,0:T(8,128)(2,1)S(1)}, u32[]{:S(2)}, u32[]{:S(2)}) collective-permute-start(bf16[152,512]{1,0:T(8,128)(2,1)S(1)} %collective-permute-done.2.refs_2_), channel_id=1, source_target_pairs={{0,8},{8,16},{16,24},{24,32},{32,40},{40,48},{48,56},{56,0},{1,9},... | collective-permute-start | bytes 466952 | tf_op jit(solution)/shard_map/ppermute | solution.py:30
  35.0 8.8 %collective-permute-start.8 = (bf16[152,512]{1,0:T(8,128)(2,1)S(1)}, bf16[152,512]{1,0:T(8,128)(2,1)S(1)}, u32[]{:S(2)}, u32[]{:S(2)}) collective-permute-start(bf16[152,512]{1,0:T(8,128)(2,1)S(1)} %collective-permute-done.4.refs_4_), channel_id=1, source_target_pairs={{0,56},{8,0},{16,8},{24,16},{32,24},{40,32},{48,40},{56,48},{1,57}... | collective-permute-start | bytes 466952 | tf_op jit(solution)/shard_map/ppermute | solution.py:30
  38.3 4.3 %collective-permute-start.23 = (bf16[19,1216]{1,0:T(8,128)(2,1)S(1)}, bf16[19,1216]{1,0:T(8,128)(2,1)S(1)}, u32[]{:S(2)}, u32[]{:S(2)}) collective-permute-start(bf16[19,1216]{1,0:T(8,128)(2,1)S(1)} %shard_map.87), channel_id=1, source_target_pairs={{0,64},{64,0},{1,65},{65,1},{2,66},{66,2},{3,67},{67,3},{4,68},{68... | collective-permute-start | bytes 138632 | tf_op jit(solution)/shard_map/ppermute | solution.py:30
  44.6 6.0 %collective-permute-start.7 = (bf16[152,512]{1,0:T(8,128)(2,1)S(1)}, bf16[152,512]{1,0:T(8,128)(2,1)S(1)}, u32[]{:S(2)}, u32[]{:S(2)}) collective-permute-start(bf16[152,512]{1,0:T(8,128)(2,1)S(1)} %collective-permute-done.3.refs_3_), channel_id=1, source_target_pairs={{0,56},{8,0},{16,8},{24,16},{32,24},{40,32},{48,40},{56,48},{1,57}... | collective-permute-start | bytes 466952 | tf_op jit(solution)/shard_map/ppermute | solution.py:30
  45.6 7.1 %collective-permute-start.9 = (bf16[152,512]{1,0:T(8,128)(2,1)S(1)}, bf16[152,512]{1,0:T(8,128)(2,1)S(1)}, u32[]{:S(2)}, u32[]{:S(2)}) collective-permute-start(bf16[152,512]{1,0:T(8,128)(2,1)S(1)} %collective-permute-done.5.refs_5_.refs_2_), channel_id=1, source_target_pairs={{0,8},{8,16},{16,24},{24,32},{32,40},{40,48},{48,56},{56,0},{1,9},... | collective-permute-start | bytes 466952 | tf_op jit(solution)/shard_map/ppermute | solution.py:30
  46.7 8.9 %collective-permute-start.10 = (bf16[152,512]{1,0:T(8,128)(2,1)S(1)}, bf16[152,512]{1,0:T(8,128)(2,1)S(1)}, u32[]{:S(2)}, u32[]{:S(2)}) collective-permute-start(bf16[152,512]{1,0:T(8,128)(2,1)S(1)} %collective-permute-done.6.refs_6_.refs_0_), channel_id=1, source_target_pairs={{0,8},{8,16},{16,24},{24,32},{32,40},{40,48},{48,56},{56,0},{1,9},... | collective-permute-start | bytes 466952 | tf_op jit(solution)/shard_map/ppermute | solution.py:30
  50.6 6.8 %collective-permute-start.11 = (bf16[152,512]{1,0:T(8,128)(2,1)S(1)}, bf16[152,512]{1,0:T(8,128)(2,1)S(1)}, u32[]{:S(2)}, u32[]{:S(2)}) collective-permute-start(bf16[152,512]{1,0:T(8,128)(2,1)S(1)} %collective-permute-done.7.refs_7_), channel_id=1, source_target_pairs={{0,56},{8,0},{16,8},{24,16},{32,24},{40,32},{48,40},{56,48},{1,57}... | collective-permute-start | bytes 466952 | tf_op jit(solution)/shard_map/ppermute | solution.py:30
  52.0 7.1 %collective-permute-start.12 = (bf16[152,512]{1,0:T(8,128)(2,1)S(1)}, bf16[152,512]{1,0:T(8,128)(2,1)S(1)}, u32[]{:S(2)}, u32[]{:S(2)}) collective-permute-start(bf16[152,512]{1,0:T(8,128)(2,1)S(1)} %collective-permute-done.8.refs_8_.refs_1_), channel_id=1, source_target_pairs={{0,56},{8,0},{16,8},{24,16},{32,24},{40,32},{48,40},{56,48},{1,57}... | collective-permute-start | bytes 466952 | tf_op jit(solution)/shard_map/ppermute | solution.py:30
  52.7 6.7 %collective-permute-start.13 = (bf16[152,512]{1,0:T(8,128)(2,1)S(1)}, bf16[152,512]{1,0:T(8,128)(2,1)S(1)}, u32[]{:S(2)}, u32[]{:S(2)}) collective-permute-start(bf16[152,512]{1,0:T(8,128)(2,1)S(1)} %collective-permute-done.9.refs_9_), channel_id=1, source_target_pairs={{0,8},{8,16},{16,24},{24,32},{32,40},{40,48},{48,56},{56,0},{1,9},... | collective-permute-start | bytes 466952 | tf_op jit(solution)/shard_map/ppermute | solution.py:30
  55.6 6.4 %collective-permute-start.14 = (bf16[152,512]{1,0:T(8,128)(2,1)S(1)}, bf16[152,512]{1,0:T(8,128)(2,1)S(1)}, u32[]{:S(2)}, u32[]{:S(2)}) collective-permute-start(bf16[152,512]{1,0:T(8,128)(2,1)S(1)} %collective-permute-done.10.refs_10_), channel_id=1, source_target_pairs={{0,8},{8,16},{16,24},{24,32},{32,40},{40,48},{48,56},{56,0},{1,9},... | collective-permute-start | bytes 466952 | tf_op jit(solution)/shard_map/ppermute | solution.py:30
  57.4 5.2 %collective-permute-start.15 = (bf16[152,512]{1,0:T(8,128)(2,1)S(1)}, bf16[152,512]{1,0:T(8,128)(2,1)S(1)}, u32[]{:S(2)}, u32[]{:S(2)}) collective-permute-start(bf16[152,512]{1,0:T(8,128)(2,1)S(1)} %collective-permute-done.11.refs_11_), channel_id=1, source_target_pairs={{0,56},{8,0},{16,8},{24,16},{32,24},{40,32},{48,40},{56,48},{1,57}... | collective-permute-start | bytes 466952 | tf_op jit(solution)/shard_map/ppermute | solution.py:30
  66.2 7.4 %collective-permute-start.18 = (bf16[1120,128]{1,0:T(8,128)(2,1)S(1)}, bf16[1120,128]{1,0:T(8,128)(2,1)S(1)}, u32[]{:S(2)}, u32[]{:S(2)}) collective-permute-start(bf16[1120,128]{1,0:T(8,128)(2,1)S(1)} %get-tuple-element.19.own), channel_id=1, source_target_pairs={{0,8},{8,0},{1,9},{9,1},{2,10},{10,2},{3,11},{11,3},{4,12},{12,4},... | collective-permute-start | bytes 860168 | tf_op jit(solution)/shard_map/ppermute | solution.py:30
  66.3 9.2 %collective-permute-start.16 = (bf16[1120,128]{1,0:T(8,128)(2,1)S(1)}, bf16[1120,128]{1,0:T(8,128)(2,1)S(1)}, u32[]{:S(2)}, u32[]{:S(2)}) collective-permute-start(bf16[1120,128]{1,0:T(8,128)(2,1)S(1)} %get-tuple-element.19.own), channel_id=1, source_target_pairs={{0,1},{1,0},{2,3},{3,2},{4,5},{5,4},{6,7},{7,6},{8,9},{9,8},{10,11... | collective-permute-start | bytes 860168 | tf_op jit(solution)/shard_map/ppermute | solution.py:30
  73.6 1.9 %collective-permute-start.19 = (bf16[1120,128]{1,0:T(8,128)(2,1)S(1)}, bf16[1120,128]{1,0:T(8,128)(2,1)S(1)}, u32[]{:S(2)}, u32[]{:S(2)}) collective-permute-start(bf16[1120,128]{1,0:T(8,128)(2,1)S(1)} %collective-permute-done.18.far), channel_id=1, source_target_pairs={{0,1},{1,0},{2,3},{3,2},{4,5},{5,4},{6,7},{7,6},{8,9},{9,8},{10,11... | collective-permute-start | bytes 860168 | tf_op jit(solution)/shard_map/ppermute | solution.py:30
  73.6 1.8 %collective-permute-start.17 = (bf16[384,192]{1,0:T(8,128)(2,1)S(1)}, bf16[384,192]{1,0:T(8,128)(2,1)S(1)}, u32[]{:S(2)}, u32[]{:S(2)}) collective-permute-start(bf16[384,192]{1,0:T(8,128)(2,1)S(1)} %get-tuple-element.20.own_q), channel_id=1, source_target_pairs={{0,1},{1,0},{2,3},{3,2},{4,5},{5,4},{6,7},{7,6},{8,9},{9,8},{10,11... | collective-permute-start | bytes 442376 | tf_op jit(solution)/shard_map/ppermute | solution.py:30
  78.5 14.5 %collective-permute-start.20 = (bf16[480,128]{1,0:T(8,128)(2,1)S(1)}, bf16[480,128]{1,0:T(8,128)(2,1)S(1)}, u32[]{:S(2)}, u32[]{:S(2)}) collective-permute-start(bf16[480,128]{1,0:T(8,128)(2,1)S(1)} %shard_map.86.a0), channel_id=1, source_target_pairs={{0,2},{2,4},{4,6},{6,0},{1,3},{3,5},{5,7},{7,1},{8,10},{10,12},{12... | collective-permute-start | bytes 368648 | tf_op jit(solution)/shard_map/ppermute | solution.py:30
  79.5 13.5 %collective-permute-start.21 = (bf16[480,128]{1,0:T(8,128)(2,1)S(1)}, bf16[480,128]{1,0:T(8,128)(2,1)S(1)}, u32[]{:S(2)}, u32[]{:S(2)}) collective-permute-start(bf16[480,128]{1,0:T(8,128)(2,1)S(1)} %shard_map.86.a0), channel_id=1, source_target_pairs={{0,4},{2,6},{4,0},{6,2},{1,5},{3,7},{5,1},{7,3},{8,12},{10,14},{12... | collective-permute-start | bytes 368648 | tf_op jit(solution)/shard_map/ppermute | solution.py:30
  81.7 11.3 %collective-permute-start.22 = (bf16[480,128]{1,0:T(8,128)(2,1)S(1)}, bf16[480,128]{1,0:T(8,128)(2,1)S(1)}, u32[]{:S(2)}, u32[]{:S(2)}) collective-permute-start(bf16[480,128]{1,0:T(8,128)(2,1)S(1)} %shard_map.86.a0), channel_id=1, source_target_pairs={{0,6},{2,0},{4,2},{6,4},{1,7},{3,1},{5,3},{7,5},{8,14},{10,8},{12,... | collective-permute-start | bytes 368648 | tf_op jit(solution)/shard_map/ppermute | solution.py:30
  94.1 5.5 %collective-permute-start.24 = (bf16[48,608]{1,0:T(8,128)(2,1)S(1)}, bf16[48,608]{1,0:T(8,128)(2,1)S(1)}, u32[]{:S(2)}, u32[]{:S(2)}) collective-permute-start(bf16[48,608]{1,0:T(8,128)(2,1)S(1)} %get-tuple-element.22), channel_id=1, source_target_pairs={{0,2},{2,4},{4,6},{6,0},{1,3},{3,5},{5,7},{7,1},{8,10},{10,12},{12... | collective-permute-start | bytes 175112 | tf_op jit(solution)/shard_map/ppermute | solution.py:30
  95.4 6.2 %collective-permute-start.25 = (bf16[48,608]{1,0:T(8,128)(2,1)S(1)}, bf16[48,608]{1,0:T(8,128)(2,1)S(1)}, u32[]{:S(2)}, u32[]{:S(2)}) collective-permute-start(bf16[48,608]{1,0:T(8,128)(2,1)S(1)} %get-tuple-element.23), channel_id=1, source_target_pairs={{0,4},{2,6},{4,0},{6,2},{1,5},{3,7},{5,1},{7,3},{8,12},{10,14},{12... | collective-permute-start | bytes 175112 | tf_op jit(solution)/shard_map/ppermute | solution.py:30
  98.1 4.2 %collective-permute-start.26 = (bf16[48,608]{1,0:T(8,128)(2,1)S(1)}, bf16[48,608]{1,0:T(8,128)(2,1)S(1)}, u32[]{:S(2)}, u32[]{:S(2)}) collective-permute-start(bf16[48,608]{1,0:T(8,128)(2,1)S(1)} %get-tuple-element.24), channel_id=1, source_target_pairs={{0,6},{2,0},{4,2},{6,4},{1,7},{3,1},{5,3},{7,5},{8,14},{10,8},{12,... | collective-permute-start | bytes 175112 | tf_op jit(solution)/shard_map/ppermute | solution.py:30
  (9 other events, 36.2 us)
Sparse Core Ops, SparseCore 0:
  19.2 30.4 all-gather.2
  51.5 39.5 all-gather.4

commit v4 on v3

--- a/solution.py
+++ b/solution.py
@@ -51,7 +51,10 @@
     out_ref[...] = room[...].astype(BF16)
 
 
-def prepare_kernel(weight_ref, text_ref, out_ref, room):
+def prepare_kernel(steps_ref, weight_ref, text_ref, table_ref, out_ref, picked_ref, room, arrived):
+    step = steps_ref[lax.axis_index("x") * 4 + lax.axis_index("z1")]
+    copy = pltpu.make_async_copy(table_ref.at[step], picked_ref, arrived)
+    copy.start()
     weight_rows = weight_ref.shape[0]
     head_width = HEADS * HD
     room[...] = jnp.zeros_like(room)
@@ -78,6 +81,7 @@
             if size == YW:
                 room[slot, 23:24, YW + 128 :] = text[7:8, split + 64 :]
     out_ref[...] = room[...].astype(BF16)
+    copy.wait()
 
 
 def compact_kernel(received_ref, *refs):
@@ -97,16 +101,10 @@
     text_ref[...] = text_room[...].astype(BF16)
 
 
-def modulate_kernel(steps_ref, raw_ref, table_ref, *refs):
-    h_ref, gate_ref, modulation, arrived = refs[-4:]
-    step = steps_ref[lax.axis_index("x") * 4 + lax.axis_index("z1")]
-    copy = pltpu.make_async_copy(table_ref.at[step], modulation, arrived)
-    copy.start()
+def modulate_kernel(modulation, raw_ref, h_ref):
     wide = raw_ref[...].astype(F32)
     centred = wide - jnp.mean(wide, axis=-1, keepdims=True)
     normed = centred * lax.rsqrt(jnp.mean(centred * centred, axis=-1, keepdims=True) + EPSILON)
-    copy.wait()
-    gate_ref[...] = modulation[2]
     modulated = normed * (1.0 + modulation[1]) + modulation[0]
     modulated = modulated.astype(BF16)
     h_ref[...] = jnp.zeros_like(h_ref)
@@ -289,7 +287,7 @@
         out_ref[...] = result[lax.rem(y + by, 4)]
 
 
-def assemble_kernel(gate_ref, raw_ref, n0, n1, n2, n3, out_ref, branch):
+def assemble_kernel(modulation, raw_ref, n0, n1, n2, n3, out_ref, branch):
     y = lax.axis_index("y")
     run = n0.shape[1] // 16
     for by, part in enumerate((n0, n1, n2, n3)):
@@ -302,7 +300,7 @@
                     at = (m * 4 + q) * run
                     branch[:, at : at + run] = value[:, m * run : (m + 1) * run]
 
-    out_ref[...] = (raw_ref[...].astype(F32) + gate_ref[...] * branch[...]).astype(BF16)
+    out_ref[...] = (raw_ref[...].astype(F32) + modulation[2] * branch[...]).astype(BF16)
 
 
 def in_vmem(kernel, out_shape, args, flops=0, scratch=(), scalars=0, after=(), anywhere=(), limit=8):
@@ -331,27 +329,21 @@
     quarter = width // 4
     split = HALF - YW
 
-    halves = in_vmem(
+    halves, modulation = in_vmem(
         prepare_kernel,
-        jax.ShapeDtypeStruct((8, 24, HALF), BF16),
-        (qkv_weight[0], text_kv),
-        scratch=[pltpu.VMEM((8, 24, HALF), F32)],
-    )
-    received = lax.all_to_all(halves, ("y", "core"), split_axis=0, concat_axis=0, tiled=True)
-    shard = jnp.transpose(out_weight[0])
-
-    raw = permuted(stale_states[0], "comp", 1)
-    h, gate = in_vmem(
-        modulate_kernel,
-        (
-            jax.ShapeDtypeStruct((rows, 16 * SLOT), BF16),
-            jax.ShapeDtypeStruct((1, width), F32),
-        ),
-        (timesteps, raw),
-        scratch=[pltpu.VMEM((3, 1, width), F32), pltpu.SemaphoreType.DMA],
+        (jax.ShapeDtypeStruct((8, 24, HALF), BF16), jax.ShapeDtypeStruct((3, 1, width), F32)),
+        (timesteps, qkv_weight[0], text_kv),
+        scratch=[pltpu.VMEM((8, 24, HALF), F32), pltpu.SemaphoreType.DMA],
         scalars=1,
         anywhere=(mod_table.reshape(mod_table.shape[1:3] + (1, width)),),
         limit=60,
+    )
+    received = lax.all_to_all(halves, ("y", "core"), split_axis=0, concat_axis=0, tiled=True)
+    shard = jnp.transpose(out_weight[0])
+
+    raw = permuted(stale_states[0], "comp", 1)
+    h = in_vmem(
+        modulate_kernel, jax.ShapeDtypeStruct((rows, 16 * SLOT), BF16), (modulation, raw)
     )
     block, text = in_vmem(
         compact_kernel,
@@ -450,7 +442,7 @@
     new = in_vmem(
         assemble_kernel,
         jax.ShapeDtypeStruct((rows, width), BF16),
-        (gate, raw, *parts),
+        (modulation, raw, *parts),
         scratch=[pltpu.VMEM((rows, width), F32)],
     )
     return new[None]

time: 111 us -> 110 us (level)
  local copies, waits for them, and re-layouts: 6.33 us -> 3.75 us
    unnamed x22 -> x14, local copies, waits for them, and re-layouts: 6.33 us -> 3.75 us
    all_gather x1, waiting for transfers between devices: 8.67 us -> 7.27 us  [per_device(): out_columns = lax.all_gather(both, ('core', 'z1', 'z0'), axis=0, tiled=True)]
    all_to_all x1, waiting for transfers between devices: 3.37 us -> 4.72 us  [per_device(): lax.all_to_all(halves, ('y', 'core'), split_axis=0, concat_axis=0, tiled=...]
  transfers between devices with their start and end apart: 30 -> 30, of which waited for: 16 -> 17; matrix products, arithmetic and copies ran while one was open for 0% -> 0% of each run, Pallas kernels for 9% -> 10%
where the time goes in v4:
time: 110 us; the launch traced here: 109 us
  waiting for transfers between devices  39.5 us (36%)
  starting transfers between devices  39.3 us (36%)
  between operations  13.5 us (12%)
  Pallas kernels  13.2 us (12%)
  local copies, waits for them, and re-layouts  3.75 us (3%)
    ppermute x27, starting transfers between devices, permuted(): lax.ppermute(array, axis, [(i, (i + by) % devices) for i in range(devices)])  34.7 us
    ppermute x27, waiting for transfers between devices, permuted(): lax.ppermute(array, axis, [(i, (i + by) % devices) for i in range(devices)])  27.5 us
    pallas_call x10, Pallas kernels, in_vmem(): pl.pallas_call(kernel, out_shape=out_shape, in_specs=[pl.BlockSpec(memory...  13.2 us
    all_gather x1, waiting for transfers between devices, per_device(): out_columns = lax.all_gather(both, ('core', 'z1', 'z0'), axis=0, tiled=True)  7.27 us
    all_to_all x1, waiting for transfers between devices, per_device(): lax.all_to_all(halves, ('y', 'core'), split_axis=0, concat_axis=0, tiled=...  4.72 us
    all_to_all x1, starting transfers between devices, per_device(): lax.all_to_all(halves, ('y', 'core'), split_axis=0, concat_axis=0, tiled=...  4.48 us
    unnamed x14, local copies, waits for them, and re-layouts  3.75 us
  transfers between devices with their start and end apart: 30, of which 17 were waited for; matrix products, arithmetic and copies ran while one was open for 0% of the time, Pallas kernels for 10%

profile of v4, /device:TPU:2, one launch (start us, length us, event | category | flops | bytes accessed | tf_op | source)
XLA Modules:
  0.0 109.2 jit_solution(2120126442883424570)
XLA Ops:
  6.5 2.1 %collective-permute-start = (bf16[48,2432]{1,0:T(8,128)(2,1)}, bf16[48,2432]{1,0:T(8,128)(2,1)S(1)}, u32[]{:S(2)}, u32[]{:S(2)}) collective-permute-start(bf16[48,2432]{1,0:T(8,128)(2,1)} %bitcast.13), channel_id=1, source_target_pairs={{0,128},{128,0},{1,129},{129,1},{2,130},{130,2},{3,131},{131,3},{4... | collective-permute-start | bytes 700424 | tf_op jit(solution)/shard_map/ppermute | solution.py:30
  8.7 2.4 %shard_map.82 = (bf16[8,24,512]{2,1,0:T(8,128)(2,1)}, f32[3,1,2432]{2,1,0:T(1,128)}) custom-call(s32[8]{0:T(128)} %steps_ref.1, bf16[19,3648]{1,0:T(8,128)(2,1)} %bitcast.12, bf16[2,8,1216]{2,1,0:T(8,128)(2,1)} %text_ref.1, f32[28,3,1,2432]{3,2,1,0:T(1,128)} %bitcast.11), custom_call_target="tpu_custom_call" | custom-call | bytes 177568 | tf_op jit(solution)/shard_map/pallas_call | solution.py:309
  11.1 4.5 %all-to-all-start = ((bf16[8,24,512]{2,1,0:T(8,128)(2,1)}), bf16[8,24,512]{2,1,0:T(8,128)(2,1)S(1)}, u32[]{:S(2)}, u32[]{:S(2)}) async-start(bf16[8,24,512]{2,1,0:T(8,128)(2,1)} %get-tuple-element.16), calls=%async_computation | async-start | bytes 393216 | tf_op jit(solution)/shard_map/all_to_all | solution.py:341
  16.4 1.1 %shard_map.83.refs_0_ = bf16[48,2560]{1,0:T(8,128)(2,1)} custom-call(f32[3,1,2432]{2,1,0:T(1,128)S(1)} %copy-done.2, bf16[48,2432]{1,0:T(8,128)(2,1)S(1)} %collective-permute-done.raw_ref), custom_call_target="tpu_custom_call" | custom-call | bytes 262656 | tf_op jit(solution)/shard_map/pallas_call | solution.py:309
  17.7 4.7 %all-to-all-done.received_ref = bf16[8,24,512]{2,1,0:T(8,128)(2,1)S(1)} async-done(((bf16[8,24,512]{2,1,0:T(8,128)(2,1)}), bf16[8,24,512]{2,1,0:T(8,128)(2,1)S(1)}, u32[]{:S(2)}, u32[]{:S(2)}) %all-to-all-start) | async-done | bytes 196640 | tf_op jit(solution)/shard_map/all_to_all | solution.py:341
  23.5 1.5 %collective-permute-start.1 = (bf16[152,512]{1,0:T(8,128)(2,1)S(1)}, bf16[152,512]{1,0:T(8,128)(2,1)S(1)}, u32[]{:S(2)}, u32[]{:S(2)}) collective-permute-start(bf16[152,512]{1,0:T(8,128)(2,1)S(1)} %get-tuple-element.18.refs_0_.after_ref), channel_id=1, source_target_pairs={{0,64},{64,0},{1,65},{65,1},{2,66},{66,2},{3,67},{67,3},{4,68},{68... | collective-permute-start | bytes 466952 | tf_op jit(solution)/shard_map/ppermute | solution.py:30
  25.0 1.9 %collective-permute-start.2 = (bf16[152,512]{1,0:T(8,128)(2,1)S(1)}, bf16[152,512]{1,0:T(8,128)(2,1)S(1)}, u32[]{:S(2)}, u32[]{:S(2)}) collective-permute-start(bf16[152,512]{1,0:T(8,128)(2,1)S(1)} %get-tuple-element.18.refs_0_.after_ref), channel_id=1, source_target_pairs={{0,8},{8,16},{16,24},{24,32},{32,40},{40,48},{48,56},{56,0},{1,9},... | collective-permute-start | bytes 466952 | tf_op jit(solution)/shard_map/ppermute | solution.py:30
  26.9 3.9 %collective-permute-start.4 = (bf16[152,512]{1,0:T(8,128)(2,1)S(1)}, bf16[152,512]{1,0:T(8,128)(2,1)S(1)}, u32[]{:S(2)}, u32[]{:S(2)}) collective-permute-start(bf16[152,512]{1,0:T(8,128)(2,1)S(1)} %get-tuple-element.18.refs_0_.after_ref), channel_id=1, source_target_pairs={{0,56},{8,0},{16,8},{24,16},{32,24},{40,32},{48,40},{56,48},{1,57}... | collective-permute-start | bytes 466952 | tf_op jit(solution)/shard_map/ppermute | solution.py:30
  30.8 4.0 %collective-permute-start.3 = (bf16[152,512]{1,0:T(8,128)(2,1)S(1)}, bf16[152,512]{1,0:T(8,128)(2,1)S(1)}, u32[]{:S(2)}, u32[]{:S(2)}) collective-permute-start(bf16[152,512]{1,0:T(8,128)(2,1)S(1)} %collective-permute-done.1.refs_1_), channel_id=1, source_target_pairs={{0,56},{8,0},{16,8},{24,16},{32,24},{40,32},{48,40},{56,48},{1,57}... | collective-permute-start | bytes 466952 | tf_op jit(solution)/shard_map/ppermute | solution.py:30
  34.9 3.3 %collective-permute-start.8 = (bf16[152,512]{1,0:T(8,128)(2,1)S(1)}, bf16[152,512]{1,0:T(8,128)(2,1)S(1)}, u32[]{:S(2)}, u32[]{:S(2)}) collective-permute-start(bf16[152,512]{1,0:T(8,128)(2,1)S(1)} %collective-permute-done.4.refs_4_), channel_id=1, source_target_pairs={{0,56},{8,0},{16,8},{24,16},{32,24},{40,32},{48,40},{56,48},{1,57}... | collective-permute-start | bytes 466952 | tf_op jit(solution)/shard_map/ppermute | solution.py:30
  38.2 1.5 %collective-permute-start.23 = (bf16[19,1216]{1,0:T(8,128)(2,1)S(1)}, bf16[19,1216]{1,0:T(8,128)(2,1)S(1)}, u32[]{:S(2)}, u32[]{:S(2)}) collective-permute-start(bf16[19,1216]{1,0:T(8,128)(2,1)S(1)} %shard_map.87), channel_id=1, source_target_pairs={{0,64},{64,0},{1,65},{65,1},{2,66},{66,2},{3,67},{67,3},{4,68},{68... | collective-permute-start | bytes 138632 | tf_op jit(solution)/shard_map/ppermute | solution.py:30
  39.7 2.8 %collective-permute-done.23.other_ref = bf16[19,1216]{1,0:T(8,128)(2,1)S(1)} collective-permute-done((bf16[19,1216]{1,0:T(8,128)(2,1)S(1)}, bf16[19,1216]{1,0:T(8,128)(2,1)S(1)}, u32[]{:S(2)}, u32[]{:S(2)}) %collective-permute-start.23) | collective-permute-done | bytes 46240 | tf_op jit(solution)/shard_map/ppermute | solution.py:30
  42.5 1.2 %collective-permute-done.6.refs_6_.refs_0_ = bf16[152,512]{1,0:T(8,128)(2,1)S(1)} collective-permute-done((bf16[152,512]{1,0:T(8,128)(2,1)S(1)}, bf16[152,512]{1,0:T(8,128)(2,1)S(1)}, u32[]{:S(2)}, u32[]{:S(2)}) %collective-permute-start.6) | collective-permute-done | bytes 155680 | tf_op jit(solution)/shard_map/ppermute | solution.py:30
  46.6 3.8 %collective-permute-done.7.refs_7_ = bf16[152,512]{1,0:T(8,128)(2,1)S(1)} collective-permute-done((bf16[152,512]{1,0:T(8,128)(2,1)S(1)}, bf16[152,512]{1,0:T(8,128)(2,1)S(1)}, u32[]{:S(2)}, u32[]{:S(2)}) %collective-permute-start.7) | collective-permute-done | bytes 155680 | tf_op jit(solution)/shard_map/ppermute | solution.py:30
  50.4 1.5 %collective-permute-start.11 = (bf16[152,512]{1,0:T(8,128)(2,1)S(1)}, bf16[152,512]{1,0:T(8,128)(2,1)S(1)}, u32[]{:S(2)}, u32[]{:S(2)}) collective-permute-start(bf16[152,512]{1,0:T(8,128)(2,1)S(1)} %collective-permute-done.7.refs_7_), channel_id=1, source_target_pairs={{0,56},{8,0},{16,8},{24,16},{32,24},{40,32},{48,40},{56,48},{1,57}... | collective-permute-start | bytes 466952 | tf_op jit(solution)/shard_map/ppermute | solution.py:30
  52.4 1.5 %collective-permute-start.13 = (bf16[152,512]{1,0:T(8,128)(2,1)S(1)}, bf16[152,512]{1,0:T(8,128)(2,1)S(1)}, u32[]{:S(2)}, u32[]{:S(2)}) collective-permute-start(bf16[152,512]{1,0:T(8,128)(2,1)S(1)} %collective-permute-done.9.refs_9_), channel_id=1, source_target_pairs={{0,8},{8,16},{16,24},{24,32},{32,40},{40,48},{48,56},{56,0},{1,9},... | collective-permute-start | bytes 466952 | tf_op jit(solution)/shard_map/ppermute | solution.py:30
  55.0 2.0 %collective-permute-done.11.refs_11_ = bf16[152,512]{1,0:T(8,128)(2,1)S(1)} collective-permute-done((bf16[152,512]{1,0:T(8,128)(2,1)S(1)}, bf16[152,512]{1,0:T(8,128)(2,1)S(1)}, u32[]{:S(2)}, u32[]{:S(2)}) %collective-permute-start.11) | collective-permute-done | bytes 155680 | tf_op jit(solution)/shard_map/ppermute | solution.py:30
  57.0 1.3 %collective-permute-start.15 = (bf16[152,512]{1,0:T(8,128)(2,1)S(1)}, bf16[152,512]{1,0:T(8,128)(2,1)S(1)}, u32[]{:S(2)}, u32[]{:S(2)}) collective-permute-start(bf16[152,512]{1,0:T(8,128)(2,1)S(1)} %collective-permute-done.11.refs_11_), channel_id=1, source_target_pairs={{0,56},{8,0},{16,8},{24,16},{32,24},{40,32},{48,40},{56,48},{1,57}... | collective-permute-start | bytes 466952 | tf_op jit(solution)/shard_map/ppermute | solution.py:30
  59.1 2.4 %collective-permute-done.14.refs_14_ = bf16[152,512]{1,0:T(8,128)(2,1)S(1)} collective-permute-done((bf16[152,512]{1,0:T(8,128)(2,1)S(1)}, bf16[152,512]{1,0:T(8,128)(2,1)S(1)}, u32[]{:S(2)}, u32[]{:S(2)}) %collective-permute-start.14) | collective-permute-done | bytes 155680 | tf_op jit(solution)/shard_map/ppermute | solution.py:30
  62.3 1.5 %copy-done = bf16[384,2560]{1,0:T(8,128)(2,1)S(1)} copy-done((bf16[384,2560]{1,0:T(8,128)(2,1)S(1)}, bf16[384,2560]{1,0:T(8,128)(2,1)}, u32[]{:S(2)}) %copy-start) | copy-done | bytes 1966104
  63.8 2.0 %shard_map.85 = (bf16[1120,128]{1,0:T(8,128)(2,1)S(1)}, bf16[384,192]{1,0:T(8,128)(2,1)S(1)}) custom-call(f32[2,1216]{1,0:T(2,128)S(1)} %bitcast.10, bf16[384,2560]{1,0:T(8,128)(2,1)S(1)} %copy-done, bf16[64,320]{1,0:T(8,128)(2,1)S(1)} %get-tuple-element.17.text_ref, bf16[152,512]{1,0:T(8,128)(2,1)S(1)} %get-tuple-element.18.refs_0_.after_ref, ...), custom_call_target="tpu_custom_call" | custom-call | flops 1006632960 | bytes 4507136 | tf_op jit(solution)/shard_map/pallas_call | solution.py:309
  66.2 7.7 %collective-permute-done.18.far = bf16[1120,128]{1,0:T(8,128)(2,1)S(1)} collective-permute-done((bf16[1120,128]{1,0:T(8,128)(2,1)S(1)}, bf16[1120,128]{1,0:T(8,128)(2,1)S(1)}, u32[]{:S(2)}, u32[]{:S(2)}) %collective-permute-start.18) | collective-permute-done | bytes 286752 | tf_op jit(solution)/shard_map/ppermute | solution.py:30
  74.4 1.4 %collective-permute-done.17.beside_q = bf16[384,192]{1,0:T(8,128)(2,1)S(1)} collective-permute-done((bf16[384,192]{1,0:T(8,128)(2,1)S(1)}, bf16[384,192]{1,0:T(8,128)(2,1)S(1)}, u32[]{:S(2)}, u32[]{:S(2)}) %collective-permute-start.17) | collective-permute-done | bytes 147488 | tf_op jit(solution)/shard_map/ppermute | solution.py:30
  75.8 3.1 %shard_map.86.a0 = bf16[480,128]{1,0:T(8,128)(2,1)S(1)} custom-call(s32[8]{0:T(128)S(1)} %copy-done.5, bf16[1120,128]{1,0:T(8,128)(2,1)S(1)} %get-tuple-element.19.own, bf16[1120,128]{1,0:T(8,128)(2,1)S(1)} %collective-permute-done.16.beside, bf16[384,192]{1,0:T(8,128)(2,1)S(1)} %get-tuple-element.20.own_q, ...), custom_call_target="tpu_custom_call" | custom-call | flops 220200960 | bytes 1441824 | tf_op jit(solution)/shard_map/pallas_call | solution.py:309
  79.5 1.7 %collective-permute-start.21 = (bf16[480,128]{1,0:T(8,128)(2,1)S(1)}, bf16[480,128]{1,0:T(8,128)(2,1)S(1)}, u32[]{:S(2)}, u32[]{:S(2)}) collective-permute-start(bf16[480,128]{1,0:T(8,128)(2,1)S(1)} %shard_map.86.a0), channel_id=1, source_target_pairs={{0,4},{2,6},{4,0},{6,2},{1,5},{3,7},{5,1},{7,3},{8,12},{10,14},{12... | collective-permute-start | bytes 368648 | tf_op jit(solution)/shard_map/ppermute | solution.py:30
  82.2 7.3 %all-gather.5.cloned.1.call-done.gathered_ref = bf16[640,1216]{1,0:T(8,128)(2,1)} async-done(((bf16[40,1216]{1,0:T(8,128)(2,1)}), bf16[640,1216]{1,0:T(8,128)(2,1)}) %all-gather.5.cloned.1.call-update) | async-done | bytes 1556496 | tf_op jit(solution)/shard_map/all_gather | solution.py:386
  89.5 1.4 %copy-done.6 = bf16[640,1216]{1,0:T(8,128)(2,1)S(1)} copy-done((bf16[640,1216]{1,0:T(8,128)(2,1)S(1)}, bf16[640,1216]{1,0:T(8,128)(2,1)}, u32[]{:S(2)}) %copy-start.6) | copy-done | bytes 1556504
  92.5 1.5 %collective-permute-start.24 = (bf16[48,608]{1,0:T(8,128)(2,1)S(1)}, bf16[48,608]{1,0:T(8,128)(2,1)S(1)}, u32[]{:S(2)}, u32[]{:S(2)}) collective-permute-start(bf16[48,608]{1,0:T(8,128)(2,1)S(1)} %get-tuple-element.22), channel_id=1, source_target_pairs={{0,2},{2,4},{4,6},{6,0},{1,3},{3,5},{5,7},{7,1},{8,10},{10,12},{12... | collective-permute-start | bytes 175112 | tf_op jit(solution)/shard_map/ppermute | solution.py:30
  94.0 2.8 %collective-permute-start.25 = (bf16[48,608]{1,0:T(8,128)(2,1)S(1)}, bf16[48,608]{1,0:T(8,128)(2,1)S(1)}, u32[]{:S(2)}, u32[]{:S(2)}) collective-permute-start(bf16[48,608]{1,0:T(8,128)(2,1)S(1)} %get-tuple-element.23), channel_id=1, source_target_pairs={{0,4},{2,6},{4,0},{6,2},{1,5},{3,7},{5,1},{7,3},{8,12},{10,14},{12... | collective-permute-start | bytes 175112 | tf_op jit(solution)/shard_map/ppermute | solution.py:30
  96.8 1.2 %collective-permute-start.26 = (bf16[48,608]{1,0:T(8,128)(2,1)S(1)}, bf16[48,608]{1,0:T(8,128)(2,1)S(1)}, u32[]{:S(2)}, u32[]{:S(2)}) collective-permute-start(bf16[48,608]{1,0:T(8,128)(2,1)S(1)} %get-tuple-element.24), channel_id=1, source_target_pairs={{0,6},{2,0},{4,2},{6,4},{1,7},{3,1},{5,3},{7,5},{8,14},{10,8},{12,... | collective-permute-start | bytes 175112 | tf_op jit(solution)/shard_map/ppermute | solution.py:30
  98.0 2.3 %collective-permute-done.25.n2 = bf16[48,608]{1,0:T(8,128)(2,1)S(1)} collective-permute-done((bf16[48,608]{1,0:T(8,128)(2,1)S(1)}, bf16[48,608]{1,0:T(8,128)(2,1)S(1)}, u32[]{:S(2)}, u32[]{:S(2)}) %collective-permute-start.25) | collective-permute-done | bytes 58400 | tf_op jit(solution)/shard_map/ppermute | solution.py:30
  101.1 1.3 %shard_map.91 = bf16[48,2432]{1,0:T(8,128)(2,1)} custom-call(f32[3,1,2432]{2,1,0:T(1,128)S(1)} %copy-done.3, bf16[48,2432]{1,0:T(8,128)(2,1)S(1)} %collective-permute-done.raw_ref, bf16[48,608]{1,0:T(8,128)(2,1)S(1)} %get-tuple-element.21.n0, bf16[48,608]{1,0:T(8,128)(2,1)S(1)} %collective-permute-done.24.n1, ...), custom_call_target="tpu_custom_call" | custom-call | bytes 496128 | tf_op jit(solution)/shard_map/pallas_call | solution.py:309
  (54 shorter events, 12.9 us)
Async XLA Ops:
  6.5 9.1 %collective-permute-start = (bf16[48,2432]{1,0:T(8,128)(2,1)}, bf16[48,2432]{1,0:T(8,128)(2,1)S(1)}, u32[]{:S(2)}, u32[]{:S(2)}) collective-permute-start(bf16[48,2432]{1,0:T(8,128)(2,1)} %bitcast.13), channel_id=1, source_target_pairs={{0,128},{128,0},{1,129},{129,1},{2,130},{130,2},{3,131},{131,3},{4... | collective-permute-start | bytes 700424 | tf_op jit(solution)/shard_map/ppermute | solution.py:30
  11.1 11.3 %all-to-all-start = ((bf16[8,24,512]{2,1,0:T(8,128)(2,1)}), bf16[8,24,512]{2,1,0:T(8,128)(2,1)S(1)}, u32[]{:S(2)}, u32[]{:S(2)}) async-start(bf16[8,24,512]{2,1,0:T(8,128)(2,1)} %get-tuple-element.16), calls=%async_computation | async-start | bytes 393216 | tf_op jit(solution)/shard_map/all_to_all | solution.py:341
  15.5 46.7 %all-gather.3.cloned.1.call-start = ((), (), s32[]{:S(2)}) async-start(), calls=%async_computation.1 | async-start | bytes 2211840 | tf_op jit(solution)/shard_map/all_gather | solution.py:359
  17.6 20.6 %copy-start.1 = (bf16[1,1216,19]{1,2,0:T(8,128)(2,1)S(1)}, bf16[1,1216,19]{1,2,0:T(8,128)(2,1)}, u32[]{:S(2)}) copy-start(bf16[1,1216,19]{1,2,0:T(8,128)(2,1)} %param.14) | copy-start | bytes 138628
  17.6 44.7 %copy-start.4 = (f32[1,2,1216]{2,1,0:T(2,128)S(1)}, f32[1,2,1216]{2,1,0:T(2,128)}, u32[]{:S(2)}) copy-start(f32[1,2,1216]{2,1,0:T(2,128)} %param.15) | copy-start | bytes 29188
  17.6 71.9 %all-gather.5.cloned.1.call-start = ((), (), s32[]{:S(2)}) async-start(), calls=%async_computation.2 | async-start | bytes 1740800 | tf_op jit(solution)/shard_map/all_gather | solution.py:386
  23.5 7.4 %collective-permute-start.1 = (bf16[152,512]{1,0:T(8,128)(2,1)S(1)}, bf16[152,512]{1,0:T(8,128)(2,1)S(1)}, u32[]{:S(2)}, u32[]{:S(2)}) collective-permute-start(bf16[152,512]{1,0:T(8,128)(2,1)S(1)} %get-tuple-element.18.refs_0_.after_ref), channel_id=1, source_target_pairs={{0,64},{64,0},{1,65},{65,1},{2,66},{66,2},{3,67},{67,3},{4,68},{68... | collective-permute-start | bytes 466952 | tf_op jit(solution)/shard_map/ppermute | solution.py:30
  25.0 9.9 %collective-permute-start.2 = (bf16[152,512]{1,0:T(8,128)(2,1)S(1)}, bf16[152,512]{1,0:T(8,128)(2,1)S(1)}, u32[]{:S(2)}, u32[]{:S(2)}) collective-permute-start(bf16[152,512]{1,0:T(8,128)(2,1)S(1)} %get-tuple-element.18.refs_0_.after_ref), channel_id=1, source_target_pairs={{0,8},{8,16},{16,24},{24,32},{32,40},{40,48},{48,56},{56,0},{1,9},... | collective-permute-start | bytes 466952 | tf_op jit(solution)/shard_map/ppermute | solution.py:30
  26.9 8.0 %collective-permute-start.4 = (bf16[152,512]{1,0:T(8,128)(2,1)S(1)}, bf16[152,512]{1,0:T(8,128)(2,1)S(1)}, u32[]{:S(2)}, u32[]{:S(2)}) collective-permute-start(bf16[152,512]{1,0:T(8,128)(2,1)S(1)} %get-tuple-element.18.refs_0_.after_ref), channel_id=1, source_target_pairs={{0,56},{8,0},{16,8},{24,16},{32,24},{40,32},{48,40},{56,48},{1,57}... | collective-permute-start | bytes 466952 | tf_op jit(solution)/shard_map/ppermute | solution.py:30
  30.8 11.7 %collective-permute-start.3 = (bf16[152,512]{1,0:T(8,128)(2,1)S(1)}, bf16[152,512]{1,0:T(8,128)(2,1)S(1)}, u32[]{:S(2)}, u32[]{:S(2)}) collective-permute-start(bf16[152,512]{1,0:T(8,128)(2,1)S(1)} %collective-permute-done.1.refs_1_), channel_id=1, source_target_pairs={{0,56},{8,0},{16,8},{24,16},{32,24},{40,32},{48,40},{56,48},{1,57}... | collective-permute-start | bytes 466952 | tf_op jit(solution)/shard_map/ppermute | solution.py:30
  34.9 7.7 %collective-permute-start.5 = (bf16[152,512]{1,0:T(8,128)(2,1)S(1)}, bf16[152,512]{1,0:T(8,128)(2,1)S(1)}, u32[]{:S(2)}, u32[]{:S(2)}) collective-permute-start(bf16[152,512]{1,0:T(8,128)(2,1)S(1)} %collective-permute-done.1.refs_1_), channel_id=1, source_target_pairs={{0,8},{8,16},{16,24},{24,32},{32,40},{40,48},{48,56},{56,0},{1,9},... | collective-permute-start | bytes 466952 | tf_op jit(solution)/shard_map/ppermute | solution.py:30
  34.9 8.8 %collective-permute-start.6 = (bf16[152,512]{1,0:T(8,128)(2,1)S(1)}, bf16[152,512]{1,0:T(8,128)(2,1)S(1)}, u32[]{:S(2)}, u32[]{:S(2)}) collective-permute-start(bf16[152,512]{1,0:T(8,128)(2,1)S(1)} %collective-permute-done.2.refs_2_), channel_id=1, source_target_pairs={{0,8},{8,16},{16,24},{24,32},{32,40},{40,48},{48,56},{56,0},{1,9},... | collective-permute-start | bytes 466952 | tf_op jit(solution)/shard_map/ppermute | solution.py:30
  34.9 8.8 %collective-permute-start.8 = (bf16[152,512]{1,0:T(8,128)(2,1)S(1)}, bf16[152,512]{1,0:T(8,128)(2,1)S(1)}, u32[]{:S(2)}, u32[]{:S(2)}) collective-permute-start(bf16[152,512]{1,0:T(8,128)(2,1)S(1)} %collective-permute-done.4.refs_4_), channel_id=1, source_target_pairs={{0,56},{8,0},{16,8},{24,16},{32,24},{40,32},{48,40},{56,48},{1,57}... | collective-permute-start | bytes 466952 | tf_op jit(solution)/shard_map/ppermute | solution.py:30
  38.2 4.3 %collective-permute-start.23 = (bf16[19,1216]{1,0:T(8,128)(2,1)S(1)}, bf16[19,1216]{1,0:T(8,128)(2,1)S(1)}, u32[]{:S(2)}, u32[]{:S(2)}) collective-permute-start(bf16[19,1216]{1,0:T(8,128)(2,1)S(1)} %shard_map.87), channel_id=1, source_target_pairs={{0,64},{64,0},{1,65},{65,1},{2,66},{66,2},{3,67},{67,3},{4,68},{68... | collective-permute-start | bytes 138632 | tf_op jit(solution)/shard_map/ppermute | solution.py:30
  44.4 5.9 %collective-permute-start.7 = (bf16[152,512]{1,0:T(8,128)(2,1)S(1)}, bf16[152,512]{1,0:T(8,128)(2,1)S(1)}, u32[]{:S(2)}, u32[]{:S(2)}) collective-permute-start(bf16[152,512]{1,0:T(8,128)(2,1)S(1)} %collective-permute-done.3.refs_3_), channel_id=1, source_target_pairs={{0,56},{8,0},{16,8},{24,16},{32,24},{40,32},{48,40},{56,48},{1,57}... | collective-permute-start | bytes 466952 | tf_op jit(solution)/shard_map/ppermute | solution.py:30
  45.5 7.0 %collective-permute-start.9 = (bf16[152,512]{1,0:T(8,128)(2,1)S(1)}, bf16[152,512]{1,0:T(8,128)(2,1)S(1)}, u32[]{:S(2)}, u32[]{:S(2)}) collective-permute-start(bf16[152,512]{1,0:T(8,128)(2,1)S(1)} %collective-permute-done.5.refs_5_.refs_2_), channel_id=1, source_target_pairs={{0,8},{8,16},{16,24},{24,32},{32,40},{40,48},{48,56},{56,0},{1,9},... | collective-permute-start | bytes 466952 | tf_op jit(solution)/shard_map/ppermute | solution.py:30
  46.5 8.5 %collective-permute-start.10 = (bf16[152,512]{1,0:T(8,128)(2,1)S(1)}, bf16[152,512]{1,0:T(8,128)(2,1)S(1)}, u32[]{:S(2)}, u32[]{:S(2)}) collective-permute-start(bf16[152,512]{1,0:T(8,128)(2,1)S(1)} %collective-permute-done.6.refs_6_.refs_0_), channel_id=1, source_target_pairs={{0,8},{8,16},{16,24},{24,32},{32,40},{40,48},{48,56},{56,0},{1,9},... | collective-permute-start | bytes 466952 | tf_op jit(solution)/shard_map/ppermute | solution.py:30
  50.4 6.7 %collective-permute-start.11 = (bf16[152,512]{1,0:T(8,128)(2,1)S(1)}, bf16[152,512]{1,0:T(8,128)(2,1)S(1)}, u32[]{:S(2)}, u32[]{:S(2)}) collective-permute-start(bf16[152,512]{1,0:T(8,128)(2,1)S(1)} %collective-permute-done.7.refs_7_), channel_id=1, source_target_pairs={{0,56},{8,0},{16,8},{24,16},{32,24},{40,32},{48,40},{56,48},{1,57}... | collective-permute-start | bytes 466952 | tf_op jit(solution)/shard_map/ppermute | solution.py:30
  51.9 7.0 %collective-permute-start.12 = (bf16[152,512]{1,0:T(8,128)(2,1)S(1)}, bf16[152,512]{1,0:T(8,128)(2,1)S(1)}, u32[]{:S(2)}, u32[]{:S(2)}) collective-permute-start(bf16[152,512]{1,0:T(8,128)(2,1)S(1)} %collective-permute-done.8.refs_8_.refs_1_), channel_id=1, source_target_pairs={{0,56},{8,0},{16,8},{24,16},{32,24},{40,32},{48,40},{56,48},{1,57}... | collective-permute-start | bytes 466952 | tf_op jit(solution)/shard_map/ppermute | solution.py:30
  52.4 6.7 %collective-permute-start.13 = (bf16[152,512]{1,0:T(8,128)(2,1)S(1)}, bf16[152,512]{1,0:T(8,128)(2,1)S(1)}, u32[]{:S(2)}, u32[]{:S(2)}) collective-permute-start(bf16[152,512]{1,0:T(8,128)(2,1)S(1)} %collective-permute-done.9.refs_9_), channel_id=1, source_target_pairs={{0,8},{8,16},{16,24},{24,32},{32,40},{40,48},{48,56},{56,0},{1,9},... | collective-permute-start | bytes 466952 | tf_op jit(solution)/shard_map/ppermute | solution.py:30
  55.0 6.4 %collective-permute-start.14 = (bf16[152,512]{1,0:T(8,128)(2,1)S(1)}, bf16[152,512]{1,0:T(8,128)(2,1)S(1)}, u32[]{:S(2)}, u32[]{:S(2)}) collective-permute-start(bf16[152,512]{1,0:T(8,128)(2,1)S(1)} %collective-permute-done.10.refs_10_), channel_id=1, source_target_pairs={{0,8},{8,16},{16,24},{24,32},{32,40},{40,48},{48,56},{56,0},{1,9},... | collective-permute-start | bytes 466952 | tf_op jit(solution)/shard_map/ppermute | solution.py:30
  57.0 5.2 %collective-permute-start.15 = (bf16[152,512]{1,0:T(8,128)(2,1)S(1)}, bf16[152,512]{1,0:T(8,128)(2,1)S(1)}, u32[]{:S(2)}, u32[]{:S(2)}) collective-permute-start(bf16[152,512]{1,0:T(8,128)(2,1)S(1)} %collective-permute-done.11.refs_11_), channel_id=1, source_target_pairs={{0,56},{8,0},{16,8},{24,16},{32,24},{40,32},{48,40},{56,48},{1,57}... | collective-permute-start | bytes 466952 | tf_op jit(solution)/shard_map/ppermute | solution.py:30
  65.8 8.1 %collective-permute-start.18 = (bf16[1120,128]{1,0:T(8,128)(2,1)S(1)}, bf16[1120,128]{1,0:T(8,128)(2,1)S(1)}, u32[]{:S(2)}, u32[]{:S(2)}) collective-permute-start(bf16[1120,128]{1,0:T(8,128)(2,1)S(1)} %get-tuple-element.19.own), channel_id=1, source_target_pairs={{0,8},{8,0},{1,9},{9,1},{2,10},{10,2},{3,11},{11,3},{4,12},{12,4},... | collective-permute-start | bytes 860168 | tf_op jit(solution)/shard_map/ppermute | solution.py:30
  66.2 9.6 %collective-permute-start.16 = (bf16[1120,128]{1,0:T(8,128)(2,1)S(1)}, bf16[1120,128]{1,0:T(8,128)(2,1)S(1)}, u32[]{:S(2)}, u32[]{:S(2)}) collective-permute-start(bf16[1120,128]{1,0:T(8,128)(2,1)S(1)} %get-tuple-element.19.own), channel_id=1, source_target_pairs={{0,1},{1,0},{2,3},{3,2},{4,5},{5,4},{6,7},{7,6},{8,9},{9,8},{10,11... | collective-permute-start | bytes 860168 | tf_op jit(solution)/shard_map/ppermute | solution.py:30
  73.9 1.9 %collective-permute-start.19 = (bf16[1120,128]{1,0:T(8,128)(2,1)S(1)}, bf16[1120,128]{1,0:T(8,128)(2,1)S(1)}, u32[]{:S(2)}, u32[]{:S(2)}) collective-permute-start(bf16[1120,128]{1,0:T(8,128)(2,1)S(1)} %collective-permute-done.18.far), channel_id=1, source_target_pairs={{0,1},{1,0},{2,3},{3,2},{4,5},{5,4},{6,7},{7,6},{8,9},{9,8},{10,11... | collective-permute-start | bytes 860168 | tf_op jit(solution)/shard_map/ppermute | solution.py:30
  73.9 1.9 %collective-permute-start.17 = (bf16[384,192]{1,0:T(8,128)(2,1)S(1)}, bf16[384,192]{1,0:T(8,128)(2,1)S(1)}, u32[]{:S(2)}, u32[]{:S(2)}) collective-permute-start(bf16[384,192]{1,0:T(8,128)(2,1)S(1)} %get-tuple-element.20.own_q), channel_id=1, source_target_pairs={{0,1},{1,0},{2,3},{3,2},{4,5},{5,4},{6,7},{7,6},{8,9},{9,8},{10,11... | collective-permute-start | bytes 442376 | tf_op jit(solution)/shard_map/ppermute | solution.py:30
  78.9 12.6 %collective-permute-start.20 = (bf16[480,128]{1,0:T(8,128)(2,1)S(1)}, bf16[480,128]{1,0:T(8,128)(2,1)S(1)}, u32[]{:S(2)}, u32[]{:S(2)}) collective-permute-start(bf16[480,128]{1,0:T(8,128)(2,1)S(1)} %shard_map.86.a0), channel_id=1, source_target_pairs={{0,2},{2,4},{4,6},{6,0},{1,3},{3,5},{5,7},{7,1},{8,10},{10,12},{12... | collective-permute-start | bytes 368648 | tf_op jit(solution)/shard_map/ppermute | solution.py:30
  79.5 12.0 %collective-permute-start.21 = (bf16[480,128]{1,0:T(8,128)(2,1)S(1)}, bf16[480,128]{1,0:T(8,128)(2,1)S(1)}, u32[]{:S(2)}, u32[]{:S(2)}) collective-permute-start(bf16[480,128]{1,0:T(8,128)(2,1)S(1)} %shard_map.86.a0), channel_id=1, source_target_pairs={{0,4},{2,6},{4,0},{6,2},{1,5},{3,7},{5,1},{7,3},{8,12},{10,14},{12... | collective-permute-start | bytes 368648 | tf_op jit(solution)/shard_map/ppermute | solution.py:30
  81.2 10.3 %collective-permute-start.22 = (bf16[480,128]{1,0:T(8,128)(2,1)S(1)}, bf16[480,128]{1,0:T(8,128)(2,1)S(1)}, u32[]{:S(2)}, u32[]{:S(2)}) collective-permute-start(bf16[480,128]{1,0:T(8,128)(2,1)S(1)} %shard_map.86.a0), channel_id=1, source_target_pairs={{0,6},{2,0},{4,2},{6,4},{1,7},{3,1},{5,3},{7,5},{8,14},{10,8},{12,... | collective-permute-start | bytes 368648 | tf_op jit(solution)/shard_map/ppermute | solution.py:30
  92.5 5.6 %collective-permute-start.24 = (bf16[48,608]{1,0:T(8,128)(2,1)S(1)}, bf16[48,608]{1,0:T(8,128)(2,1)S(1)}, u32[]{:S(2)}, u32[]{:S(2)}) collective-permute-start(bf16[48,608]{1,0:T(8,128)(2,1)S(1)} %get-tuple-element.22), channel_id=1, source_target_pairs={{0,2},{2,4},{4,6},{6,0},{1,3},{3,5},{5,7},{7,1},{8,10},{10,12},{12... | collective-permute-start | bytes 175112 | tf_op jit(solution)/shard_map/ppermute | solution.py:30
  94.0 6.3 %collective-permute-start.25 = (bf16[48,608]{1,0:T(8,128)(2,1)S(1)}, bf16[48,608]{1,0:T(8,128)(2,1)S(1)}, u32[]{:S(2)}, u32[]{:S(2)}) collective-permute-start(bf16[48,608]{1,0:T(8,128)(2,1)S(1)} %get-tuple-element.23), channel_id=1, source_target_pairs={{0,4},{2,6},{4,0},{6,2},{1,5},{3,7},{5,1},{7,3},{8,12},{10,14},{12... | collective-permute-start | bytes 175112 | tf_op jit(solution)/shard_map/ppermute | solution.py:30
  96.8 4.2 %collective-permute-start.26 = (bf16[48,608]{1,0:T(8,128)(2,1)S(1)}, bf16[48,608]{1,0:T(8,128)(2,1)S(1)}, u32[]{:S(2)}, u32[]{:S(2)}) collective-permute-start(bf16[48,608]{1,0:T(8,128)(2,1)S(1)} %get-tuple-element.24), channel_id=1, source_target_pairs={{0,6},{2,0},{4,2},{6,4},{1,7},{3,1},{5,3},{7,5},{8,14},{10,8},{12,... | collective-permute-start | bytes 175112 | tf_op jit(solution)/shard_map/ppermute | solution.py:30
  (5 other events, 25.4 us)
Sparse Core Ops, SparseCore 0:
  18.2 29.9 all-gather.2
  50.0 39.4 all-gather.4

commit v5 on v4

--- a/solution.py
+++ b/solution.py
@@ -102,14 +102,20 @@
 
 
 def modulate_kernel(modulation, raw_ref, h_ref):
-    wide = raw_ref[...].astype(F32)
-    centred = wide - jnp.mean(wide, axis=-1, keepdims=True)
-    normed = centred * lax.rsqrt(jnp.mean(centred * centred, axis=-1, keepdims=True) + EPSILON)
-    modulated = normed * (1.0 + modulation[1]) + modulation[0]
-    modulated = modulated.astype(BF16)
     h_ref[...] = jnp.zeros_like(h_ref)
-    for slot in range(16):
-        h_ref[:, slot * SLOT : slot * SLOT + CHUNK] = modulated[:, slot * CHUNK : (slot + 1) * CHUNK]
+    rows = raw_ref.shape[0] // 8
+    for part in range(8):
+        at = slice(part * rows, (part + 1) * rows)
+        wide = raw_ref[at, :].astype(F32)
+        centred = wide - jnp.mean(wide, axis=-1, keepdims=True)
+        square = jnp.mean(centred * centred, axis=-1, keepdims=True)
+        normed = centred * lax.rsqrt(square + EPSILON)
+        modulated = normed * (1.0 + modulation[1]) + modulation[0]
+        modulated = modulated.astype(BF16)
+        for slot in range(16):
+            h_ref[at, slot * SLOT : slot * SLOT + CHUNK] = modulated[
+                :, slot * CHUNK : (slot + 1) * CHUNK
+            ]
 
 
 def places_of_blocks():
@@ -287,19 +293,27 @@
         out_ref[...] = result[lax.rem(y + by, 4)]
 
 
-def assemble_kernel(modulation, raw_ref, n0, n1, n2, n3, out_ref, branch):
+def place_columns(part, by, branch):
     y = lax.axis_index("y")
-    run = n0.shape[1] // 16
-    for by, part in enumerate((n0, n1, n2, n3)):
-        value = part[...].astype(F32)
-        for q in range(4):
-
-            @pl.when(lax.rem(y + 4 - by, 4) == q)
-            def _():
-                for m in range(16):
-                    at = (m * 4 + q) * run
-                    branch[:, at : at + run] = value[:, m * run : (m + 1) * run]
-
+    run = part.shape[1] // 16
+    value = part[...].astype(F32)
+    for q in range(4):
+
+        @pl.when(lax.rem(y + 4 - by, 4) == q)
+        def _():
+            for m in range(16):
+                at = (m * 4 + q) * run
+                branch[:, at : at + run] = value[:, m * run : (m + 1) * run]
+
+
+def assemble_early_kernel(n0, n1, n3, branch):
+    for by, part in ((0, n0), (1, n1), (3, n3)):
+        place_columns(part, by, branch)
+
+
+def assemble_kernel(modulation, raw_ref, early_ref, n2, out_ref, branch):
+    branch[...] = early_ref[...]
+    place_columns(n2, 2, branch)
     out_ref[...] = (raw_ref[...].astype(F32) + modulation[2] * branch[...]).astype(BF16)
 
 
@@ -342,9 +356,6 @@
     shard = jnp.transpose(out_weight[0])
 
     raw = permuted(stale_states[0], "comp", 1)
-    h = in_vmem(
-        modulate_kernel, jax.ShapeDtypeStruct((rows, 16 * SLOT), BF16), (modulation, raw)
-    )
     block, text = in_vmem(
         compact_kernel,
         (
@@ -352,11 +363,16 @@
             jax.ShapeDtypeStruct((8 * TEXT_ROWS, YW), BF16),
         ),
         (received,),
-        flops=7 * 10**10,
+        flops=35 * 10**9,
         scratch=[pltpu.VMEM((CHUNK, HALF), F32), pltpu.VMEM((8 * TEXT_ROWS, YW), F32)],
-        after=(h,),
-    )
-    h = lax.all_gather(h, ("y", "core"), axis=0, tiled=True)
+        after=(raw,),
+    )
+    h = in_vmem(
+        modulate_kernel,
+        jax.ShapeDtypeStruct((8 * rows, 16 * SLOT), BF16),
+        (modulation, lax.all_gather(raw, ("y", "core"), axis=0, tiled=True)),
+        flops=2 * 10**10,
+    )
 
     ahead = lambda part: permuted(part, Z, 1)
     behind = lambda part: permuted(part, Z, 7)
@@ -439,10 +455,16 @@
         ],
     )
     parts = [parts[0]] + [permuted(parts[by], "y", by) for by in (1, 2, 3)]
+    early = in_vmem(
+        assemble_early_kernel,
+        jax.ShapeDtypeStruct((rows, width), F32),
+        (parts[0], parts[1], parts[3]),
+        flops=10**10,
+    )
     new = in_vmem(
         assemble_kernel,
         jax.ShapeDtypeStruct((rows, width), BF16),
-        (modulation, raw, *parts),
+        (modulation, raw, early, parts[2]),
         scratch=[pltpu.VMEM((rows, width), F32)],
     )
     return new[None]

time: 110 us -> 109 us (level)
  waiting for transfers between devices: 39.5 us -> 36.6 us
    ppermute x27, waiting for transfers between devices: 27.5 us -> 22.9 us  [permuted(): lax.ppermute(array, axis, [(i, (i + by) % devices) for i in range(devices)])]
    all_to_all x1, waiting for transfers between devices: 4.72 us -> 5.95 us  [per_device(): lax.all_to_all(halves, ('y', 'core'), split_axis=0, concat_axis=0, tiled=...]
    unnamed x14 -> x18, local copies, waits for them, and re-layouts: 3.75 us -> 4.59 us
    pallas_call x10 -> x11, Pallas kernels: 13.2 us -> 13.8 us  [in_vmem(): pl.pallas_call(kernel, out_shape=out_shape, in_specs=[pl.BlockSpec(memory...]
  transfers between devices with their start and end apart: 30 -> 30, of which waited for: 17 -> 14; matrix products, arithmetic and copies ran while one was open for 0% -> 0% of each run, Pallas kernels for 10% -> 11%
where the time goes in v5:
time: 109 us
  starting transfers between devices  40.2 us (37%)
  waiting for transfers between devices  36.6 us (34%)
  Pallas kernels  13.8 us (13%)
  between operations  13.6 us (12%)
  local copies, waits for them, and re-layouts  4.59 us (4%)
    ppermute x27, starting transfers between devices, permuted(): lax.ppermute(array, axis, [(i, (i + by) % devices) for i in range(devices)])  35.6 us
    ppermute x27, waiting for transfers between devices, permuted(): lax.ppermute(array, axis, [(i, (i + by) % devices) for i in range(devices)])  22.9 us
    pallas_call x11, Pallas kernels, in_vmem(): pl.pallas_call(kernel, out_shape=out_shape, in_specs=[pl.BlockSpec(memory...  13.8 us
    all_gather x1, waiting for transfers between devices, per_device(): out_columns = lax.all_gather(both, ('core', 'z1', 'z0'), axis=0, tiled=True)  7.73 us
    all_to_all x1, waiting for transfers between devices, per_device(): lax.all_to_all(halves, ('y', 'core'), split_axis=0, concat_axis=0, tiled=...  5.95 us
    unnamed x18, local copies, waits for them, and re-layouts  4.59 us
    all_to_all x1, starting transfers between devices, per_device(): lax.all_to_all(halves, ('y', 'core'), split_axis=0, concat_axis=0, tiled=...  4.48 us
  transfers between devices with their start and end apart: 30, of which 14 were waited for; matrix products, arithmetic and copies ran while one was open for 0% of the time, Pallas kernels for 11%

profile of v5, /device:TPU:2, one launch (start us, length us, event | category | flops | bytes accessed | tf_op | source)
XLA Modules:
  0.0 108.8 jit_solution(14809548801463529579)
XLA Ops:
  6.5 2.1 %collective-permute-start = (bf16[48,2432]{1,0:T(8,128)(2,1)}, bf16[48,2432]{1,0:T(8,128)(2,1)S(1)}, u32[]{:S(2)}, u32[]{:S(2)}) collective-permute-start(bf16[48,2432]{1,0:T(8,128)(2,1)} %bitcast.13), channel_id=1, source_target_pairs={{0,128},{128,0},{1,129},{129,1},{2,130},{130,2},{3,131},{131,3},{4... | collective-permute-start | bytes 700424 | tf_op jit(solution)/shard_map/ppermute | solution.py:30
  8.7 2.4 %shard_map.82 = (bf16[8,24,512]{2,1,0:T(8,128)(2,1)}, f32[3,1,2432]{2,1,0:T(1,128)}) custom-call(s32[8]{0:T(128)} %steps_ref.1, bf16[19,3648]{1,0:T(8,128)(2,1)} %bitcast.12, bf16[2,8,1216]{2,1,0:T(8,128)(2,1)} %text_ref.1, f32[28,3,1,2432]{3,2,1,0:T(1,128)} %bitcast.11), custom_call_target="tpu_custom_call" | custom-call | bytes 177568 | tf_op jit(solution)/shard_map/pallas_call | solution.py:323
  11.1 4.5 %all-to-all-start = ((bf16[8,24,512]{2,1,0:T(8,128)(2,1)}), bf16[8,24,512]{2,1,0:T(8,128)(2,1)S(1)}, u32[]{:S(2)}, u32[]{:S(2)}) async-start(bf16[8,24,512]{2,1,0:T(8,128)(2,1)} %get-tuple-element.16), calls=%async_computation | async-start | bytes 393216 | tf_op jit(solution)/shard_map/all_to_all | solution.py:355
  16.4 5.9 %all-to-all-done.received_ref = bf16[8,24,512]{2,1,0:T(8,128)(2,1)S(1)} async-done(((bf16[8,24,512]{2,1,0:T(8,128)(2,1)}), bf16[8,24,512]{2,1,0:T(8,128)(2,1)S(1)}, u32[]{:S(2)}, u32[]{:S(2)}) %all-to-all-start) | async-done | bytes 196640 | tf_op jit(solution)/shard_map/all_to_all | solution.py:355
  23.5 1.5 %collective-permute-start.1 = (bf16[152,512]{1,0:T(8,128)(2,1)S(1)}, bf16[152,512]{1,0:T(8,128)(2,1)S(1)}, u32[]{:S(2)}, u32[]{:S(2)}) collective-permute-start(bf16[152,512]{1,0:T(8,128)(2,1)S(1)} %get-tuple-element.18.refs_0_.after_ref), channel_id=1, source_target_pairs={{0,64},{64,0},{1,65},{65,1},{2,66},{66,2},{3,67},{67,3},{4,68},{68... | collective-permute-start | bytes 466952 | tf_op jit(solution)/shard_map/ppermute | solution.py:30
  25.0 1.9 %collective-permute-start.2 = (bf16[152,512]{1,0:T(8,128)(2,1)S(1)}, bf16[152,512]{1,0:T(8,128)(2,1)S(1)}, u32[]{:S(2)}, u32[]{:S(2)}) collective-permute-start(bf16[152,512]{1,0:T(8,128)(2,1)S(1)} %get-tuple-element.18.refs_0_.after_ref), channel_id=1, source_target_pairs={{0,8},{8,16},{16,24},{24,32},{32,40},{40,48},{48,56},{56,0},{1,9},... | collective-permute-start | bytes 466952 | tf_op jit(solution)/shard_map/ppermute | solution.py:30
  26.9 3.9 %collective-permute-start.4 = (bf16[152,512]{1,0:T(8,128)(2,1)S(1)}, bf16[152,512]{1,0:T(8,128)(2,1)S(1)}, u32[]{:S(2)}, u32[]{:S(2)}) collective-permute-start(bf16[152,512]{1,0:T(8,128)(2,1)S(1)} %get-tuple-element.18.refs_0_.after_ref), channel_id=1, source_target_pairs={{0,56},{8,0},{16,8},{24,16},{32,24},{40,32},{48,40},{56,48},{1,57}... | collective-permute-start | bytes 466952 | tf_op jit(solution)/shard_map/ppermute | solution.py:30
  30.8 4.0 %collective-permute-start.3 = (bf16[152,512]{1,0:T(8,128)(2,1)S(1)}, bf16[152,512]{1,0:T(8,128)(2,1)S(1)}, u32[]{:S(2)}, u32[]{:S(2)}) collective-permute-start(bf16[152,512]{1,0:T(8,128)(2,1)S(1)} %collective-permute-done.1.refs_1_), channel_id=1, source_target_pairs={{0,56},{8,0},{16,8},{24,16},{32,24},{40,32},{48,40},{56,48},{1,57}... | collective-permute-start | bytes 466952 | tf_op jit(solution)/shard_map/ppermute | solution.py:30
  34.9 3.3 %collective-permute-start.8 = (bf16[152,512]{1,0:T(8,128)(2,1)S(1)}, bf16[152,512]{1,0:T(8,128)(2,1)S(1)}, u32[]{:S(2)}, u32[]{:S(2)}) collective-permute-start(bf16[152,512]{1,0:T(8,128)(2,1)S(1)} %collective-permute-done.4.refs_4_), channel_id=1, source_target_pairs={{0,56},{8,0},{16,8},{24,16},{32,24},{40,32},{48,40},{56,48},{1,57}... | collective-permute-start | bytes 466952 | tf_op jit(solution)/shard_map/ppermute | solution.py:30
  38.2 1.5 %collective-permute-start.23 = (bf16[19,1216]{1,0:T(8,128)(2,1)S(1)}, bf16[19,1216]{1,0:T(8,128)(2,1)S(1)}, u32[]{:S(2)}, u32[]{:S(2)}) collective-permute-start(bf16[19,1216]{1,0:T(8,128)(2,1)S(1)} %shard_map.87), channel_id=1, source_target_pairs={{0,64},{64,0},{1,65},{65,1},{2,66},{66,2},{3,67},{67,3},{4,68},{68... | collective-permute-start | bytes 138632 | tf_op jit(solution)/shard_map/ppermute | solution.py:30
  39.8 2.8 %collective-permute-done.23.other_ref = bf16[19,1216]{1,0:T(8,128)(2,1)S(1)} collective-permute-done((bf16[19,1216]{1,0:T(8,128)(2,1)S(1)}, bf16[19,1216]{1,0:T(8,128)(2,1)S(1)}, u32[]{:S(2)}, u32[]{:S(2)}) %collective-permute-start.23) | collective-permute-done | bytes 46240 | tf_op jit(solution)/shard_map/ppermute | solution.py:30
  42.5 1.2 %collective-permute-done.6.refs_6_.refs_0_ = bf16[152,512]{1,0:T(8,128)(2,1)S(1)} collective-permute-done((bf16[152,512]{1,0:T(8,128)(2,1)S(1)}, bf16[152,512]{1,0:T(8,128)(2,1)S(1)}, u32[]{:S(2)}, u32[]{:S(2)}) %collective-permute-start.6) | collective-permute-done | bytes 155680 | tf_op jit(solution)/shard_map/ppermute | solution.py:30
  45.4 1.1 %collective-permute-start.9 = (bf16[152,512]{1,0:T(8,128)(2,1)S(1)}, bf16[152,512]{1,0:T(8,128)(2,1)S(1)}, u32[]{:S(2)}, u32[]{:S(2)}) collective-permute-start(bf16[152,512]{1,0:T(8,128)(2,1)S(1)} %collective-permute-done.5.refs_5_.refs_2_), channel_id=1, source_target_pairs={{0,8},{8,16},{16,24},{24,32},{32,40},{40,48},{48,56},{56,0},{1,9},... | collective-permute-start | bytes 466952 | tf_op jit(solution)/shard_map/ppermute | solution.py:30
  46.6 3.8 %collective-permute-done.7.refs_7_ = bf16[152,512]{1,0:T(8,128)(2,1)S(1)} collective-permute-done((bf16[152,512]{1,0:T(8,128)(2,1)S(1)}, bf16[152,512]{1,0:T(8,128)(2,1)S(1)}, u32[]{:S(2)}, u32[]{:S(2)}) %collective-permute-start.7) | collective-permute-done | bytes 155680 | tf_op jit(solution)/shard_map/ppermute | solution.py:30
  50.3 1.5 %collective-permute-start.11 = (bf16[152,512]{1,0:T(8,128)(2,1)S(1)}, bf16[152,512]{1,0:T(8,128)(2,1)S(1)}, u32[]{:S(2)}, u32[]{:S(2)}) collective-permute-start(bf16[152,512]{1,0:T(8,128)(2,1)S(1)} %collective-permute-done.7.refs_7_), channel_id=1, source_target_pairs={{0,56},{8,0},{16,8},{24,16},{32,24},{40,32},{48,40},{56,48},{1,57}... | collective-permute-start | bytes 466952 | tf_op jit(solution)/shard_map/ppermute | solution.py:30
  52.1 1.8 %collective-permute-start.13 = (bf16[152,512]{1,0:T(8,128)(2,1)S(1)}, bf16[152,512]{1,0:T(8,128)(2,1)S(1)}, u32[]{:S(2)}, u32[]{:S(2)}) collective-permute-start(bf16[152,512]{1,0:T(8,128)(2,1)S(1)} %collective-permute-done.9.refs_9_), channel_id=1, source_target_pairs={{0,8},{8,16},{16,24},{24,32},{32,40},{40,48},{48,56},{56,0},{1,9},... | collective-permute-start | bytes 466952 | tf_op jit(solution)/shard_map/ppermute | solution.py:30
  54.7 2.4 %collective-permute-done.11.refs_11_ = bf16[152,512]{1,0:T(8,128)(2,1)S(1)} collective-permute-done((bf16[152,512]{1,0:T(8,128)(2,1)S(1)}, bf16[152,512]{1,0:T(8,128)(2,1)S(1)}, u32[]{:S(2)}, u32[]{:S(2)}) %collective-permute-start.11) | collective-permute-done | bytes 155680 | tf_op jit(solution)/shard_map/ppermute | solution.py:30
  57.0 1.3 %collective-permute-start.15 = (bf16[152,512]{1,0:T(8,128)(2,1)S(1)}, bf16[152,512]{1,0:T(8,128)(2,1)S(1)}, u32[]{:S(2)}, u32[]{:S(2)}) collective-permute-start(bf16[152,512]{1,0:T(8,128)(2,1)S(1)} %collective-permute-done.11.refs_11_), channel_id=1, source_target_pairs={{0,56},{8,0},{16,8},{24,16},{32,24},{40,32},{48,40},{56,48},{1,57}... | collective-permute-start | bytes 466952 | tf_op jit(solution)/shard_map/ppermute | solution.py:30
  58.3 1.5 %copy-done.7 = bf16[384,2432]{1,0:T(8,128)(2,1)S(1)} copy-done((bf16[384,2432]{1,0:T(8,128)(2,1)S(1)}, bf16[384,2432]{1,0:T(8,128)(2,1)}, u32[]{:S(2)}) %copy-start.7) | copy-done | bytes 1867800
  59.8 2.7 %shard_map.83.h_ref = bf16[384,2560]{1,0:T(8,128)(2,1)S(1)} custom-call(f32[3,1,2432]{2,1,0:T(1,128)S(1)} %copy-done.4, bf16[384,2432]{1,0:T(8,128)(2,1)S(1)} %copy-done.7), custom_call_target="tpu_custom_call" | custom-call | flops 20000000000 | bytes 1896960 | tf_op jit(solution)/shard_map/pallas_call | solution.py:323
  62.6 2.0 %shard_map.85 = (bf16[1120,128]{1,0:T(8,128)(2,1)S(1)}, bf16[384,192]{1,0:T(8,128)(2,1)S(1)}) custom-call(f32[2,1216]{1,0:T(2,128)S(1)} %bitcast.10, bf16[384,2560]{1,0:T(8,128)(2,1)S(1)} %shard_map.83.h_ref, bf16[64,320]{1,0:T(8,128)(2,1)S(1)} %get-tuple-element.17.text_ref, bf16[152,512]{1,0:T(8,128)(2,1)S(1)} %get-tuple-element.18.refs_0_.after_ref, ...), custom_call_target="tpu_custom_call" | custom-call | flops 1006632960 | bytes 4507136 | tf_op jit(solution)/shard_map/pallas_call | solution.py:323
  65.5 7.0 %collective-permute-done.18.far = bf16[1120,128]{1,0:T(8,128)(2,1)S(1)} collective-permute-done((bf16[1120,128]{1,0:T(8,128)(2,1)S(1)}, bf16[1120,128]{1,0:T(8,128)(2,1)S(1)}, u32[]{:S(2)}, u32[]{:S(2)}) %collective-permute-start.18) | collective-permute-done | bytes 286752 | tf_op jit(solution)/shard_map/ppermute | solution.py:30
  73.0 1.3 %collective-permute-done.17.beside_q = bf16[384,192]{1,0:T(8,128)(2,1)S(1)} collective-permute-done((bf16[384,192]{1,0:T(8,128)(2,1)S(1)}, bf16[384,192]{1,0:T(8,128)(2,1)S(1)}, u32[]{:S(2)}, u32[]{:S(2)}) %collective-permute-start.17) | collective-permute-done | bytes 147488 | tf_op jit(solution)/shard_map/ppermute | solution.py:30
  74.4 3.1 %shard_map.86.a0 = bf16[480,128]{1,0:T(8,128)(2,1)S(1)} custom-call(s32[8]{0:T(128)S(1)} %copy-done.6, bf16[1120,128]{1,0:T(8,128)(2,1)S(1)} %get-tuple-element.19.own, bf16[1120,128]{1,0:T(8,128)(2,1)S(1)} %collective-permute-done.16.beside, bf16[384,192]{1,0:T(8,128)(2,1)S(1)} %get-tuple-element.20.own_q, ...), custom_call_target="tpu_custom_call" | custom-call | flops 220200960 | bytes 1441824 | tf_op jit(solution)/shard_map/pallas_call | solution.py:323
  77.9 2.3 %collective-permute-start.21 = (bf16[480,128]{1,0:T(8,128)(2,1)S(1)}, bf16[480,128]{1,0:T(8,128)(2,1)S(1)}, u32[]{:S(2)}, u32[]{:S(2)}) collective-permute-start(bf16[480,128]{1,0:T(8,128)(2,1)S(1)} %shard_map.86.a0), channel_id=1, source_target_pairs={{0,4},{2,6},{4,0},{6,2},{1,5},{3,7},{5,1},{7,3},{8,12},{10,14},{12... | collective-permute-start | bytes 368648 | tf_op jit(solution)/shard_map/ppermute | solution.py:30
  80.2 1.1 collective-permute-start.22
  81.3 7.7 %all-gather.5.cloned.1.call-done.gathered_ref = bf16[640,1216]{1,0:T(8,128)(2,1)} async-done(((bf16[40,1216]{1,0:T(8,128)(2,1)}), bf16[640,1216]{1,0:T(8,128)(2,1)}) %all-gather.5.cloned.1.call-update) | async-done | bytes 1556496 | tf_op jit(solution)/shard_map/all_gather | solution.py:402
  89.0 1.4 %copy-done.8 = bf16[640,1216]{1,0:T(8,128)(2,1)S(1)} copy-done((bf16[640,1216]{1,0:T(8,128)(2,1)S(1)}, bf16[640,1216]{1,0:T(8,128)(2,1)}, u32[]{:S(2)}) %copy-start.8) | copy-done | bytes 1556504
  92.0 1.9 %collective-permute-start.24 = (bf16[48,608]{1,0:T(8,128)(2,1)S(1)}, bf16[48,608]{1,0:T(8,128)(2,1)S(1)}, u32[]{:S(2)}, u32[]{:S(2)}) collective-permute-start(bf16[48,608]{1,0:T(8,128)(2,1)S(1)} %get-tuple-element.22), channel_id=1, source_target_pairs={{0,2},{2,4},{4,6},{6,0},{1,3},{3,5},{5,7},{7,1},{8,10},{10,12},{12... | collective-permute-start | bytes 175112 | tf_op jit(solution)/shard_map/ppermute | solution.py:30
  93.8 1.5 %collective-permute-start.25 = (bf16[48,608]{1,0:T(8,128)(2,1)S(1)}, bf16[48,608]{1,0:T(8,128)(2,1)S(1)}, u32[]{:S(2)}, u32[]{:S(2)}) collective-permute-start(bf16[48,608]{1,0:T(8,128)(2,1)S(1)} %get-tuple-element.23), channel_id=1, source_target_pairs={{0,6},{2,0},{4,2},{6,4},{1,7},{3,1},{5,3},{7,5},{8,14},{10,8},{12,... | collective-permute-start | bytes 175112 | tf_op jit(solution)/shard_map/ppermute | solution.py:30
  95.3 2.0 %collective-permute-start.26 = (bf16[48,608]{1,0:T(8,128)(2,1)S(1)}, bf16[48,608]{1,0:T(8,128)(2,1)S(1)}, u32[]{:S(2)}, u32[]{:S(2)}) collective-permute-start(bf16[48,608]{1,0:T(8,128)(2,1)S(1)} %get-tuple-element.24), channel_id=1, source_target_pairs={{0,4},{2,6},{4,0},{6,2},{1,5},{3,7},{5,1},{7,3},{8,12},{10,14},{12... | collective-permute-start | bytes 175112 | tf_op jit(solution)/shard_map/ppermute | solution.py:30
  98.6 2.4 %collective-permute-done.26.n2 = bf16[48,608]{1,0:T(8,128)(2,1)S(1)} collective-permute-done((bf16[48,608]{1,0:T(8,128)(2,1)S(1)}, bf16[48,608]{1,0:T(8,128)(2,1)S(1)}, u32[]{:S(2)}, u32[]{:S(2)}) %collective-permute-start.26) | collective-permute-done | bytes 58400 | tf_op jit(solution)/shard_map/ppermute | solution.py:30
  (59 shorter events, 10.3 us)
Async XLA Ops:
  6.5 9.1 %collective-permute-start = (bf16[48,2432]{1,0:T(8,128)(2,1)}, bf16[48,2432]{1,0:T(8,128)(2,1)S(1)}, u32[]{:S(2)}, u32[]{:S(2)}) collective-permute-start(bf16[48,2432]{1,0:T(8,128)(2,1)} %bitcast.13), channel_id=1, source_target_pairs={{0,128},{128,0},{1,129},{129,1},{2,130},{130,2},{3,131},{131,3},{4... | collective-permute-start | bytes 700424 | tf_op jit(solution)/shard_map/ppermute | solution.py:30
  11.1 11.3 %all-to-all-start = ((bf16[8,24,512]{2,1,0:T(8,128)(2,1)}), bf16[8,24,512]{2,1,0:T(8,128)(2,1)S(1)}, u32[]{:S(2)}, u32[]{:S(2)}) async-start(bf16[8,24,512]{2,1,0:T(8,128)(2,1)} %get-tuple-element.16), calls=%async_computation | async-start | bytes 393216 | tf_op jit(solution)/shard_map/all_to_all | solution.py:355
  15.6 42.8 %all-gather.3.cloned.1.call-start = ((), (), s32[]{:S(2)}) async-start(), calls=%async_computation.1 | async-start | bytes 2101248 | tf_op jit(solution)/shard_map/all_gather | solution.py:373
  15.7 22.5 %copy-start.3 = (bf16[1,1216,19]{1,2,0:T(8,128)(2,1)S(1)}, bf16[1,1216,19]{1,2,0:T(8,128)(2,1)}, u32[]{:S(2)}) copy-start(bf16[1,1216,19]{1,2,0:T(8,128)(2,1)} %param.14) | copy-start | bytes 138628
  15.7 42.6 %copy-start.4 = (f32[3,1,2432]{2,1,0:T(1,128)S(1)}, f32[3,1,2432]{2,1,0:T(1,128)}, u32[]{:S(2)}) copy-start(f32[3,1,2432]{2,1,0:T(1,128)} %get-tuple-element.15.modulation) | copy-start | bytes 87556
  16.4 72.6 %all-gather.5.cloned.1.call-start = ((), (), s32[]{:S(2)}) async-start(), calls=%async_computation.2 | async-start | bytes 1740800 | tf_op jit(solution)/shard_map/all_gather | solution.py:402
  23.5 7.4 %collective-permute-start.1 = (bf16[152,512]{1,0:T(8,128)(2,1)S(1)}, bf16[152,512]{1,0:T(8,128)(2,1)S(1)}, u32[]{:S(2)}, u32[]{:S(2)}) collective-permute-start(bf16[152,512]{1,0:T(8,128)(2,1)S(1)} %get-tuple-element.18.refs_0_.after_ref), channel_id=1, source_target_pairs={{0,64},{64,0},{1,65},{65,1},{2,66},{66,2},{3,67},{67,3},{4,68},{68... | collective-permute-start | bytes 466952 | tf_op jit(solution)/shard_map/ppermute | solution.py:30
  25.0 9.9 %collective-permute-start.2 = (bf16[152,512]{1,0:T(8,128)(2,1)S(1)}, bf16[152,512]{1,0:T(8,128)(2,1)S(1)}, u32[]{:S(2)}, u32[]{:S(2)}) collective-permute-start(bf16[152,512]{1,0:T(8,128)(2,1)S(1)} %get-tuple-element.18.refs_0_.after_ref), channel_id=1, source_target_pairs={{0,8},{8,16},{16,24},{24,32},{32,40},{40,48},{48,56},{56,0},{1,9},... | collective-permute-start | bytes 466952 | tf_op jit(solution)/shard_map/ppermute | solution.py:30
  26.9 8.0 %collective-permute-start.4 = (bf16[152,512]{1,0:T(8,128)(2,1)S(1)}, bf16[152,512]{1,0:T(8,128)(2,1)S(1)}, u32[]{:S(2)}, u32[]{:S(2)}) collective-permute-start(bf16[152,512]{1,0:T(8,128)(2,1)S(1)} %get-tuple-element.18.refs_0_.after_ref), channel_id=1, source_target_pairs={{0,56},{8,0},{16,8},{24,16},{32,24},{40,32},{48,40},{56,48},{1,57}... | collective-permute-start | bytes 466952 | tf_op jit(solution)/shard_map/ppermute | solution.py:30
  30.8 11.7 %collective-permute-start.3 = (bf16[152,512]{1,0:T(8,128)(2,1)S(1)}, bf16[152,512]{1,0:T(8,128)(2,1)S(1)}, u32[]{:S(2)}, u32[]{:S(2)}) collective-permute-start(bf16[152,512]{1,0:T(8,128)(2,1)S(1)} %collective-permute-done.1.refs_1_), channel_id=1, source_target_pairs={{0,56},{8,0},{16,8},{24,16},{32,24},{40,32},{48,40},{56,48},{1,57}... | collective-permute-start | bytes 466952 | tf_op jit(solution)/shard_map/ppermute | solution.py:30
  34.9 7.7 %collective-permute-start.5 = (bf16[152,512]{1,0:T(8,128)(2,1)S(1)}, bf16[152,512]{1,0:T(8,128)(2,1)S(1)}, u32[]{:S(2)}, u32[]{:S(2)}) collective-permute-start(bf16[152,512]{1,0:T(8,128)(2,1)S(1)} %collective-permute-done.1.refs_1_), channel_id=1, source_target_pairs={{0,8},{8,16},{16,24},{24,32},{32,40},{40,48},{48,56},{56,0},{1,9},... | collective-permute-start | bytes 466952 | tf_op jit(solution)/shard_map/ppermute | solution.py:30
  34.9 8.8 %collective-permute-start.6 = (bf16[152,512]{1,0:T(8,128)(2,1)S(1)}, bf16[152,512]{1,0:T(8,128)(2,1)S(1)}, u32[]{:S(2)}, u32[]{:S(2)}) collective-permute-start(bf16[152,512]{1,0:T(8,128)(2,1)S(1)} %collective-permute-done.2.refs_2_), channel_id=1, source_target_pairs={{0,8},{8,16},{16,24},{24,32},{32,40},{40,48},{48,56},{56,0},{1,9},... | collective-permute-start | bytes 466952 | tf_op jit(solution)/shard_map/ppermute | solution.py:30
  34.9 8.8 %collective-permute-start.8 = (bf16[152,512]{1,0:T(8,128)(2,1)S(1)}, bf16[152,512]{1,0:T(8,128)(2,1)S(1)}, u32[]{:S(2)}, u32[]{:S(2)}) collective-permute-start(bf16[152,512]{1,0:T(8,128)(2,1)S(1)} %collective-permute-done.4.refs_4_), channel_id=1, source_target_pairs={{0,56},{8,0},{16,8},{24,16},{32,24},{40,32},{48,40},{56,48},{1,57}... | collective-permute-start | bytes 466952 | tf_op jit(solution)/shard_map/ppermute | solution.py:30
  38.2 4.3 %collective-permute-start.23 = (bf16[19,1216]{1,0:T(8,128)(2,1)S(1)}, bf16[19,1216]{1,0:T(8,128)(2,1)S(1)}, u32[]{:S(2)}, u32[]{:S(2)}) collective-permute-start(bf16[19,1216]{1,0:T(8,128)(2,1)S(1)} %shard_map.87), channel_id=1, source_target_pairs={{0,64},{64,0},{1,65},{65,1},{2,66},{66,2},{3,67},{67,3},{4,68},{68... | collective-permute-start | bytes 138632 | tf_op jit(solution)/shard_map/ppermute | solution.py:30
  44.4 5.9 %collective-permute-start.7 = (bf16[152,512]{1,0:T(8,128)(2,1)S(1)}, bf16[152,512]{1,0:T(8,128)(2,1)S(1)}, u32[]{:S(2)}, u32[]{:S(2)}) collective-permute-start(bf16[152,512]{1,0:T(8,128)(2,1)S(1)} %collective-permute-done.3.refs_3_), channel_id=1, source_target_pairs={{0,56},{8,0},{16,8},{24,16},{32,24},{40,32},{48,40},{56,48},{1,57}... | collective-permute-start | bytes 466952 | tf_op jit(solution)/shard_map/ppermute | solution.py:30
  45.4 6.7 %collective-permute-start.9 = (bf16[152,512]{1,0:T(8,128)(2,1)S(1)}, bf16[152,512]{1,0:T(8,128)(2,1)S(1)}, u32[]{:S(2)}, u32[]{:S(2)}) collective-permute-start(bf16[152,512]{1,0:T(8,128)(2,1)S(1)} %collective-permute-done.5.refs_5_.refs_2_), channel_id=1, source_target_pairs={{0,8},{8,16},{16,24},{24,32},{32,40},{40,48},{48,56},{56,0},{1,9},... | collective-permute-start | bytes 466952 | tf_op jit(solution)/shard_map/ppermute | solution.py:30
  46.5 8.1 %collective-permute-start.10 = (bf16[152,512]{1,0:T(8,128)(2,1)S(1)}, bf16[152,512]{1,0:T(8,128)(2,1)S(1)}, u32[]{:S(2)}, u32[]{:S(2)}) collective-permute-start(bf16[152,512]{1,0:T(8,128)(2,1)S(1)} %collective-permute-done.6.refs_6_.refs_0_), channel_id=1, source_target_pairs={{0,8},{8,16},{16,24},{24,32},{32,40},{40,48},{48,56},{56,0},{1,9},... | collective-permute-start | bytes 466952 | tf_op jit(solution)/shard_map/ppermute | solution.py:30
  50.3 6.7 %collective-permute-start.11 = (bf16[152,512]{1,0:T(8,128)(2,1)S(1)}, bf16[152,512]{1,0:T(8,128)(2,1)S(1)}, u32[]{:S(2)}, u32[]{:S(2)}) collective-permute-start(bf16[152,512]{1,0:T(8,128)(2,1)S(1)} %collective-permute-done.7.refs_7_), channel_id=1, source_target_pairs={{0,56},{8,0},{16,8},{24,16},{32,24},{40,32},{48,40},{56,48},{1,57}... | collective-permute-start | bytes 466952 | tf_op jit(solution)/shard_map/ppermute | solution.py:30
  51.9 10.7 %collective-permute-start.12 = (bf16[152,512]{1,0:T(8,128)(2,1)S(1)}, bf16[152,512]{1,0:T(8,128)(2,1)S(1)}, u32[]{:S(2)}, u32[]{:S(2)}) collective-permute-start(bf16[152,512]{1,0:T(8,128)(2,1)S(1)} %collective-permute-done.8.refs_8_.refs_1_), channel_id=1, source_target_pairs={{0,56},{8,0},{16,8},{24,16},{32,24},{40,32},{48,40},{56,48},{1,57}... | collective-permute-start | bytes 466952 | tf_op jit(solution)/shard_map/ppermute | solution.py:30
  52.1 10.4 %collective-permute-start.13 = (bf16[152,512]{1,0:T(8,128)(2,1)S(1)}, bf16[152,512]{1,0:T(8,128)(2,1)S(1)}, u32[]{:S(2)}, u32[]{:S(2)}) collective-permute-start(bf16[152,512]{1,0:T(8,128)(2,1)S(1)} %collective-permute-done.9.refs_9_), channel_id=1, source_target_pairs={{0,8},{8,16},{16,24},{24,32},{32,40},{40,48},{48,56},{56,0},{1,9},... | collective-permute-start | bytes 466952 | tf_op jit(solution)/shard_map/ppermute | solution.py:30
  54.7 7.9 %collective-permute-start.14 = (bf16[152,512]{1,0:T(8,128)(2,1)S(1)}, bf16[152,512]{1,0:T(8,128)(2,1)S(1)}, u32[]{:S(2)}, u32[]{:S(2)}) collective-permute-start(bf16[152,512]{1,0:T(8,128)(2,1)S(1)} %collective-permute-done.10.refs_10_), channel_id=1, source_target_pairs={{0,8},{8,16},{16,24},{24,32},{32,40},{40,48},{48,56},{56,0},{1,9},... | collective-permute-start | bytes 466952 | tf_op jit(solution)/shard_map/ppermute | solution.py:30
  57.0 5.5 %collective-permute-start.15 = (bf16[152,512]{1,0:T(8,128)(2,1)S(1)}, bf16[152,512]{1,0:T(8,128)(2,1)S(1)}, u32[]{:S(2)}, u32[]{:S(2)}) collective-permute-start(bf16[152,512]{1,0:T(8,128)(2,1)S(1)} %collective-permute-done.11.refs_11_), channel_id=1, source_target_pairs={{0,56},{8,0},{16,8},{24,16},{32,24},{40,32},{48,40},{56,48},{1,57}... | collective-permute-start | bytes 466952 | tf_op jit(solution)/shard_map/ppermute | solution.py:30
  64.6 7.9 %collective-permute-start.18 = (bf16[1120,128]{1,0:T(8,128)(2,1)S(1)}, bf16[1120,128]{1,0:T(8,128)(2,1)S(1)}, u32[]{:S(2)}, u32[]{:S(2)}) collective-permute-start(bf16[1120,128]{1,0:T(8,128)(2,1)S(1)} %get-tuple-element.19.own), channel_id=1, source_target_pairs={{0,8},{8,0},{1,9},{9,1},{2,10},{10,2},{3,11},{11,3},{4,12},{12,4},... | collective-permute-start | bytes 860168 | tf_op jit(solution)/shard_map/ppermute | solution.py:30
  65.4 8.9 %collective-permute-start.16 = (bf16[1120,128]{1,0:T(8,128)(2,1)S(1)}, bf16[1120,128]{1,0:T(8,128)(2,1)S(1)}, u32[]{:S(2)}, u32[]{:S(2)}) collective-permute-start(bf16[1120,128]{1,0:T(8,128)(2,1)S(1)} %get-tuple-element.19.own), channel_id=1, source_target_pairs={{0,1},{1,0},{2,3},{3,2},{4,5},{5,4},{6,7},{7,6},{8,9},{9,8},{10,11... | collective-permute-start | bytes 860168 | tf_op jit(solution)/shard_map/ppermute | solution.py:30
  72.5 1.9 %collective-permute-start.19 = (bf16[1120,128]{1,0:T(8,128)(2,1)S(1)}, bf16[1120,128]{1,0:T(8,128)(2,1)S(1)}, u32[]{:S(2)}, u32[]{:S(2)}) collective-permute-start(bf16[1120,128]{1,0:T(8,128)(2,1)S(1)} %collective-permute-done.18.far), channel_id=1, source_target_pairs={{0,1},{1,0},{2,3},{3,2},{4,5},{5,4},{6,7},{7,6},{8,9},{9,8},{10,11... | collective-permute-start | bytes 860168 | tf_op jit(solution)/shard_map/ppermute | solution.py:30
  72.5 1.8 %collective-permute-start.17 = (bf16[384,192]{1,0:T(8,128)(2,1)S(1)}, bf16[384,192]{1,0:T(8,128)(2,1)S(1)}, u32[]{:S(2)}, u32[]{:S(2)}) collective-permute-start(bf16[384,192]{1,0:T(8,128)(2,1)S(1)} %get-tuple-element.20.own_q), channel_id=1, source_target_pairs={{0,1},{1,0},{2,3},{3,2},{4,5},{5,4},{6,7},{7,6},{8,9},{9,8},{10,11... | collective-permute-start | bytes 442376 | tf_op jit(solution)/shard_map/ppermute | solution.py:30
  77.4 13.5 %collective-permute-start.20 = (bf16[480,128]{1,0:T(8,128)(2,1)S(1)}, bf16[480,128]{1,0:T(8,128)(2,1)S(1)}, u32[]{:S(2)}, u32[]{:S(2)}) collective-permute-start(bf16[480,128]{1,0:T(8,128)(2,1)S(1)} %shard_map.86.a0), channel_id=1, source_target_pairs={{0,2},{2,4},{4,6},{6,0},{1,3},{3,5},{5,7},{7,1},{8,10},{10,12},{12... | collective-permute-start | bytes 368648 | tf_op jit(solution)/shard_map/ppermute | solution.py:30
  77.9 13.1 %collective-permute-start.21 = (bf16[480,128]{1,0:T(8,128)(2,1)S(1)}, bf16[480,128]{1,0:T(8,128)(2,1)S(1)}, u32[]{:S(2)}, u32[]{:S(2)}) collective-permute-start(bf16[480,128]{1,0:T(8,128)(2,1)S(1)} %shard_map.86.a0), channel_id=1, source_target_pairs={{0,4},{2,6},{4,0},{6,2},{1,5},{3,7},{5,1},{7,3},{8,12},{10,14},{12... | collective-permute-start | bytes 368648 | tf_op jit(solution)/shard_map/ppermute | solution.py:30
  80.2 10.7 %collective-permute-start.22 = (bf16[480,128]{1,0:T(8,128)(2,1)S(1)}, bf16[480,128]{1,0:T(8,128)(2,1)S(1)}, u32[]{:S(2)}, u32[]{:S(2)}) collective-permute-start(bf16[480,128]{1,0:T(8,128)(2,1)S(1)} %shard_map.86.a0), channel_id=1, source_target_pairs={{0,6},{2,0},{4,2},{6,4},{1,7},{3,1},{5,3},{7,5},{8,14},{10,8},{12,... | collective-permute-start | bytes 368648 | tf_op jit(solution)/shard_map/ppermute | solution.py:30
  92.0 5.5 %collective-permute-start.24 = (bf16[48,608]{1,0:T(8,128)(2,1)S(1)}, bf16[48,608]{1,0:T(8,128)(2,1)S(1)}, u32[]{:S(2)}, u32[]{:S(2)}) collective-permute-start(bf16[48,608]{1,0:T(8,128)(2,1)S(1)} %get-tuple-element.22), channel_id=1, source_target_pairs={{0,2},{2,4},{4,6},{6,0},{1,3},{3,5},{5,7},{7,1},{8,10},{10,12},{12... | collective-permute-start | bytes 175112 | tf_op jit(solution)/shard_map/ppermute | solution.py:30
  93.8 4.3 %collective-permute-start.25 = (bf16[48,608]{1,0:T(8,128)(2,1)S(1)}, bf16[48,608]{1,0:T(8,128)(2,1)S(1)}, u32[]{:S(2)}, u32[]{:S(2)}) collective-permute-start(bf16[48,608]{1,0:T(8,128)(2,1)S(1)} %get-tuple-element.23), channel_id=1, source_target_pairs={{0,6},{2,0},{4,2},{6,4},{1,7},{3,1},{5,3},{7,5},{8,14},{10,8},{12,... | collective-permute-start | bytes 175112 | tf_op jit(solution)/shard_map/ppermute | solution.py:30
  95.3 5.7 %collective-permute-start.26 = (bf16[48,608]{1,0:T(8,128)(2,1)S(1)}, bf16[48,608]{1,0:T(8,128)(2,1)S(1)}, u32[]{:S(2)}, u32[]{:S(2)}) collective-permute-start(bf16[48,608]{1,0:T(8,128)(2,1)S(1)} %get-tuple-element.24), channel_id=1, source_target_pairs={{0,4},{2,6},{4,0},{6,2},{1,5},{3,7},{5,1},{7,3},{8,12},{10,14},{12... | collective-permute-start | bytes 175112 | tf_op jit(solution)/shard_map/ppermute | solution.py:30
  (7 other events, 21.9 us)
Sparse Core Ops, SparseCore 0:
  18.2 29.6 all-gather.2
  49.7 39.2 all-gather.4

commit v6 on v5

--- a/solution.py
+++ b/solution.py
@@ -255,19 +255,7 @@
             out_ref[at : at + half, HD:] = attended[half:]
 
 
-def arrange_kernel(gathered_ref, out_ref, weights):
-    each = weights.shape[0] // 32
-    gap = gathered_ref.shape[0] // 16
-    for place in range(16):
-        value = gathered_ref[place * gap : (place + 1) * gap, :].astype(F32)
-        core, z = divmod(place, 8)
-        for x in range(2):
-            at = ((x * 8 + z) * 2 + core) * each
-            weights[at : at + each, :] = value[x * each : (x + 1) * each]
-    out_ref[...] = weights[...].astype(BF16)
-
-
-def finish_kernel(a0, a1, a2, a3, weight_ref, o0, o1, o2, o3, heads, result):
+def finish_kernel(a0, a1, a2, a3, gathered_ref, o0, o1, o2, o3, heads, result):
     y = lax.axis_index("y")
     rows = a0.shape[0] * 2 // YH
     half = rows // 2
@@ -282,28 +270,31 @@
         size = min(YW, HEADS * HD - q * YW)
         part = lax.dot_general(
             heads[q][:, :size],
-            weight_ref[:, q * YW : q * YW + size],
+            gathered_ref[:, q * YW : q * YW + size],
             (((1,), (1,)), ((), ())),
             preferred_element_type=F32,
         )
         total = part if total is None else total + part
-    rows = o0.shape[0]
-    result[...] = total.astype(BF16).reshape(4, rows, total.shape[1])
+    result[...] = total.astype(BF16).reshape(4, rows // 4, total.shape[1])
     for by, out_ref in enumerate((o0, o1, o2, o3)):
         out_ref[...] = result[lax.rem(y + by, 4)]
 
 
 def place_columns(part, by, branch):
     y = lax.axis_index("y")
-    run = part.shape[1] // 16
+    run = branch.shape[1] // 128
+    gap = part.shape[1] // 16
     value = part[...].astype(F32)
     for q in range(4):
 
         @pl.when(lax.rem(y + 4 - by, 4) == q)
         def _():
-            for m in range(16):
-                at = (m * 4 + q) * run
-                branch[:, at : at + run] = value[:, m * run : (m + 1) * run]
+            for place in range(16):
+                core, z = divmod(place, 8)
+                for x in range(2):
+                    at = (((x * 8 + z) * 4 + q) * 2 + core) * run
+                    begin = place * gap + x * run
+                    branch[:, at : at + run] = value[:, begin : begin + run]
 
 
 def assemble_early_kernel(n0, n1, n3, branch):
@@ -340,7 +331,6 @@
     rows, width = stale_states.shape[1:]
     head_width = HEADS * HD
     weight_rows = qkv_weight.shape[1]
-    quarter = width // 4
     split = HALF - YW
 
     halves, modulation = in_vmem(
@@ -434,24 +424,16 @@
         scalars=1,
     )
 
-    out_columns = in_vmem(
-        arrange_kernel,
-        jax.ShapeDtypeStruct((32 * weight_rows, head_width), BF16),
-        (out_columns,),
-        flops=10**10,
-        scratch=[pltpu.VMEM((32 * weight_rows, head_width), F32)],
-    )
     gathered = tuple(permuted(attended, "y", by) for by in (1, 2, 3))
+    columns = out_columns.shape[0]
     parts = in_vmem(
         finish_kernel,
-        (jax.ShapeDtypeStruct((rows, quarter), BF16),) * 4,
-        (attended,)
-        + gathered
-        + (out_columns,),
-        flops=2 * 4 * rows * head_width * quarter,
+        (jax.ShapeDtypeStruct((rows, columns), BF16),) * 4,
+        (attended,) + gathered + (out_columns,),
+        flops=2 * 4 * rows * head_width * columns,
         scratch=[
             pltpu.VMEM((4, 4 * rows, YW), BF16),
-            pltpu.VMEM((4, rows, quarter), BF16),
+            pltpu.VMEM((4, rows, columns), BF16),
         ],
     )
     parts = [parts[0]] + [permuted(parts[by], "y", by) for by in (1, 2, 3)]

time: 109 us -> 112 us (1.028); the launches traced: 109 us -> 111 us
  starting transfers between devices: 40.2 us -> 43.8 us
  waiting for transfers between devices: 36.6 us -> 35.1 us
    ppermute x27, starting transfers between devices: 35.6 us -> 39.2 us  [permuted(): lax.ppermute(array, axis, [(i, (i + by) % devices) for i in range(devices)])]
    all_gather x1, waiting for transfers between devices: 7.73 us -> 4.48 us  [per_device(): out_columns = lax.all_gather(both, ('core', 'z1', 'z0'), axis=0, tiled=True)]
    ppermute x27, waiting for transfers between devices: 22.9 us -> 24.6 us  [permuted(): lax.ppermute(array, axis, [(i, (i + by) % devices) for i in range(devices)])]
    pallas_call x11 -> x10, Pallas kernels: 13.8 us -> 13.6 us  [in_vmem(): pl.pallas_call(kernel, out_shape=out_shape, in_specs=[pl.BlockSpec(memory...]
  transfers between devices with their start and end apart: 30 -> 30, of which waited for: 14 -> 14; matrix products, arithmetic and copies ran while one was open for 0% -> 0% of each run, Pallas kernels for 11% -> 10%
where the time goes in v6:
time: 112 us; the launch traced here: 111 us
  starting transfers between devices  43.8 us (39%)
  waiting for transfers between devices  35.1 us (31%)
  Pallas kernels  13.6 us (12%)
  between operations  13.6 us (12%)
  local copies, waits for them, and re-layouts  4.59 us (4%)
    ppermute x27, starting transfers between devices, permuted(): lax.ppermute(array, axis, [(i, (i + by) % devices) for i in range(devices)])  39.2 us
    ppermute x27, waiting for transfers between devices, permuted(): lax.ppermute(array, axis, [(i, (i + by) % devices) for i in range(devices)])  24.6 us
    pallas_call x10, Pallas kernels, in_vmem(): pl.pallas_call(kernel, out_shape=out_shape, in_specs=[pl.BlockSpec(memory...  13.6 us
    all_to_all x1, waiting for transfers between devices, per_device(): lax.all_to_all(halves, ('y', 'core'), split_axis=0, concat_axis=0, tiled=...  5.95 us
    unnamed x18, local copies, waits for them, and re-layouts  4.59 us
    all_to_all x1, starting transfers between devices, per_device(): lax.all_to_all(halves, ('y', 'core'), split_axis=0, concat_axis=0, tiled=...  4.48 us
    all_gather x1, waiting for transfers between devices, per_device(): out_columns = lax.all_gather(both, ('core', 'z1', 'z0'), axis=0, tiled=True)  4.48 us
  transfers between devices with their start and end apart: 30, of which 14 were waited for; matrix products, arithmetic and copies ran while one was open for 0% of the time, Pallas kernels for 10%

profile of v6, /device:TPU:2, one launch (start us, length us, event | category | flops | bytes accessed | tf_op | source)
XLA Modules:
  0.0 110.6 jit_solution(6344141096032719405)
XLA Ops:
  6.5 2.1 %collective-permute-start = (bf16[48,2432]{1,0:T(8,128)(2,1)}, bf16[48,2432]{1,0:T(8,128)(2,1)S(1)}, u32[]{:S(2)}, u32[]{:S(2)}) collective-permute-start(bf16[48,2432]{1,0:T(8,128)(2,1)} %bitcast.13), channel_id=1, source_target_pairs={{0,128},{128,0},{1,129},{129,1},{2,130},{130,2},{3,131},{131,3},{4... | collective-permute-start | bytes 700424 | tf_op jit(solution)/shard_map/ppermute | solution.py:30
  8.7 2.4 %shard_map.82 = (bf16[8,24,512]{2,1,0:T(8,128)(2,1)}, f32[3,1,2432]{2,1,0:T(1,128)}) custom-call(s32[8]{0:T(128)} %steps_ref.1, bf16[19,3648]{1,0:T(8,128)(2,1)} %bitcast.12, bf16[2,8,1216]{2,1,0:T(8,128)(2,1)} %text_ref.1, f32[28,3,1,2432]{3,2,1,0:T(1,128)} %bitcast.11), custom_call_target="tpu_custom_call" | custom-call | bytes 177568 | tf_op jit(solution)/shard_map/pallas_call | solution.py:314
  11.1 4.5 %all-to-all-start = ((bf16[8,24,512]{2,1,0:T(8,128)(2,1)}), bf16[8,24,512]{2,1,0:T(8,128)(2,1)S(1)}, u32[]{:S(2)}, u32[]{:S(2)}) async-start(bf16[8,24,512]{2,1,0:T(8,128)(2,1)} %get-tuple-element.16), calls=%async_computation | async-start | bytes 393216 | tf_op jit(solution)/shard_map/all_to_all | solution.py:345
  16.4 5.9 %all-to-all-done.received_ref = bf16[8,24,512]{2,1,0:T(8,128)(2,1)S(1)} async-done(((bf16[8,24,512]{2,1,0:T(8,128)(2,1)}), bf16[8,24,512]{2,1,0:T(8,128)(2,1)S(1)}, u32[]{:S(2)}, u32[]{:S(2)}) %all-to-all-start) | async-done | bytes 196640 | tf_op jit(solution)/shard_map/all_to_all | solution.py:345
  23.5 1.5 %collective-permute-start.1 = (bf16[152,512]{1,0:T(8,128)(2,1)S(1)}, bf16[152,512]{1,0:T(8,128)(2,1)S(1)}, u32[]{:S(2)}, u32[]{:S(2)}) collective-permute-start(bf16[152,512]{1,0:T(8,128)(2,1)S(1)} %get-tuple-element.18.refs_0_.after_ref), channel_id=1, source_target_pairs={{0,64},{64,0},{1,65},{65,1},{2,66},{66,2},{3,67},{67,3},{4,68},{68... | collective-permute-start | bytes 466952 | tf_op jit(solution)/shard_map/ppermute | solution.py:30
  25.0 1.9 %collective-permute-start.2 = (bf16[152,512]{1,0:T(8,128)(2,1)S(1)}, bf16[152,512]{1,0:T(8,128)(2,1)S(1)}, u32[]{:S(2)}, u32[]{:S(2)}) collective-permute-start(bf16[152,512]{1,0:T(8,128)(2,1)S(1)} %get-tuple-element.18.refs_0_.after_ref), channel_id=1, source_target_pairs={{0,8},{8,16},{16,24},{24,32},{32,40},{40,48},{48,56},{56,0},{1,9},... | collective-permute-start | bytes 466952 | tf_op jit(solution)/shard_map/ppermute | solution.py:30
  26.9 3.9 %collective-permute-start.4 = (bf16[152,512]{1,0:T(8,128)(2,1)S(1)}, bf16[152,512]{1,0:T(8,128)(2,1)S(1)}, u32[]{:S(2)}, u32[]{:S(2)}) collective-permute-start(bf16[152,512]{1,0:T(8,128)(2,1)S(1)} %get-tuple-element.18.refs_0_.after_ref), channel_id=1, source_target_pairs={{0,56},{8,0},{16,8},{24,16},{32,24},{40,32},{48,40},{56,48},{1,57}... | collective-permute-start | bytes 466952 | tf_op jit(solution)/shard_map/ppermute | solution.py:30
  30.8 4.0 %collective-permute-start.3 = (bf16[152,512]{1,0:T(8,128)(2,1)S(1)}, bf16[152,512]{1,0:T(8,128)(2,1)S(1)}, u32[]{:S(2)}, u32[]{:S(2)}) collective-permute-start(bf16[152,512]{1,0:T(8,128)(2,1)S(1)} %collective-permute-done.1.refs_1_), channel_id=1, source_target_pairs={{0,56},{8,0},{16,8},{24,16},{32,24},{40,32},{48,40},{56,48},{1,57}... | collective-permute-start | bytes 466952 | tf_op jit(solution)/shard_map/ppermute | solution.py:30
  34.9 3.3 %collective-permute-start.8 = (bf16[152,512]{1,0:T(8,128)(2,1)S(1)}, bf16[152,512]{1,0:T(8,128)(2,1)S(1)}, u32[]{:S(2)}, u32[]{:S(2)}) collective-permute-start(bf16[152,512]{1,0:T(8,128)(2,1)S(1)} %collective-permute-done.4.refs_4_), channel_id=1, source_target_pairs={{0,56},{8,0},{16,8},{24,16},{32,24},{40,32},{48,40},{56,48},{1,57}... | collective-permute-start | bytes 466952 | tf_op jit(solution)/shard_map/ppermute | solution.py:30
  38.9 3.7 %collective-permute-start.7 = (bf16[152,512]{1,0:T(8,128)(2,1)S(1)}, bf16[152,512]{1,0:T(8,128)(2,1)S(1)}, u32[]{:S(2)}, u32[]{:S(2)}) collective-permute-start(bf16[152,512]{1,0:T(8,128)(2,1)S(1)} %collective-permute-done.3.refs_3_), channel_id=1, source_target_pairs={{0,56},{8,0},{16,8},{24,16},{32,24},{40,32},{48,40},{56,48},{1,57}... | collective-permute-start | bytes 466952 | tf_op jit(solution)/shard_map/ppermute | solution.py:30
  42.7 1.5 %collective-permute-start.23 = (bf16[19,1216]{1,0:T(8,128)(2,1)S(1)}, bf16[19,1216]{1,0:T(8,128)(2,1)S(1)}, u32[]{:S(2)}, u32[]{:S(2)}) collective-permute-start(bf16[19,1216]{1,0:T(8,128)(2,1)S(1)} %shard_map.87), channel_id=1, source_target_pairs={{0,64},{64,0},{1,65},{65,1},{2,66},{66,2},{3,67},{67,3},{4,68},{68... | collective-permute-start | bytes 138632 | tf_op jit(solution)/shard_map/ppermute | solution.py:30
  44.2 2.8 %collective-permute-done.23.other_ref = bf16[19,1216]{1,0:T(8,128)(2,1)S(1)} collective-permute-done((bf16[19,1216]{1,0:T(8,128)(2,1)S(1)}, bf16[19,1216]{1,0:T(8,128)(2,1)S(1)}, u32[]{:S(2)}, u32[]{:S(2)}) %collective-permute-start.23) | collective-permute-done | bytes 46240 | tf_op jit(solution)/shard_map/ppermute | solution.py:30
  47.9 3.2 %collective-permute-start.11 = (bf16[152,512]{1,0:T(8,128)(2,1)S(1)}, bf16[152,512]{1,0:T(8,128)(2,1)S(1)}, u32[]{:S(2)}, u32[]{:S(2)}) collective-permute-start(bf16[152,512]{1,0:T(8,128)(2,1)S(1)} %collective-permute-done.7.refs_7_), channel_id=1, source_target_pairs={{0,56},{8,0},{16,8},{24,16},{32,24},{40,32},{48,40},{56,48},{1,57}... | collective-permute-start | bytes 466952 | tf_op jit(solution)/shard_map/ppermute | solution.py:30
  51.1 1.9 %collective-permute-start.12 = (bf16[152,512]{1,0:T(8,128)(2,1)S(1)}, bf16[152,512]{1,0:T(8,128)(2,1)S(1)}, u32[]{:S(2)}, u32[]{:S(2)}) collective-permute-start(bf16[152,512]{1,0:T(8,128)(2,1)S(1)} %collective-permute-done.8.refs_8_.refs_1_), channel_id=1, source_target_pairs={{0,56},{8,0},{16,8},{24,16},{32,24},{40,32},{48,40},{56,48},{1,57}... | collective-permute-start | bytes 466952 | tf_op jit(solution)/shard_map/ppermute | solution.py:30
  53.0 2.8 %collective-permute-done.9.refs_9_ = bf16[152,512]{1,0:T(8,128)(2,1)S(1)} collective-permute-done((bf16[152,512]{1,0:T(8,128)(2,1)S(1)}, bf16[152,512]{1,0:T(8,128)(2,1)S(1)}, u32[]{:S(2)}, u32[]{:S(2)}) %collective-permute-start.9) | collective-permute-done | bytes 155680 | tf_op jit(solution)/shard_map/ppermute | solution.py:30
  55.8 2.9 %collective-permute-done.10.refs_10_ = bf16[152,512]{1,0:T(8,128)(2,1)S(1)} collective-permute-done((bf16[152,512]{1,0:T(8,128)(2,1)S(1)}, bf16[152,512]{1,0:T(8,128)(2,1)S(1)}, u32[]{:S(2)}, u32[]{:S(2)}) %collective-permute-start.10) | collective-permute-done | bytes 155680 | tf_op jit(solution)/shard_map/ppermute | solution.py:30
  58.7 3.2 %collective-permute-start.15 = (bf16[152,512]{1,0:T(8,128)(2,1)S(1)}, bf16[152,512]{1,0:T(8,128)(2,1)S(1)}, u32[]{:S(2)}, u32[]{:S(2)}) collective-permute-start(bf16[152,512]{1,0:T(8,128)(2,1)S(1)} %collective-permute-done.11.refs_11_), channel_id=1, source_target_pairs={{0,56},{8,0},{16,8},{24,16},{32,24},{40,32},{48,40},{56,48},{1,57}... | collective-permute-start | bytes 466952 | tf_op jit(solution)/shard_map/ppermute | solution.py:30
  61.9 1.5 %copy-done.8 = bf16[384,2432]{1,0:T(8,128)(2,1)S(1)} copy-done((bf16[384,2432]{1,0:T(8,128)(2,1)S(1)}, bf16[384,2432]{1,0:T(8,128)(2,1)}, u32[]{:S(2)}) %copy-start.8) | copy-done | bytes 1867800
  63.4 2.7 %shard_map.83.h_ref = bf16[384,2560]{1,0:T(8,128)(2,1)S(1)} custom-call(f32[3,1,2432]{2,1,0:T(1,128)S(1)} %copy-done.5, bf16[384,2432]{1,0:T(8,128)(2,1)S(1)} %copy-done.8), custom_call_target="tpu_custom_call" | custom-call | flops 20000000000 | bytes 1896960 | tf_op jit(solution)/shard_map/pallas_call | solution.py:314
  66.2 2.0 %shard_map.85 = (bf16[1120,128]{1,0:T(8,128)(2,1)S(1)}, bf16[384,192]{1,0:T(8,128)(2,1)S(1)}) custom-call(f32[2,1216]{1,0:T(2,128)S(1)} %bitcast.10, bf16[384,2560]{1,0:T(8,128)(2,1)S(1)} %shard_map.83.h_ref, bf16[64,320]{1,0:T(8,128)(2,1)S(1)} %get-tuple-element.17.text_ref, bf16[152,512]{1,0:T(8,128)(2,1)S(1)} %get-tuple-element.18.refs_0_.after_ref, ...), custom_call_target="tpu_custom_call" | custom-call | flops 1006632960 | bytes 4507136 | tf_op jit(solution)/shard_map/pallas_call | solution.py:314
  68.4 7.8 %collective-permute-done.18.far = bf16[1120,128]{1,0:T(8,128)(2,1)S(1)} collective-permute-done((bf16[1120,128]{1,0:T(8,128)(2,1)S(1)}, bf16[1120,128]{1,0:T(8,128)(2,1)S(1)}, u32[]{:S(2)}, u32[]{:S(2)}) %collective-permute-start.18) | collective-permute-done | bytes 286752 | tf_op jit(solution)/shard_map/ppermute | solution.py:30
  76.7 1.4 %collective-permute-done.17.beside_q = bf16[384,192]{1,0:T(8,128)(2,1)S(1)} collective-permute-done((bf16[384,192]{1,0:T(8,128)(2,1)S(1)}, bf16[384,192]{1,0:T(8,128)(2,1)S(1)}, u32[]{:S(2)}, u32[]{:S(2)}) %collective-permute-start.17) | collective-permute-done | bytes 147488 | tf_op jit(solution)/shard_map/ppermute | solution.py:30
  78.1 3.1 %shard_map.86.a0 = bf16[480,128]{1,0:T(8,128)(2,1)S(1)} custom-call(s32[8]{0:T(128)S(1)} %copy-done.7, bf16[1120,128]{1,0:T(8,128)(2,1)S(1)} %get-tuple-element.19.own, bf16[1120,128]{1,0:T(8,128)(2,1)S(1)} %collective-permute-done.16.beside, bf16[384,192]{1,0:T(8,128)(2,1)S(1)} %get-tuple-element.20.own_q, ...), custom_call_target="tpu_custom_call" | custom-call | flops 220200960 | bytes 1441824 | tf_op jit(solution)/shard_map/pallas_call | solution.py:314
  81.8 2.4 %collective-permute-start.21 = (bf16[480,128]{1,0:T(8,128)(2,1)S(1)}, bf16[480,128]{1,0:T(8,128)(2,1)S(1)}, u32[]{:S(2)}, u32[]{:S(2)}) collective-permute-start(bf16[480,128]{1,0:T(8,128)(2,1)S(1)} %shard_map.86.a0), channel_id=1, source_target_pairs={{0,4},{2,6},{4,0},{6,2},{1,5},{3,7},{5,1},{7,3},{8,12},{10,14},{12... | collective-permute-start | bytes 368648 | tf_op jit(solution)/shard_map/ppermute | solution.py:30
  84.9 4.5 %all-gather.5.cloned.1.call-done.gathered_ref = bf16[640,1216]{1,0:T(8,128)(2,1)} async-done(((bf16[40,1216]{1,0:T(8,128)(2,1)}), bf16[640,1216]{1,0:T(8,128)(2,1)}) %all-gather.5.cloned.1.call-update) | async-done | bytes 1556496 | tf_op jit(solution)/shard_map/all_gather | solution.py:392
  89.4 1.1 collective-permute-done.20.a1
  91.1 1.4 %copy-done = bf16[640,1216]{1,0:T(8,128)(2,1)S(1)} copy-done((bf16[640,1216]{1,0:T(8,128)(2,1)S(1)}, bf16[640,1216]{1,0:T(8,128)(2,1)}, u32[]{:S(2)}) %copy-start) | copy-done | bytes 1556504
  92.5 1.0 shard_map.89
  94.1 2.9 %collective-permute-start.25 = (bf16[48,640]{1,0:T(8,128)(2,1)S(1)}, bf16[48,640]{1,0:T(8,128)(2,1)S(1)}, u32[]{:S(2)}, u32[]{:S(2)}) collective-permute-start(bf16[48,640]{1,0:T(8,128)(2,1)S(1)} %get-tuple-element.23), channel_id=1, source_target_pairs={{0,6},{2,0},{4,2},{6,4},{1,7},{3,1},{5,3},{7,5},{8,14},{10,8},{12,... | collective-permute-start | bytes 184328 | tf_op jit(solution)/shard_map/ppermute | solution.py:30
  97.7 1.5 %collective-permute-done.24.n1 = bf16[48,640]{1,0:T(8,128)(2,1)S(1)} collective-permute-done((bf16[48,640]{1,0:T(8,128)(2,1)S(1)}, bf16[48,640]{1,0:T(8,128)(2,1)S(1)}, u32[]{:S(2)}, u32[]{:S(2)}) %collective-permute-start.24) | collective-permute-done | bytes 61472 | tf_op jit(solution)/shard_map/ppermute | solution.py:30
  99.9 2.9 %collective-permute-done.26.n2 = bf16[48,640]{1,0:T(8,128)(2,1)S(1)} collective-permute-done((bf16[48,640]{1,0:T(8,128)(2,1)S(1)}, bf16[48,640]{1,0:T(8,128)(2,1)S(1)}, u32[]{:S(2)}, u32[]{:S(2)}) %collective-permute-start.26) | collective-permute-done | bytes 61472 | tf_op jit(solution)/shard_map/ppermute | solution.py:30
  102.8 1.0 shard_map.91
  (58 shorter events, 8.2 us)
Async XLA Ops:
  6.5 9.1 %collective-permute-start = (bf16[48,2432]{1,0:T(8,128)(2,1)}, bf16[48,2432]{1,0:T(8,128)(2,1)S(1)}, u32[]{:S(2)}, u32[]{:S(2)}) collective-permute-start(bf16[48,2432]{1,0:T(8,128)(2,1)} %bitcast.13), channel_id=1, source_target_pairs={{0,128},{128,0},{1,129},{129,1},{2,130},{130,2},{3,131},{131,3},{4... | collective-permute-start | bytes 700424 | tf_op jit(solution)/shard_map/ppermute | solution.py:30
  11.1 11.3 %all-to-all-start = ((bf16[8,24,512]{2,1,0:T(8,128)(2,1)}), bf16[8,24,512]{2,1,0:T(8,128)(2,1)S(1)}, u32[]{:S(2)}, u32[]{:S(2)}) async-start(bf16[8,24,512]{2,1,0:T(8,128)(2,1)} %get-tuple-element.16), calls=%async_computation | async-start | bytes 393216 | tf_op jit(solution)/shard_map/all_to_all | solution.py:345
  15.6 46.4 %all-gather.3.cloned.1.call-start = ((), (), s32[]{:S(2)}) async-start(), calls=%async_computation.1 | async-start | bytes 2101248 | tf_op jit(solution)/shard_map/all_gather | solution.py:363
  15.7 27.0 %copy-start.4 = (bf16[1,1216,19]{1,2,0:T(8,128)(2,1)S(1)}, bf16[1,1216,19]{1,2,0:T(8,128)(2,1)}, u32[]{:S(2)}) copy-start(bf16[1,1216,19]{1,2,0:T(8,128)(2,1)} %param.14) | copy-start | bytes 138628
  15.7 46.2 %copy-start.5 = (f32[3,1,2432]{2,1,0:T(1,128)S(1)}, f32[3,1,2432]{2,1,0:T(1,128)}, u32[]{:S(2)}) copy-start(f32[3,1,2432]{2,1,0:T(1,128)} %get-tuple-element.15.modulation) | copy-start | bytes 87556
  16.4 73.0 %all-gather.5.cloned.1.call-start = ((), (), s32[]{:S(2)}) async-start(), calls=%async_computation.2 | async-start | bytes 1740800 | tf_op jit(solution)/shard_map/all_gather | solution.py:392
  23.5 7.4 %collective-permute-start.1 = (bf16[152,512]{1,0:T(8,128)(2,1)S(1)}, bf16[152,512]{1,0:T(8,128)(2,1)S(1)}, u32[]{:S(2)}, u32[]{:S(2)}) collective-permute-start(bf16[152,512]{1,0:T(8,128)(2,1)S(1)} %get-tuple-element.18.refs_0_.after_ref), channel_id=1, source_target_pairs={{0,64},{64,0},{1,65},{65,1},{2,66},{66,2},{3,67},{67,3},{4,68},{68... | collective-permute-start | bytes 466952 | tf_op jit(solution)/shard_map/ppermute | solution.py:30
  25.0 9.9 %collective-permute-start.2 = (bf16[152,512]{1,0:T(8,128)(2,1)S(1)}, bf16[152,512]{1,0:T(8,128)(2,1)S(1)}, u32[]{:S(2)}, u32[]{:S(2)}) collective-permute-start(bf16[152,512]{1,0:T(8,128)(2,1)S(1)} %get-tuple-element.18.refs_0_.after_ref), channel_id=1, source_target_pairs={{0,8},{8,16},{16,24},{24,32},{32,40},{40,48},{48,56},{56,0},{1,9},... | collective-permute-start | bytes 466952 | tf_op jit(solution)/shard_map/ppermute | solution.py:30
  26.9 8.0 %collective-permute-start.4 = (bf16[152,512]{1,0:T(8,128)(2,1)S(1)}, bf16[152,512]{1,0:T(8,128)(2,1)S(1)}, u32[]{:S(2)}, u32[]{:S(2)}) collective-permute-start(bf16[152,512]{1,0:T(8,128)(2,1)S(1)} %get-tuple-element.18.refs_0_.after_ref), channel_id=1, source_target_pairs={{0,56},{8,0},{16,8},{24,16},{32,24},{40,32},{48,40},{56,48},{1,57}... | collective-permute-start | bytes 466952 | tf_op jit(solution)/shard_map/ppermute | solution.py:30
  30.8 8.1 %collective-permute-start.3 = (bf16[152,512]{1,0:T(8,128)(2,1)S(1)}, bf16[152,512]{1,0:T(8,128)(2,1)S(1)}, u32[]{:S(2)}, u32[]{:S(2)}) collective-permute-start(bf16[152,512]{1,0:T(8,128)(2,1)S(1)} %collective-permute-done.1.refs_1_), channel_id=1, source_target_pairs={{0,56},{8,0},{16,8},{24,16},{32,24},{40,32},{48,40},{56,48},{1,57}... | collective-permute-start | bytes 466952 | tf_op jit(solution)/shard_map/ppermute | solution.py:30
  34.9 12.1 %collective-permute-start.5 = (bf16[152,512]{1,0:T(8,128)(2,1)S(1)}, bf16[152,512]{1,0:T(8,128)(2,1)S(1)}, u32[]{:S(2)}, u32[]{:S(2)}) collective-permute-start(bf16[152,512]{1,0:T(8,128)(2,1)S(1)} %collective-permute-done.1.refs_1_), channel_id=1, source_target_pairs={{0,8},{8,16},{16,24},{24,32},{32,40},{40,48},{48,56},{56,0},{1,9},... | collective-permute-start | bytes 466952 | tf_op jit(solution)/shard_map/ppermute | solution.py:30
  34.9 12.1 %collective-permute-start.6 = (bf16[152,512]{1,0:T(8,128)(2,1)S(1)}, bf16[152,512]{1,0:T(8,128)(2,1)S(1)}, u32[]{:S(2)}, u32[]{:S(2)}) collective-permute-start(bf16[152,512]{1,0:T(8,128)(2,1)S(1)} %collective-permute-done.2.refs_2_), channel_id=1, source_target_pairs={{0,8},{8,16},{16,24},{24,32},{32,40},{40,48},{48,56},{56,0},{1,9},... | collective-permute-start | bytes 466952 | tf_op jit(solution)/shard_map/ppermute | solution.py:30
  34.9 12.1 %collective-permute-start.8 = (bf16[152,512]{1,0:T(8,128)(2,1)S(1)}, bf16[152,512]{1,0:T(8,128)(2,1)S(1)}, u32[]{:S(2)}, u32[]{:S(2)}) collective-permute-start(bf16[152,512]{1,0:T(8,128)(2,1)S(1)} %collective-permute-done.4.refs_4_), channel_id=1, source_target_pairs={{0,56},{8,0},{16,8},{24,16},{32,24},{40,32},{48,40},{56,48},{1,57}... | collective-permute-start | bytes 466952 | tf_op jit(solution)/shard_map/ppermute | solution.py:30
  38.9 8.9 %collective-permute-start.7 = (bf16[152,512]{1,0:T(8,128)(2,1)S(1)}, bf16[152,512]{1,0:T(8,128)(2,1)S(1)}, u32[]{:S(2)}, u32[]{:S(2)}) collective-permute-start(bf16[152,512]{1,0:T(8,128)(2,1)S(1)} %collective-permute-done.3.refs_3_), channel_id=1, source_target_pairs={{0,56},{8,0},{16,8},{24,16},{32,24},{40,32},{48,40},{56,48},{1,57}... | collective-permute-start | bytes 466952 | tf_op jit(solution)/shard_map/ppermute | solution.py:30
  42.7 4.3 %collective-permute-start.23 = (bf16[19,1216]{1,0:T(8,128)(2,1)S(1)}, bf16[19,1216]{1,0:T(8,128)(2,1)S(1)}, u32[]{:S(2)}, u32[]{:S(2)}) collective-permute-start(bf16[19,1216]{1,0:T(8,128)(2,1)S(1)} %shard_map.87), channel_id=1, source_target_pairs={{0,64},{64,0},{1,65},{65,1},{2,66},{66,2},{3,67},{67,3},{4,68},{68... | collective-permute-start | bytes 138632 | tf_op jit(solution)/shard_map/ppermute | solution.py:30
  47.7 8.1 %collective-permute-start.9 = (bf16[152,512]{1,0:T(8,128)(2,1)S(1)}, bf16[152,512]{1,0:T(8,128)(2,1)S(1)}, u32[]{:S(2)}, u32[]{:S(2)}) collective-permute-start(bf16[152,512]{1,0:T(8,128)(2,1)S(1)} %collective-permute-done.5.refs_5_.refs_2_), channel_id=1, source_target_pairs={{0,8},{8,16},{16,24},{24,32},{32,40},{40,48},{48,56},{56,0},{1,9},... | collective-permute-start | bytes 466952 | tf_op jit(solution)/shard_map/ppermute | solution.py:30
  47.8 10.9 %collective-permute-start.10 = (bf16[152,512]{1,0:T(8,128)(2,1)S(1)}, bf16[152,512]{1,0:T(8,128)(2,1)S(1)}, u32[]{:S(2)}, u32[]{:S(2)}) collective-permute-start(bf16[152,512]{1,0:T(8,128)(2,1)S(1)} %collective-permute-done.6.refs_6_.refs_0_), channel_id=1, source_target_pairs={{0,8},{8,16},{16,24},{24,32},{32,40},{40,48},{48,56},{56,0},{1,9},... | collective-permute-start | bytes 466952 | tf_op jit(solution)/shard_map/ppermute | solution.py:30
  47.9 10.8 %collective-permute-start.11 = (bf16[152,512]{1,0:T(8,128)(2,1)S(1)}, bf16[152,512]{1,0:T(8,128)(2,1)S(1)}, u32[]{:S(2)}, u32[]{:S(2)}) collective-permute-start(bf16[152,512]{1,0:T(8,128)(2,1)S(1)} %collective-permute-done.7.refs_7_), channel_id=1, source_target_pairs={{0,56},{8,0},{16,8},{24,16},{32,24},{40,32},{48,40},{56,48},{1,57}... | collective-permute-start | bytes 466952 | tf_op jit(solution)/shard_map/ppermute | solution.py:30
  51.1 15.0 %collective-permute-start.12 = (bf16[152,512]{1,0:T(8,128)(2,1)S(1)}, bf16[152,512]{1,0:T(8,128)(2,1)S(1)}, u32[]{:S(2)}, u32[]{:S(2)}) collective-permute-start(bf16[152,512]{1,0:T(8,128)(2,1)S(1)} %collective-permute-done.8.refs_8_.refs_1_), channel_id=1, source_target_pairs={{0,56},{8,0},{16,8},{24,16},{32,24},{40,32},{48,40},{56,48},{1,57}... | collective-permute-start | bytes 466952 | tf_op jit(solution)/shard_map/ppermute | solution.py:30
  55.8 10.4 %collective-permute-start.13 = (bf16[152,512]{1,0:T(8,128)(2,1)S(1)}, bf16[152,512]{1,0:T(8,128)(2,1)S(1)}, u32[]{:S(2)}, u32[]{:S(2)}) collective-permute-start(bf16[152,512]{1,0:T(8,128)(2,1)S(1)} %collective-permute-done.9.refs_9_), channel_id=1, source_target_pairs={{0,8},{8,16},{16,24},{24,32},{32,40},{40,48},{48,56},{56,0},{1,9},... | collective-permute-start | bytes 466952 | tf_op jit(solution)/shard_map/ppermute | solution.py:30
  58.7 7.5 %collective-permute-start.14 = (bf16[152,512]{1,0:T(8,128)(2,1)S(1)}, bf16[152,512]{1,0:T(8,128)(2,1)S(1)}, u32[]{:S(2)}, u32[]{:S(2)}) collective-permute-start(bf16[152,512]{1,0:T(8,128)(2,1)S(1)} %collective-permute-done.10.refs_10_), channel_id=1, source_target_pairs={{0,8},{8,16},{16,24},{24,32},{32,40},{40,48},{48,56},{56,0},{1,9},... | collective-permute-start | bytes 466952 | tf_op jit(solution)/shard_map/ppermute | solution.py:30
  58.7 7.5 %collective-permute-start.15 = (bf16[152,512]{1,0:T(8,128)(2,1)S(1)}, bf16[152,512]{1,0:T(8,128)(2,1)S(1)}, u32[]{:S(2)}, u32[]{:S(2)}) collective-permute-start(bf16[152,512]{1,0:T(8,128)(2,1)S(1)} %collective-permute-done.11.refs_11_), channel_id=1, source_target_pairs={{0,56},{8,0},{16,8},{24,16},{32,24},{40,32},{48,40},{56,48},{1,57}... | collective-permute-start | bytes 466952 | tf_op jit(solution)/shard_map/ppermute | solution.py:30
  68.2 8.0 %collective-permute-start.18 = (bf16[1120,128]{1,0:T(8,128)(2,1)S(1)}, bf16[1120,128]{1,0:T(8,128)(2,1)S(1)}, u32[]{:S(2)}, u32[]{:S(2)}) collective-permute-start(bf16[1120,128]{1,0:T(8,128)(2,1)S(1)} %get-tuple-element.19.own), channel_id=1, source_target_pairs={{0,8},{8,0},{1,9},{9,1},{2,10},{10,2},{3,11},{11,3},{4,12},{12,4},... | collective-permute-start | bytes 860168 | tf_op jit(solution)/shard_map/ppermute | solution.py:30
  68.3 9.8 %collective-permute-start.16 = (bf16[1120,128]{1,0:T(8,128)(2,1)S(1)}, bf16[1120,128]{1,0:T(8,128)(2,1)S(1)}, u32[]{:S(2)}, u32[]{:S(2)}) collective-permute-start(bf16[1120,128]{1,0:T(8,128)(2,1)S(1)} %get-tuple-element.19.own), channel_id=1, source_target_pairs={{0,1},{1,0},{2,3},{3,2},{4,5},{5,4},{6,7},{7,6},{8,9},{9,8},{10,11... | collective-permute-start | bytes 860168 | tf_op jit(solution)/shard_map/ppermute | solution.py:30
  76.2 1.9 %collective-permute-start.19 = (bf16[1120,128]{1,0:T(8,128)(2,1)S(1)}, bf16[1120,128]{1,0:T(8,128)(2,1)S(1)}, u32[]{:S(2)}, u32[]{:S(2)}) collective-permute-start(bf16[1120,128]{1,0:T(8,128)(2,1)S(1)} %collective-permute-done.18.far), channel_id=1, source_target_pairs={{0,1},{1,0},{2,3},{3,2},{4,5},{5,4},{6,7},{7,6},{8,9},{9,8},{10,11... | collective-permute-start | bytes 860168 | tf_op jit(solution)/shard_map/ppermute | solution.py:30
  76.2 1.9 %collective-permute-start.17 = (bf16[384,192]{1,0:T(8,128)(2,1)S(1)}, bf16[384,192]{1,0:T(8,128)(2,1)S(1)}, u32[]{:S(2)}, u32[]{:S(2)}) collective-permute-start(bf16[384,192]{1,0:T(8,128)(2,1)S(1)} %get-tuple-element.20.own_q), channel_id=1, source_target_pairs={{0,1},{1,0},{2,3},{3,2},{4,5},{5,4},{6,7},{7,6},{8,9},{9,8},{10,11... | collective-permute-start | bytes 442376 | tf_op jit(solution)/shard_map/ppermute | solution.py:30
  81.2 9.3 %collective-permute-start.20 = (bf16[480,128]{1,0:T(8,128)(2,1)S(1)}, bf16[480,128]{1,0:T(8,128)(2,1)S(1)}, u32[]{:S(2)}, u32[]{:S(2)}) collective-permute-start(bf16[480,128]{1,0:T(8,128)(2,1)S(1)} %shard_map.86.a0), channel_id=1, source_target_pairs={{0,2},{2,4},{4,6},{6,0},{1,3},{3,5},{5,7},{7,1},{8,10},{10,12},{12... | collective-permute-start | bytes 368648 | tf_op jit(solution)/shard_map/ppermute | solution.py:30
  81.8 8.7 %collective-permute-start.21 = (bf16[480,128]{1,0:T(8,128)(2,1)S(1)}, bf16[480,128]{1,0:T(8,128)(2,1)S(1)}, u32[]{:S(2)}, u32[]{:S(2)}) collective-permute-start(bf16[480,128]{1,0:T(8,128)(2,1)S(1)} %shard_map.86.a0), channel_id=1, source_target_pairs={{0,4},{2,6},{4,0},{6,2},{1,5},{3,7},{5,1},{7,3},{8,12},{10,14},{12... | collective-permute-start | bytes 368648 | tf_op jit(solution)/shard_map/ppermute | solution.py:30
  84.2 6.9 %collective-permute-start.22 = (bf16[480,128]{1,0:T(8,128)(2,1)S(1)}, bf16[480,128]{1,0:T(8,128)(2,1)S(1)}, u32[]{:S(2)}, u32[]{:S(2)}) collective-permute-start(bf16[480,128]{1,0:T(8,128)(2,1)S(1)} %shard_map.86.a0), channel_id=1, source_target_pairs={{0,6},{2,0},{4,2},{6,4},{1,7},{3,1},{5,3},{7,5},{8,14},{10,8},{12,... | collective-permute-start | bytes 368648 | tf_op jit(solution)/shard_map/ppermute | solution.py:30
  93.5 5.7 %collective-permute-start.24 = (bf16[48,640]{1,0:T(8,128)(2,1)S(1)}, bf16[48,640]{1,0:T(8,128)(2,1)S(1)}, u32[]{:S(2)}, u32[]{:S(2)}) collective-permute-start(bf16[48,640]{1,0:T(8,128)(2,1)S(1)} %get-tuple-element.22), channel_id=1, source_target_pairs={{0,2},{2,4},{4,6},{6,0},{1,3},{3,5},{5,7},{7,1},{8,10},{10,12},{12... | collective-permute-start | bytes 184328 | tf_op jit(solution)/shard_map/ppermute | solution.py:30
  94.1 5.2 %collective-permute-start.25 = (bf16[48,640]{1,0:T(8,128)(2,1)S(1)}, bf16[48,640]{1,0:T(8,128)(2,1)S(1)}, u32[]{:S(2)}, u32[]{:S(2)}) collective-permute-start(bf16[48,640]{1,0:T(8,128)(2,1)S(1)} %get-tuple-element.23), channel_id=1, source_target_pairs={{0,6},{2,0},{4,2},{6,4},{1,7},{3,1},{5,3},{7,5},{8,14},{10,8},{12,... | collective-permute-start | bytes 184328 | tf_op jit(solution)/shard_map/ppermute | solution.py:30
  97.0 5.7 %collective-permute-start.26 = (bf16[48,640]{1,0:T(8,128)(2,1)S(1)}, bf16[48,640]{1,0:T(8,128)(2,1)S(1)}, u32[]{:S(2)}, u32[]{:S(2)}) collective-permute-start(bf16[48,640]{1,0:T(8,128)(2,1)S(1)} %get-tuple-element.24), channel_id=1, source_target_pairs={{0,4},{2,6},{4,0},{6,2},{1,5},{3,7},{5,1},{7,3},{8,12},{10,14},{12... | collective-permute-start | bytes 184328 | tf_op jit(solution)/shard_map/ppermute | solution.py:30
  (7 other events, 22.7 us)
Sparse Core Ops, SparseCore 0:
  18.2 29.6 all-gather.2
  49.7 39.5 all-gather.4

commit v7 on v4

--- a/solution.py
+++ b/solution.py
@@ -287,19 +287,27 @@
         out_ref[...] = result[lax.rem(y + by, 4)]
 
 
-def assemble_kernel(modulation, raw_ref, n0, n1, n2, n3, out_ref, branch):
+def place_columns(part, by, branch):
     y = lax.axis_index("y")
-    run = n0.shape[1] // 16
-    for by, part in enumerate((n0, n1, n2, n3)):
-        value = part[...].astype(F32)
-        for q in range(4):
-
-            @pl.when(lax.rem(y + 4 - by, 4) == q)
-            def _():
-                for m in range(16):
-                    at = (m * 4 + q) * run
-                    branch[:, at : at + run] = value[:, m * run : (m + 1) * run]
-
+    run = part.shape[1] // 16
+    value = part[...].astype(F32)
+    for q in range(4):
+
+        @pl.when(lax.rem(y + 4 - by, 4) == q)
+        def _():
+            for m in range(16):
+                at = (m * 4 + q) * run
+                branch[:, at : at + run] = value[:, m * run : (m + 1) * run]
+
+
+def assemble_early_kernel(n0, n1, n3, branch):
+    for by, part in ((0, n0), (1, n1), (3, n3)):
+        place_columns(part, by, branch)
+
+
+def assemble_kernel(modulation, raw_ref, early_ref, n2, out_ref, branch):
+    branch[...] = early_ref[...]
+    place_columns(n2, 2, branch)
     out_ref[...] = (raw_ref[...].astype(F32) + modulation[2] * branch[...]).astype(BF16)
 
 
@@ -439,10 +447,16 @@
         ],
     )
     parts = [parts[0]] + [permuted(parts[by], "y", by) for by in (1, 2, 3)]
+    early = in_vmem(
+        assemble_early_kernel,
+        jax.ShapeDtypeStruct((rows, width), F32),
+        (parts[0], parts[1], parts[3]),
+        flops=10**10,
+    )
     new = in_vmem(
         assemble_kernel,
         jax.ShapeDtypeStruct((rows, width), BF16),
-        (modulation, raw, *parts),
+        (modulation, raw, early, parts[2]),
         scratch=[pltpu.VMEM((rows, width), F32)],
     )
     return new[None]

time: 110 us -> 110 us (level)
    pallas_call x10 -> x11, Pallas kernels: 13.2 us -> 13.2 us  [in_vmem(): pl.pallas_call(kernel, out_shape=out_shape, in_specs=[pl.BlockSpec(memory...]
  transfers between devices with their start and end apart: 30 -> 30, of which waited for: 17 -> 18; matrix products, arithmetic and copies ran while one was open for 0% -> 0% of each run, Pallas kernels for 10% -> 10%
where the time goes in v7:
time: 110 us; the launch traced here: 109 us
  waiting for transfers between devices  40.1 us (36%)
  starting transfers between devices  38.7 us (35%)
  between operations  13.5 us (12%)
  Pallas kernels  13.2 us (12%)
  local copies, waits for them, and re-layouts  3.75 us (3%)
    ppermute x27, starting transfers between devices, permuted(): lax.ppermute(array, axis, [(i, (i + by) % devices) for i in range(devices)])  34.1 us
    ppermute x27, waiting for transfers between devices, permuted(): lax.ppermute(array, axis, [(i, (i + by) % devices) for i in range(devices)])  28.1 us
    pallas_call x11, Pallas kernels, in_vmem(): pl.pallas_call(kernel, out_shape=out_shape, in_specs=[pl.BlockSpec(memory...  13.2 us
    all_gather x1, waiting for transfers between devices, per_device(): out_columns = lax.all_gather(both, ('core', 'z1', 'z0'), axis=0, tiled=True)  7.27 us
    all_to_all x1, waiting for transfers between devices, per_device(): lax.all_to_all(halves, ('y', 'core'), split_axis=0, concat_axis=0, tiled=...  4.72 us
    all_to_all x1, starting transfers between devices, per_device(): lax.all_to_all(halves, ('y', 'core'), split_axis=0, concat_axis=0, tiled=...  4.48 us
    unnamed x14, local copies, waits for them, and re-layouts  3.75 us
  transfers between devices with their start and end apart: 30, of which 18 were waited for; matrix products, arithmetic and copies ran while one was open for 0% of the time, Pallas kernels for 10%

profile of v7, /device:TPU:2, one launch (start us, length us, event | category | flops | bytes accessed | tf_op | source)
XLA Modules:
  0.0 109.3 jit_solution(3834148916229990377)
XLA Ops:
  6.5 2.1 %collective-permute-start = (bf16[48,2432]{1,0:T(8,128)(2,1)}, bf16[48,2432]{1,0:T(8,128)(2,1)S(1)}, u32[]{:S(2)}, u32[]{:S(2)}) collective-permute-start(bf16[48,2432]{1,0:T(8,128)(2,1)} %bitcast.13), channel_id=1, source_target_pairs={{0,128},{128,0},{1,129},{129,1},{2,130},{130,2},{3,131},{131,3},{4... | collective-permute-start | bytes 700424 | tf_op jit(solution)/shard_map/ppermute | solution.py:30
  8.7 2.4 %shard_map.82 = (bf16[8,24,512]{2,1,0:T(8,128)(2,1)}, f32[3,1,2432]{2,1,0:T(1,128)}) custom-call(s32[8]{0:T(128)} %steps_ref.1, bf16[19,3648]{1,0:T(8,128)(2,1)} %bitcast.12, bf16[2,8,1216]{2,1,0:T(8,128)(2,1)} %text_ref.1, f32[28,3,1,2432]{3,2,1,0:T(1,128)} %bitcast.11), custom_call_target="tpu_custom_call" | custom-call | bytes 177568 | tf_op jit(solution)/shard_map/pallas_call | solution.py:317
  11.1 4.5 %all-to-all-start = ((bf16[8,24,512]{2,1,0:T(8,128)(2,1)}), bf16[8,24,512]{2,1,0:T(8,128)(2,1)S(1)}, u32[]{:S(2)}, u32[]{:S(2)}) async-start(bf16[8,24,512]{2,1,0:T(8,128)(2,1)} %get-tuple-element.16), calls=%async_computation | async-start | bytes 393216 | tf_op jit(solution)/shard_map/all_to_all | solution.py:349
  16.4 1.1 %shard_map.83.refs_0_ = bf16[48,2560]{1,0:T(8,128)(2,1)} custom-call(f32[3,1,2432]{2,1,0:T(1,128)S(1)} %copy-done.2, bf16[48,2432]{1,0:T(8,128)(2,1)S(1)} %collective-permute-done.raw_ref), custom_call_target="tpu_custom_call" | custom-call | bytes 262656 | tf_op jit(solution)/shard_map/pallas_call | solution.py:317
  17.7 4.7 %all-to-all-done.received_ref = bf16[8,24,512]{2,1,0:T(8,128)(2,1)S(1)} async-done(((bf16[8,24,512]{2,1,0:T(8,128)(2,1)}), bf16[8,24,512]{2,1,0:T(8,128)(2,1)S(1)}, u32[]{:S(2)}, u32[]{:S(2)}) %all-to-all-start) | async-done | bytes 196640 | tf_op jit(solution)/shard_map/all_to_all | solution.py:349
  23.5 1.5 %collective-permute-start.1 = (bf16[152,512]{1,0:T(8,128)(2,1)S(1)}, bf16[152,512]{1,0:T(8,128)(2,1)S(1)}, u32[]{:S(2)}, u32[]{:S(2)}) collective-permute-start(bf16[152,512]{1,0:T(8,128)(2,1)S(1)} %get-tuple-element.18.refs_0_.after_ref), channel_id=1, source_target_pairs={{0,64},{64,0},{1,65},{65,1},{2,66},{66,2},{3,67},{67,3},{4,68},{68... | collective-permute-start | bytes 466952 | tf_op jit(solution)/shard_map/ppermute | solution.py:30
  25.0 1.9 %collective-permute-start.2 = (bf16[152,512]{1,0:T(8,128)(2,1)S(1)}, bf16[152,512]{1,0:T(8,128)(2,1)S(1)}, u32[]{:S(2)}, u32[]{:S(2)}) collective-permute-start(bf16[152,512]{1,0:T(8,128)(2,1)S(1)} %get-tuple-element.18.refs_0_.after_ref), channel_id=1, source_target_pairs={{0,8},{8,16},{16,24},{24,32},{32,40},{40,48},{48,56},{56,0},{1,9},... | collective-permute-start | bytes 466952 | tf_op jit(solution)/shard_map/ppermute | solution.py:30
  26.9 3.9 %collective-permute-start.4 = (bf16[152,512]{1,0:T(8,128)(2,1)S(1)}, bf16[152,512]{1,0:T(8,128)(2,1)S(1)}, u32[]{:S(2)}, u32[]{:S(2)}) collective-permute-start(bf16[152,512]{1,0:T(8,128)(2,1)S(1)} %get-tuple-element.18.refs_0_.after_ref), channel_id=1, source_target_pairs={{0,56},{8,0},{16,8},{24,16},{32,24},{40,32},{48,40},{56,48},{1,57}... | collective-permute-start | bytes 466952 | tf_op jit(solution)/shard_map/ppermute | solution.py:30
  30.8 4.0 %collective-permute-start.3 = (bf16[152,512]{1,0:T(8,128)(2,1)S(1)}, bf16[152,512]{1,0:T(8,128)(2,1)S(1)}, u32[]{:S(2)}, u32[]{:S(2)}) collective-permute-start(bf16[152,512]{1,0:T(8,128)(2,1)S(1)} %collective-permute-done.1.refs_1_), channel_id=1, source_target_pairs={{0,56},{8,0},{16,8},{24,16},{32,24},{40,32},{48,40},{56,48},{1,57}... | collective-permute-start | bytes 466952 | tf_op jit(solution)/shard_map/ppermute | solution.py:30
  34.9 3.3 %collective-permute-start.8 = (bf16[152,512]{1,0:T(8,128)(2,1)S(1)}, bf16[152,512]{1,0:T(8,128)(2,1)S(1)}, u32[]{:S(2)}, u32[]{:S(2)}) collective-permute-start(bf16[152,512]{1,0:T(8,128)(2,1)S(1)} %collective-permute-done.4.refs_4_), channel_id=1, source_target_pairs={{0,56},{8,0},{16,8},{24,16},{32,24},{40,32},{48,40},{56,48},{1,57}... | collective-permute-start | bytes 466952 | tf_op jit(solution)/shard_map/ppermute | solution.py:30
  38.2 1.5 %collective-permute-start.23 = (bf16[19,1216]{1,0:T(8,128)(2,1)S(1)}, bf16[19,1216]{1,0:T(8,128)(2,1)S(1)}, u32[]{:S(2)}, u32[]{:S(2)}) collective-permute-start(bf16[19,1216]{1,0:T(8,128)(2,1)S(1)} %shard_map.87), channel_id=1, source_target_pairs={{0,64},{64,0},{1,65},{65,1},{2,66},{66,2},{3,67},{67,3},{4,68},{68... | collective-permute-start | bytes 138632 | tf_op jit(solution)/shard_map/ppermute | solution.py:30
  39.7 2.8 %collective-permute-done.23.other_ref = bf16[19,1216]{1,0:T(8,128)(2,1)S(1)} collective-permute-done((bf16[19,1216]{1,0:T(8,128)(2,1)S(1)}, bf16[19,1216]{1,0:T(8,128)(2,1)S(1)}, u32[]{:S(2)}, u32[]{:S(2)}) %collective-permute-start.23) | collective-permute-done | bytes 46240 | tf_op jit(solution)/shard_map/ppermute | solution.py:30
  42.5 1.2 %collective-permute-done.6.refs_6_.refs_0_ = bf16[152,512]{1,0:T(8,128)(2,1)S(1)} collective-permute-done((bf16[152,512]{1,0:T(8,128)(2,1)S(1)}, bf16[152,512]{1,0:T(8,128)(2,1)S(1)}, u32[]{:S(2)}, u32[]{:S(2)}) %collective-permute-start.6) | collective-permute-done | bytes 155680 | tf_op jit(solution)/shard_map/ppermute | solution.py:30
  46.6 3.8 %collective-permute-done.7.refs_7_ = bf16[152,512]{1,0:T(8,128)(2,1)S(1)} collective-permute-done((bf16[152,512]{1,0:T(8,128)(2,1)S(1)}, bf16[152,512]{1,0:T(8,128)(2,1)S(1)}, u32[]{:S(2)}, u32[]{:S(2)}) %collective-permute-start.7) | collective-permute-done | bytes 155680 | tf_op jit(solution)/shard_map/ppermute | solution.py:30
  50.4 1.5 %collective-permute-start.11 = (bf16[152,512]{1,0:T(8,128)(2,1)S(1)}, bf16[152,512]{1,0:T(8,128)(2,1)S(1)}, u32[]{:S(2)}, u32[]{:S(2)}) collective-permute-start(bf16[152,512]{1,0:T(8,128)(2,1)S(1)} %collective-permute-done.7.refs_7_), channel_id=1, source_target_pairs={{0,56},{8,0},{16,8},{24,16},{32,24},{40,32},{48,40},{56,48},{1,57}... | collective-permute-start | bytes 466952 | tf_op jit(solution)/shard_map/ppermute | solution.py:30
  52.4 1.5 %collective-permute-start.13 = (bf16[152,512]{1,0:T(8,128)(2,1)S(1)}, bf16[152,512]{1,0:T(8,128)(2,1)S(1)}, u32[]{:S(2)}, u32[]{:S(2)}) collective-permute-start(bf16[152,512]{1,0:T(8,128)(2,1)S(1)} %collective-permute-done.9.refs_9_), channel_id=1, source_target_pairs={{0,8},{8,16},{16,24},{24,32},{32,40},{40,48},{48,56},{56,0},{1,9},... | collective-permute-start | bytes 466952 | tf_op jit(solution)/shard_map/ppermute | solution.py:30
  53.9 1.1 %collective-permute-done.10.refs_10_ = bf16[152,512]{1,0:T(8,128)(2,1)S(1)} collective-permute-done((bf16[152,512]{1,0:T(8,128)(2,1)S(1)}, bf16[152,512]{1,0:T(8,128)(2,1)S(1)}, u32[]{:S(2)}, u32[]{:S(2)}) %collective-permute-start.10) | collective-permute-done | bytes 155680 | tf_op jit(solution)/shard_map/ppermute | solution.py:30
  55.0 2.0 %collective-permute-done.11.refs_11_ = bf16[152,512]{1,0:T(8,128)(2,1)S(1)} collective-permute-done((bf16[152,512]{1,0:T(8,128)(2,1)S(1)}, bf16[152,512]{1,0:T(8,128)(2,1)S(1)}, u32[]{:S(2)}, u32[]{:S(2)}) %collective-permute-start.11) | collective-permute-done | bytes 155680 | tf_op jit(solution)/shard_map/ppermute | solution.py:30
  57.0 1.3 %collective-permute-start.15 = (bf16[152,512]{1,0:T(8,128)(2,1)S(1)}, bf16[152,512]{1,0:T(8,128)(2,1)S(1)}, u32[]{:S(2)}, u32[]{:S(2)}) collective-permute-start(bf16[152,512]{1,0:T(8,128)(2,1)S(1)} %collective-permute-done.11.refs_11_), channel_id=1, source_target_pairs={{0,56},{8,0},{16,8},{24,16},{32,24},{40,32},{48,40},{56,48},{1,57}... | collective-permute-start | bytes 466952 | tf_op jit(solution)/shard_map/ppermute | solution.py:30
  59.1 2.4 %collective-permute-done.14.refs_14_ = bf16[152,512]{1,0:T(8,128)(2,1)S(1)} collective-permute-done((bf16[152,512]{1,0:T(8,128)(2,1)S(1)}, bf16[152,512]{1,0:T(8,128)(2,1)S(1)}, u32[]{:S(2)}, u32[]{:S(2)}) %collective-permute-start.14) | collective-permute-done | bytes 155680 | tf_op jit(solution)/shard_map/ppermute | solution.py:30
  62.3 1.5 %copy-done = bf16[384,2560]{1,0:T(8,128)(2,1)S(1)} copy-done((bf16[384,2560]{1,0:T(8,128)(2,1)S(1)}, bf16[384,2560]{1,0:T(8,128)(2,1)}, u32[]{:S(2)}) %copy-start) | copy-done | bytes 1966104
  63.8 2.0 %shard_map.85 = (bf16[1120,128]{1,0:T(8,128)(2,1)S(1)}, bf16[384,192]{1,0:T(8,128)(2,1)S(1)}) custom-call(f32[2,1216]{1,0:T(2,128)S(1)} %bitcast.10, bf16[384,2560]{1,0:T(8,128)(2,1)S(1)} %copy-done, bf16[64,320]{1,0:T(8,128)(2,1)S(1)} %get-tuple-element.17.text_ref, bf16[152,512]{1,0:T(8,128)(2,1)S(1)} %get-tuple-element.18.refs_0_.after_ref, ...), custom_call_target="tpu_custom_call" | custom-call | flops 1006632960 | bytes 4507136 | tf_op jit(solution)/shard_map/pallas_call | solution.py:317
  66.2 7.7 %collective-permute-done.18.far = bf16[1120,128]{1,0:T(8,128)(2,1)S(1)} collective-permute-done((bf16[1120,128]{1,0:T(8,128)(2,1)S(1)}, bf16[1120,128]{1,0:T(8,128)(2,1)S(1)}, u32[]{:S(2)}, u32[]{:S(2)}) %collective-permute-start.18) | collective-permute-done | bytes 286752 | tf_op jit(solution)/shard_map/ppermute | solution.py:30
  74.4 1.4 %collective-permute-done.17.beside_q = bf16[384,192]{1,0:T(8,128)(2,1)S(1)} collective-permute-done((bf16[384,192]{1,0:T(8,128)(2,1)S(1)}, bf16[384,192]{1,0:T(8,128)(2,1)S(1)}, u32[]{:S(2)}, u32[]{:S(2)}) %collective-permute-start.17) | collective-permute-done | bytes 147488 | tf_op jit(solution)/shard_map/ppermute | solution.py:30
  75.8 3.1 %shard_map.86.a0 = bf16[480,128]{1,0:T(8,128)(2,1)S(1)} custom-call(s32[8]{0:T(128)S(1)} %copy-done.5, bf16[1120,128]{1,0:T(8,128)(2,1)S(1)} %get-tuple-element.19.own, bf16[1120,128]{1,0:T(8,128)(2,1)S(1)} %collective-permute-done.16.beside, bf16[384,192]{1,0:T(8,128)(2,1)S(1)} %get-tuple-element.20.own_q, ...), custom_call_target="tpu_custom_call" | custom-call | flops 220200960 | bytes 1441824 | tf_op jit(solution)/shard_map/pallas_call | solution.py:317
  79.5 1.7 %collective-permute-start.21 = (bf16[480,128]{1,0:T(8,128)(2,1)S(1)}, bf16[480,128]{1,0:T(8,128)(2,1)S(1)}, u32[]{:S(2)}, u32[]{:S(2)}) collective-permute-start(bf16[480,128]{1,0:T(8,128)(2,1)S(1)} %shard_map.86.a0), channel_id=1, source_target_pairs={{0,4},{2,6},{4,0},{6,2},{1,5},{3,7},{5,1},{7,3},{8,12},{10,14},{12... | collective-permute-start | bytes 368648 | tf_op jit(solution)/shard_map/ppermute | solution.py:30
  82.2 7.3 %all-gather.5.cloned.1.call-done.gathered_ref = bf16[640,1216]{1,0:T(8,128)(2,1)} async-done(((bf16[40,1216]{1,0:T(8,128)(2,1)}), bf16[640,1216]{1,0:T(8,128)(2,1)}) %all-gather.5.cloned.1.call-update) | async-done | bytes 1556496 | tf_op jit(solution)/shard_map/all_gather | solution.py:394
  89.5 1.4 %copy-done.6 = bf16[640,1216]{1,0:T(8,128)(2,1)S(1)} copy-done((bf16[640,1216]{1,0:T(8,128)(2,1)S(1)}, bf16[640,1216]{1,0:T(8,128)(2,1)}, u32[]{:S(2)}) %copy-start.6) | copy-done | bytes 1556504
  92.5 1.5 %collective-permute-start.24 = (bf16[48,608]{1,0:T(8,128)(2,1)S(1)}, bf16[48,608]{1,0:T(8,128)(2,1)S(1)}, u32[]{:S(2)}, u32[]{:S(2)}) collective-permute-start(bf16[48,608]{1,0:T(8,128)(2,1)S(1)} %get-tuple-element.22), channel_id=1, source_target_pairs={{0,2},{2,4},{4,6},{6,0},{1,3},{3,5},{5,7},{7,1},{8,10},{10,12},{12... | collective-permute-start | bytes 175112 | tf_op jit(solution)/shard_map/ppermute | solution.py:30
  94.0 1.8 %collective-permute-start.25 = (bf16[48,608]{1,0:T(8,128)(2,1)S(1)}, bf16[48,608]{1,0:T(8,128)(2,1)S(1)}, u32[]{:S(2)}, u32[]{:S(2)}) collective-permute-start(bf16[48,608]{1,0:T(8,128)(2,1)S(1)} %get-tuple-element.23), channel_id=1, source_target_pairs={{0,6},{2,0},{4,2},{6,4},{1,7},{3,1},{5,3},{7,5},{8,14},{10,8},{12,... | collective-permute-start | bytes 175112 | tf_op jit(solution)/shard_map/ppermute | solution.py:30
  95.8 1.7 %collective-permute-start.26 = (bf16[48,608]{1,0:T(8,128)(2,1)S(1)}, bf16[48,608]{1,0:T(8,128)(2,1)S(1)}, u32[]{:S(2)}, u32[]{:S(2)}) collective-permute-start(bf16[48,608]{1,0:T(8,128)(2,1)S(1)} %get-tuple-element.24), channel_id=1, source_target_pairs={{0,4},{2,6},{4,0},{6,2},{1,5},{3,7},{5,1},{7,3},{8,12},{10,14},{12... | collective-permute-start | bytes 175112 | tf_op jit(solution)/shard_map/ppermute | solution.py:30
  98.7 2.8 %collective-permute-done.26.n2 = bf16[48,608]{1,0:T(8,128)(2,1)S(1)} collective-permute-done((bf16[48,608]{1,0:T(8,128)(2,1)S(1)}, bf16[48,608]{1,0:T(8,128)(2,1)S(1)}, u32[]{:S(2)}, u32[]{:S(2)}) %collective-permute-start.26) | collective-permute-done | bytes 58400 | tf_op jit(solution)/shard_map/ppermute | solution.py:30
  (55 shorter events, 13.2 us)
Async XLA Ops:
  6.5 9.1 %collective-permute-start = (bf16[48,2432]{1,0:T(8,128)(2,1)}, bf16[48,2432]{1,0:T(8,128)(2,1)S(1)}, u32[]{:S(2)}, u32[]{:S(2)}) collective-permute-start(bf16[48,2432]{1,0:T(8,128)(2,1)} %bitcast.13), channel_id=1, source_target_pairs={{0,128},{128,0},{1,129},{129,1},{2,130},{130,2},{3,131},{131,3},{4... | collective-permute-start | bytes 700424 | tf_op jit(solution)/shard_map/ppermute | solution.py:30
  11.1 11.3 %all-to-all-start = ((bf16[8,24,512]{2,1,0:T(8,128)(2,1)}), bf16[8,24,512]{2,1,0:T(8,128)(2,1)S(1)}, u32[]{:S(2)}, u32[]{:S(2)}) async-start(bf16[8,24,512]{2,1,0:T(8,128)(2,1)} %get-tuple-element.16), calls=%async_computation | async-start | bytes 393216 | tf_op jit(solution)/shard_map/all_to_all | solution.py:349
  15.5 46.7 %all-gather.3.cloned.1.call-start = ((), (), s32[]{:S(2)}) async-start(), calls=%async_computation.1 | async-start | bytes 2211840 | tf_op jit(solution)/shard_map/all_gather | solution.py:367
  17.6 20.6 %copy-start.1 = (bf16[1,1216,19]{1,2,0:T(8,128)(2,1)S(1)}, bf16[1,1216,19]{1,2,0:T(8,128)(2,1)}, u32[]{:S(2)}) copy-start(bf16[1,1216,19]{1,2,0:T(8,128)(2,1)} %param.14) | copy-start | bytes 138628
  17.6 44.7 %copy-start.4 = (f32[1,2,1216]{2,1,0:T(2,128)S(1)}, f32[1,2,1216]{2,1,0:T(2,128)}, u32[]{:S(2)}) copy-start(f32[1,2,1216]{2,1,0:T(2,128)} %param.15) | copy-start | bytes 29188
  17.6 71.9 %all-gather.5.cloned.1.call-start = ((), (), s32[]{:S(2)}) async-start(), calls=%async_computation.2 | async-start | bytes 1740800 | tf_op jit(solution)/shard_map/all_gather | solution.py:394
  23.5 7.4 %collective-permute-start.1 = (bf16[152,512]{1,0:T(8,128)(2,1)S(1)}, bf16[152,512]{1,0:T(8,128)(2,1)S(1)}, u32[]{:S(2)}, u32[]{:S(2)}) collective-permute-start(bf16[152,512]{1,0:T(8,128)(2,1)S(1)} %get-tuple-element.18.refs_0_.after_ref), channel_id=1, source_target_pairs={{0,64},{64,0},{1,65},{65,1},{2,66},{66,2},{3,67},{67,3},{4,68},{68... | collective-permute-start | bytes 466952 | tf_op jit(solution)/shard_map/ppermute | solution.py:30
  25.0 9.9 %collective-permute-start.2 = (bf16[152,512]{1,0:T(8,128)(2,1)S(1)}, bf16[152,512]{1,0:T(8,128)(2,1)S(1)}, u32[]{:S(2)}, u32[]{:S(2)}) collective-permute-start(bf16[152,512]{1,0:T(8,128)(2,1)S(1)} %get-tuple-element.18.refs_0_.after_ref), channel_id=1, source_target_pairs={{0,8},{8,16},{16,24},{24,32},{32,40},{40,48},{48,56},{56,0},{1,9},... | collective-permute-start | bytes 466952 | tf_op jit(solution)/shard_map/ppermute | solution.py:30
  26.9 8.0 %collective-permute-start.4 = (bf16[152,512]{1,0:T(8,128)(2,1)S(1)}, bf16[152,512]{1,0:T(8,128)(2,1)S(1)}, u32[]{:S(2)}, u32[]{:S(2)}) collective-permute-start(bf16[152,512]{1,0:T(8,128)(2,1)S(1)} %get-tuple-element.18.refs_0_.after_ref), channel_id=1, source_target_pairs={{0,56},{8,0},{16,8},{24,16},{32,24},{40,32},{48,40},{56,48},{1,57}... | collective-permute-start | bytes 466952 | tf_op jit(solution)/shard_map/ppermute | solution.py:30
  30.8 11.7 %collective-permute-start.3 = (bf16[152,512]{1,0:T(8,128)(2,1)S(1)}, bf16[152,512]{1,0:T(8,128)(2,1)S(1)}, u32[]{:S(2)}, u32[]{:S(2)}) collective-permute-start(bf16[152,512]{1,0:T(8,128)(2,1)S(1)} %collective-permute-done.1.refs_1_), channel_id=1, source_target_pairs={{0,56},{8,0},{16,8},{24,16},{32,24},{40,32},{48,40},{56,48},{1,57}... | collective-permute-start | bytes 466952 | tf_op jit(solution)/shard_map/ppermute | solution.py:30
  34.9 7.7 %collective-permute-start.5 = (bf16[152,512]{1,0:T(8,128)(2,1)S(1)}, bf16[152,512]{1,0:T(8,128)(2,1)S(1)}, u32[]{:S(2)}, u32[]{:S(2)}) collective-permute-start(bf16[152,512]{1,0:T(8,128)(2,1)S(1)} %collective-permute-done.1.refs_1_), channel_id=1, source_target_pairs={{0,8},{8,16},{16,24},{24,32},{32,40},{40,48},{48,56},{56,0},{1,9},... | collective-permute-start | bytes 466952 | tf_op jit(solution)/shard_map/ppermute | solution.py:30
  34.9 8.8 %collective-permute-start.6 = (bf16[152,512]{1,0:T(8,128)(2,1)S(1)}, bf16[152,512]{1,0:T(8,128)(2,1)S(1)}, u32[]{:S(2)}, u32[]{:S(2)}) collective-permute-start(bf16[152,512]{1,0:T(8,128)(2,1)S(1)} %collective-permute-done.2.refs_2_), channel_id=1, source_target_pairs={{0,8},{8,16},{16,24},{24,32},{32,40},{40,48},{48,56},{56,0},{1,9},... | collective-permute-start | bytes 466952 | tf_op jit(solution)/shard_map/ppermute | solution.py:30
  34.9 8.8 %collective-permute-start.8 = (bf16[152,512]{1,0:T(8,128)(2,1)S(1)}, bf16[152,512]{1,0:T(8,128)(2,1)S(1)}, u32[]{:S(2)}, u32[]{:S(2)}) collective-permute-start(bf16[152,512]{1,0:T(8,128)(2,1)S(1)} %collective-permute-done.4.refs_4_), channel_id=1, source_target_pairs={{0,56},{8,0},{16,8},{24,16},{32,24},{40,32},{48,40},{56,48},{1,57}... | collective-permute-start | bytes 466952 | tf_op jit(solution)/shard_map/ppermute | solution.py:30
  38.2 4.3 %collective-permute-start.23 = (bf16[19,1216]{1,0:T(8,128)(2,1)S(1)}, bf16[19,1216]{1,0:T(8,128)(2,1)S(1)}, u32[]{:S(2)}, u32[]{:S(2)}) collective-permute-start(bf16[19,1216]{1,0:T(8,128)(2,1)S(1)} %shard_map.87), channel_id=1, source_target_pairs={{0,64},{64,0},{1,65},{65,1},{2,66},{66,2},{3,67},{67,3},{4,68},{68... | collective-permute-start | bytes 138632 | tf_op jit(solution)/shard_map/ppermute | solution.py:30
  44.4 5.9 %collective-permute-start.7 = (bf16[152,512]{1,0:T(8,128)(2,1)S(1)}, bf16[152,512]{1,0:T(8,128)(2,1)S(1)}, u32[]{:S(2)}, u32[]{:S(2)}) collective-permute-start(bf16[152,512]{1,0:T(8,128)(2,1)S(1)} %collective-permute-done.3.refs_3_), channel_id=1, source_target_pairs={{0,56},{8,0},{16,8},{24,16},{32,24},{40,32},{48,40},{56,48},{1,57}... | collective-permute-start | bytes 466952 | tf_op jit(solution)/shard_map/ppermute | solution.py:30
  45.5 7.0 %collective-permute-start.9 = (bf16[152,512]{1,0:T(8,128)(2,1)S(1)}, bf16[152,512]{1,0:T(8,128)(2,1)S(1)}, u32[]{:S(2)}, u32[]{:S(2)}) collective-permute-start(bf16[152,512]{1,0:T(8,128)(2,1)S(1)} %collective-permute-done.5.refs_5_.refs_2_), channel_id=1, source_target_pairs={{0,8},{8,16},{16,24},{24,32},{32,40},{40,48},{48,56},{56,0},{1,9},... | collective-permute-start | bytes 466952 | tf_op jit(solution)/shard_map/ppermute | solution.py:30
  46.5 8.5 %collective-permute-start.10 = (bf16[152,512]{1,0:T(8,128)(2,1)S(1)}, bf16[152,512]{1,0:T(8,128)(2,1)S(1)}, u32[]{:S(2)}, u32[]{:S(2)}) collective-permute-start(bf16[152,512]{1,0:T(8,128)(2,1)S(1)} %collective-permute-done.6.refs_6_.refs_0_), channel_id=1, source_target_pairs={{0,8},{8,16},{16,24},{24,32},{32,40},{40,48},{48,56},{56,0},{1,9},... | collective-permute-start | bytes 466952 | tf_op jit(solution)/shard_map/ppermute | solution.py:30
  50.4 6.7 %collective-permute-start.11 = (bf16[152,512]{1,0:T(8,128)(2,1)S(1)}, bf16[152,512]{1,0:T(8,128)(2,1)S(1)}, u32[]{:S(2)}, u32[]{:S(2)}) collective-permute-start(bf16[152,512]{1,0:T(8,128)(2,1)S(1)} %collective-permute-done.7.refs_7_), channel_id=1, source_target_pairs={{0,56},{8,0},{16,8},{24,16},{32,24},{40,32},{48,40},{56,48},{1,57}... | collective-permute-start | bytes 466952 | tf_op jit(solution)/shard_map/ppermute | solution.py:30
  51.9 7.0 %collective-permute-start.12 = (bf16[152,512]{1,0:T(8,128)(2,1)S(1)}, bf16[152,512]{1,0:T(8,128)(2,1)S(1)}, u32[]{:S(2)}, u32[]{:S(2)}) collective-permute-start(bf16[152,512]{1,0:T(8,128)(2,1)S(1)} %collective-permute-done.8.refs_8_.refs_1_), channel_id=1, source_target_pairs={{0,56},{8,0},{16,8},{24,16},{32,24},{40,32},{48,40},{56,48},{1,57}... | collective-permute-start | bytes 466952 | tf_op jit(solution)/shard_map/ppermute | solution.py:30
  52.4 6.7 %collective-permute-start.13 = (bf16[152,512]{1,0:T(8,128)(2,1)S(1)}, bf16[152,512]{1,0:T(8,128)(2,1)S(1)}, u32[]{:S(2)}, u32[]{:S(2)}) collective-permute-start(bf16[152,512]{1,0:T(8,128)(2,1)S(1)} %collective-permute-done.9.refs_9_), channel_id=1, source_target_pairs={{0,8},{8,16},{16,24},{24,32},{32,40},{40,48},{48,56},{56,0},{1,9},... | collective-permute-start | bytes 466952 | tf_op jit(solution)/shard_map/ppermute | solution.py:30
  55.0 6.4 %collective-permute-start.14 = (bf16[152,512]{1,0:T(8,128)(2,1)S(1)}, bf16[152,512]{1,0:T(8,128)(2,1)S(1)}, u32[]{:S(2)}, u32[]{:S(2)}) collective-permute-start(bf16[152,512]{1,0:T(8,128)(2,1)S(1)} %collective-permute-done.10.refs_10_), channel_id=1, source_target_pairs={{0,8},{8,16},{16,24},{24,32},{32,40},{40,48},{48,56},{56,0},{1,9},... | collective-permute-start | bytes 466952 | tf_op jit(solution)/shard_map/ppermute | solution.py:30
  57.0 5.2 %collective-permute-start.15 = (bf16[152,512]{1,0:T(8,128)(2,1)S(1)}, bf16[152,512]{1,0:T(8,128)(2,1)S(1)}, u32[]{:S(2)}, u32[]{:S(2)}) collective-permute-start(bf16[152,512]{1,0:T(8,128)(2,1)S(1)} %collective-permute-done.11.refs_11_), channel_id=1, source_target_pairs={{0,56},{8,0},{16,8},{24,16},{32,24},{40,32},{48,40},{56,48},{1,57}... | collective-permute-start | bytes 466952 | tf_op jit(solution)/shard_map/ppermute | solution.py:30
  65.8 8.1 %collective-permute-start.18 = (bf16[1120,128]{1,0:T(8,128)(2,1)S(1)}, bf16[1120,128]{1,0:T(8,128)(2,1)S(1)}, u32[]{:S(2)}, u32[]{:S(2)}) collective-permute-start(bf16[1120,128]{1,0:T(8,128)(2,1)S(1)} %get-tuple-element.19.own), channel_id=1, source_target_pairs={{0,8},{8,0},{1,9},{9,1},{2,10},{10,2},{3,11},{11,3},{4,12},{12,4},... | collective-permute-start | bytes 860168 | tf_op jit(solution)/shard_map/ppermute | solution.py:30
  66.2 9.6 %collective-permute-start.16 = (bf16[1120,128]{1,0:T(8,128)(2,1)S(1)}, bf16[1120,128]{1,0:T(8,128)(2,1)S(1)}, u32[]{:S(2)}, u32[]{:S(2)}) collective-permute-start(bf16[1120,128]{1,0:T(8,128)(2,1)S(1)} %get-tuple-element.19.own), channel_id=1, source_target_pairs={{0,1},{1,0},{2,3},{3,2},{4,5},{5,4},{6,7},{7,6},{8,9},{9,8},{10,11... | collective-permute-start | bytes 860168 | tf_op jit(solution)/shard_map/ppermute | solution.py:30
  73.9 1.9 %collective-permute-start.19 = (bf16[1120,128]{1,0:T(8,128)(2,1)S(1)}, bf16[1120,128]{1,0:T(8,128)(2,1)S(1)}, u32[]{:S(2)}, u32[]{:S(2)}) collective-permute-start(bf16[1120,128]{1,0:T(8,128)(2,1)S(1)} %collective-permute-done.18.far), channel_id=1, source_target_pairs={{0,1},{1,0},{2,3},{3,2},{4,5},{5,4},{6,7},{7,6},{8,9},{9,8},{10,11... | collective-permute-start | bytes 860168 | tf_op jit(solution)/shard_map/ppermute | solution.py:30
  73.9 1.9 %collective-permute-start.17 = (bf16[384,192]{1,0:T(8,128)(2,1)S(1)}, bf16[384,192]{1,0:T(8,128)(2,1)S(1)}, u32[]{:S(2)}, u32[]{:S(2)}) collective-permute-start(bf16[384,192]{1,0:T(8,128)(2,1)S(1)} %get-tuple-element.20.own_q), channel_id=1, source_target_pairs={{0,1},{1,0},{2,3},{3,2},{4,5},{5,4},{6,7},{7,6},{8,9},{9,8},{10,11... | collective-permute-start | bytes 442376 | tf_op jit(solution)/shard_map/ppermute | solution.py:30
  78.9 12.5 %collective-permute-start.20 = (bf16[480,128]{1,0:T(8,128)(2,1)S(1)}, bf16[480,128]{1,0:T(8,128)(2,1)S(1)}, u32[]{:S(2)}, u32[]{:S(2)}) collective-permute-start(bf16[480,128]{1,0:T(8,128)(2,1)S(1)} %shard_map.86.a0), channel_id=1, source_target_pairs={{0,2},{2,4},{4,6},{6,0},{1,3},{3,5},{5,7},{7,1},{8,10},{10,12},{12... | collective-permute-start | bytes 368648 | tf_op jit(solution)/shard_map/ppermute | solution.py:30
  79.5 12.0 %collective-permute-start.21 = (bf16[480,128]{1,0:T(8,128)(2,1)S(1)}, bf16[480,128]{1,0:T(8,128)(2,1)S(1)}, u32[]{:S(2)}, u32[]{:S(2)}) collective-permute-start(bf16[480,128]{1,0:T(8,128)(2,1)S(1)} %shard_map.86.a0), channel_id=1, source_target_pairs={{0,4},{2,6},{4,0},{6,2},{1,5},{3,7},{5,1},{7,3},{8,12},{10,14},{12... | collective-permute-start | bytes 368648 | tf_op jit(solution)/shard_map/ppermute | solution.py:30
  81.2 10.3 %collective-permute-start.22 = (bf16[480,128]{1,0:T(8,128)(2,1)S(1)}, bf16[480,128]{1,0:T(8,128)(2,1)S(1)}, u32[]{:S(2)}, u32[]{:S(2)}) collective-permute-start(bf16[480,128]{1,0:T(8,128)(2,1)S(1)} %shard_map.86.a0), channel_id=1, source_target_pairs={{0,6},{2,0},{4,2},{6,4},{1,7},{3,1},{5,3},{7,5},{8,14},{10,8},{12,... | collective-permute-start | bytes 368648 | tf_op jit(solution)/shard_map/ppermute | solution.py:30
  92.5 5.5 %collective-permute-start.24 = (bf16[48,608]{1,0:T(8,128)(2,1)S(1)}, bf16[48,608]{1,0:T(8,128)(2,1)S(1)}, u32[]{:S(2)}, u32[]{:S(2)}) collective-permute-start(bf16[48,608]{1,0:T(8,128)(2,1)S(1)} %get-tuple-element.22), channel_id=1, source_target_pairs={{0,2},{2,4},{4,6},{6,0},{1,3},{3,5},{5,7},{7,1},{8,10},{10,12},{12... | collective-permute-start | bytes 175112 | tf_op jit(solution)/shard_map/ppermute | solution.py:30
  94.0 4.2 %collective-permute-start.25 = (bf16[48,608]{1,0:T(8,128)(2,1)S(1)}, bf16[48,608]{1,0:T(8,128)(2,1)S(1)}, u32[]{:S(2)}, u32[]{:S(2)}) collective-permute-start(bf16[48,608]{1,0:T(8,128)(2,1)S(1)} %get-tuple-element.23), channel_id=1, source_target_pairs={{0,6},{2,0},{4,2},{6,4},{1,7},{3,1},{5,3},{7,5},{8,14},{10,8},{12,... | collective-permute-start | bytes 175112 | tf_op jit(solution)/shard_map/ppermute | solution.py:30
  95.8 5.7 %collective-permute-start.26 = (bf16[48,608]{1,0:T(8,128)(2,1)S(1)}, bf16[48,608]{1,0:T(8,128)(2,1)S(1)}, u32[]{:S(2)}, u32[]{:S(2)}) collective-permute-start(bf16[48,608]{1,0:T(8,128)(2,1)S(1)} %get-tuple-element.24), channel_id=1, source_target_pairs={{0,4},{2,6},{4,0},{6,2},{1,5},{3,7},{5,1},{7,3},{8,12},{10,14},{12... | collective-permute-start | bytes 175112 | tf_op jit(solution)/shard_map/ppermute | solution.py:30
  (5 other events, 19.0 us)
Sparse Core Ops, SparseCore 0:
  18.2 29.9 all-gather.2
  50.0 39.4 all-gather.4
